TPU v7x, 256 devices: a whole 4x4x8 slice. The times are simulated.
256 devices in a mesh: dp: 64 (over z, y, core), replica: 4 (over x).
Axes of the slice: x: 4, y: 4, z: 8, core: 2. Of those that a mesh axis runs over, the one named last changes fastest.
Arguments:
- text_features: bfloat16 [256, 4, 64, 4096], P('dp', 'replica'), may hold values from -6 to 6
- head_weight: bfloat16 [4096, 1024], replicated, may hold values from -0.09375 to 0.09375
- image_embeds: bfloat16 [256, 256, 1024], P('dp'), may hold values from -6 to 6
- doc_ids: int32 [256, 256], P('dp'), may hold values from 0 to 63, never falling along the last dimension, each value on 1 to 8 neighbouring positions
- hard_lists: int32 [256, 63], replicated, may hold values from -1 to 255, as said below
- logit_scale: float32 [], replicated, may hold values from 20 to 40
- logit_bias: float32 [], replicated, may hold values from -4 to -2
Outputs:
- row_loss: float32 [256, 256], P('dp', 'replica')
- head_grad: float32 [4096, 1024], P('replica', 'dp')
Inputs may be any that keep to these rules, and one draw needn't show every extreme that they name: `hard_lists`: each row lists its text blocks first and -1 after them. The image blocks d * 4 to d * 4 + 3 together name at most one text block of each other dp index and none of blocks d * 4 to d * 4 + 3; some dp index names a block of every other dp index. `doc_ids`: within a row, ids never fall.
All inputs are finite; a program needn't handle non-finite values.
Results may differ from a plain program's by a relative error of at most 0.012.
Values may be sent and summed in bfloat16 or wider, within the bound.
No kernel may reach another device: no remote copies, remote signals or barrier semaphores. Data moves between devices by JAX's collectives and lax.ppermute only.
A program may use at most 128 MiB of HBM per device.

v0:
```python
import math

import jax
import jax.numpy as jnp
from jax import lax
from jax.sharding import PartitionSpec as P

EPSILON = 1e-06


def unit_rows(values):
    inverse = lax.rsqrt(jnp.sum(values * values, axis=-1, keepdims=True) + EPSILON)
    return (values * inverse, inverse)


def on_device(
    text_features, head_weight, image_embeds, doc_ids, hard_lists, logit_scale, logit_bias
):
    dp_count = lax.axis_size("dp")
    dp_index = lax.axis_index("dp")
    quarter = lax.axis_index("replica")
    block_count = text_features.shape[0]
    quarter_rows = text_features.shape[2]
    feat_width = text_features.shape[3]
    block_rows = image_embeds.shape[1]
    emb_width = head_weight.shape[1]
    list_width = hard_lists.shape[1]
    text_rows = text_features.reshape(block_count * quarter_rows, feat_width)
    projected = jnp.dot(text_rows, head_weight, preferred_element_type=jnp.float32)
    unit_text, inverse = unit_rows(projected)
    text_emb = unit_text.astype(jnp.bfloat16).reshape(block_count, quarter_rows, emb_width)
    image_unit = unit_rows(image_embeds.astype(jnp.float32))[0].astype(jnp.bfloat16)
    block_iota = jnp.arange(block_count, dtype=jnp.int32)
    peer_iota = jnp.arange(dp_count, dtype=jnp.int32)
    owner_dp = jnp.where(hard_lists >= 0, hard_lists // block_count, -1).reshape(
        dp_count, block_count, list_width
    )
    local_id = (hard_lists % block_count).reshape(dp_count, block_count, list_width)
    my_lists = lax.dynamic_index_in_dim(owner_dp, dp_index, 0, keepdims=False)
    was_asked = jnp.any(my_lists[None, :, :] == peer_iota[:, None, None], axis=2)
    present = jnp.any(was_asked, axis=1).astype(jnp.float32)
    asker_block = jnp.sum(was_asked.astype(jnp.int32) * block_iota[None, :], axis=1)
    wanted = (owner_dp == dp_index)[..., None] & (local_id[..., None] == block_iota)
    give_block = jnp.any(wanted, axis=(1, 2)).astype(jnp.bfloat16)
    outgoing = jnp.einsum(
        "ec,cqk->eqk", give_block, text_emb, preferred_element_type=jnp.float32
    ).astype(jnp.bfloat16)
    arrived = lax.all_to_all(outgoing, "dp", split_axis=0, concat_axis=0, tiled=True)
    group_size = math.gcd(dp_count, 8)
    group_count = dp_count // group_size

    def visit_group(row_sums, inputs):
        text_units, which_block, live_flag = inputs
        image_rows = jnp.take(image_unit, which_block, axis=0)
        logits = (
            logit_scale
            * jnp.einsum("gik,gjk->gij", image_rows, text_units, preferred_element_type=jnp.float32)
            + logit_bias
        )
        live_mask = live_flag[:, None, None]
        elem_loss = jax.nn.softplus(logits) * live_mask
        weights = (jax.nn.sigmoid(logits) * live_mask).astype(jnp.bfloat16)
        grad_units = (
            logit_scale
            * jnp.einsum("gij,gik->gjk", weights, image_rows, preferred_element_type=jnp.float32)
        ).astype(jnp.bfloat16)
        pick_rows = (which_block[:, None] == block_iota[None, :]).astype(jnp.float32)
        row_sums = row_sums + jnp.einsum("gb,gi->bi", pick_rows, jnp.sum(elem_loss, axis=2))
        return (row_sums, grad_units)

    group_inputs = (
        arrived.reshape(group_count, group_size, quarter_rows, emb_width),
        asker_block.reshape(group_count, group_size),
        present.reshape(group_count, group_size),
    )
    row_sums, sent_grads = lax.scan(
        visit_group, jnp.zeros((block_count, block_rows), jnp.float32), group_inputs
    )
    sent_grads = sent_grads.reshape(dp_count, quarter_rows, emb_width)
    returned = lax.all_to_all(sent_grads, "dp", split_axis=0, concat_axis=0, tiled=True)
    remote = jnp.einsum("ec,eqk->cqk", give_block, returned, preferred_element_type=jnp.float32)
    text_docs = lax.dynamic_slice_in_dim(doc_ids, quarter * quarter_rows, quarter_rows, 1)
    label_sign = jnp.where(doc_ids[:, :, None] == text_docs[:, None, :], 1.0, -1.0).astype(
        jnp.float32
    )
    own_logits = (
        logit_scale
        * jnp.einsum("bik,bjk->bij", image_unit, text_emb, preferred_element_type=jnp.float32)
        + logit_bias
    )
    own_loss = jax.nn.softplus(-label_sign * own_logits)
    own_weights = (-label_sign * jax.nn.sigmoid(-label_sign * own_logits)).astype(jnp.bfloat16)
    own_grad = logit_scale * jnp.einsum(
        "bij,bik->bjk", own_weights, image_unit, preferred_element_type=jnp.float32
    )
    row_sums = row_sums + jnp.sum(own_loss, axis=2)
    row_share = lax.psum_scatter(row_sums, "replica", scatter_dimension=1, tiled=True) / block_rows
    text_grad = (own_grad + remote).reshape(block_count * quarter_rows, emb_width)
    along = jnp.sum(unit_text * text_grad, axis=-1, keepdims=True)
    proj_grad = ((text_grad - unit_text * along) * inverse).astype(jnp.bfloat16)
    head_part = lax.psum_scatter(
        lax.dot_general(
            text_rows, proj_grad, (((0,), (0,)), ((), ())), preferred_element_type=jnp.float32
        ).astype(jnp.bfloat16),
        "replica",
        scatter_dimension=0,
        tiled=True,
    ).astype(jnp.float32)
    col_width = emb_width // dp_count
    summed = lax.psum(head_part, "dp")
    head_grad = lax.dynamic_slice_in_dim(summed, dp_index * col_width, col_width, 1)
    return (row_share, head_grad)


def solution(mesh):
    placed = (
        P("dp", "replica", None, None),
        P(),
        P("dp", None, None),
        P("dp", None),
        P(),
        P(),
        P(),
    )
    return jax.shard_map(
        on_device,
        mesh=mesh,
        in_specs=placed,
        out_specs=(P("dp", "replica"), P("replica", "dp")),
        check_vma=False,
    )
```

profile of v0, /device:TPU:4, one launch (start us, length us, event | category | flops | bytes accessed | tf_op | source)
XLA Modules:
  0.0 932.7 jit_solution(7478021596919673614)
XLA Ops:
  8.8 5.8 multiply_reduce_fusion.1
  15.8 5.6 convolution_convert_fusion
  21.5 11.3 %copy.33 = bf16[64,64,1024]{2,1,0:T(8,128)(2,1)} copy(bf16[64,64,1024]{2,0,1:T(8,128)(2,1)} %convolution_convert_fusion) | data formatting | bytes 16777216 | tf_op jit(solution)/shard_map/convert_element_type | solution.py:47
  32.7 12.5 %all-to-all-start = ((bf16[64,64,1024]{2,1,0:T(8,128)(2,1)}), bf16[64,64,1024]{2,1,0:T(8,128)(2,1)}, u32[]{:S(2)}, u32[]{:S(2)}) async-start(bf16[64,64,1024]{2,1,0:T(8,128)(2,1)} %copy.33), calls=%async_computation | async-start | bytes 16777216 | tf_op jit(solution)/shard_map/all_to_all | solution.py:48
  51.3 179.9 %all-to-all-done = bf16[64,64,1024]{2,1,0:T(8,128)(2,1)} async-done(((bf16[64,64,1024]{2,1,0:T(8,128)(2,1)}), bf16[64,64,1024]{2,1,0:T(8,128)(2,1)}, u32[]{:S(2)}, u32[]{:S(2)}) %all-to-all-start) | async-done | bytes 8388640 | tf_op jit(solution)/shard_map/all_to_all | solution.py:48
  231.2 106.1 %while.13 = (s32[]{:T(128)}, f32[4,256]{1,0:T(4,128)S(1)}, bf16[8,8,64,1024]{3,2,1,0:T(8,128)(2,1)}, s32[8,8]{1,0:T(8,128)S(1)}, f32[]{:T(128)}, /*index=5*/bf16...) while((s32[]{:T(128)}, f32[4,256]{1,0:T(4,128)S(1)}, ...), condition=%wide.region_8.9_spmd.clone, body=%wide.region_6.8_spmd.clone.sunk | while | flops 545129600 | bytes 37279784 | solution.py:76
  235.6 5.6 fusion.64
  248.9 5.6 fusion.64
  257.8 4.4 gather_fusion
  262.2 5.6 fusion.64
  275.4 5.6 fusion.64
  284.3 4.4 gather_fusion
  288.7 5.6 fusion.64
  297.5 4.4 gather_fusion
  301.9 5.6 fusion.64
  310.8 4.4 gather_fusion
  315.2 5.6 fusion.64
  328.5 5.6 fusion.64
  337.3 6.7 all-to-all-start.1
  349.0 181.1 %all-to-all-done.1 = bf16[64,64,1024]{2,1,0:T(8,128)(2,1)} async-done(((bf16[64,64,1024]{2,1,0:T(8,128)(2,1)}), bf16[64,64,1024]{2,1,0:T(8,128)(2,1)}, u32[]{:S(2)}, u32[]{:S(2)}) %all-to-all-start.1) | async-done | bytes 8388640 | tf_op jit(solution)/shard_map/all_to_all | solution.py:80
  530.1 12.4 %fusion.21 = f32[4,64,1024]{2,0,1:T(4,128)S(1)} fusion(bf16[64,64,1024]{2,1,0:T(8,128)(2,1)} %all-to-all-done.1, pred[64,4]{0,1:T(4,128)(4,1)S(1)} %fusion.33), kind=kOutput, calls=%fused_computation.35 | convolution fusion | flops 33554432 | bytes 9437440 | tf_op jit(solution)/shard_map/ec,eqk->cqk/dot_general | solution.py:81
  544.1 5.6 convert_bitcast_fusion
  551.2 77.3 %reduce-scatter.5.cloned.1.call-done = bf16[1024,1024]{0,1:T(8,128)(2,1)} async-done(((bf16[4096,1024]{0,1:T(8,128)(2,1)}), bf16[1024,1024]{0,1:T(8,128)(2,1)}) %reduce-scatter.5.cloned.1.call-update) | async-done | bytes 2097168 | tf_op jit(solution)/shard_map/reduce_scatter | solution.py:101
  628.5 295.9 %all-reduce.1 = f32[1024,1024]{0,1:T(8,128)} all-reduce(bf16[1024,1024]{0,1:T(8,128)(2,1)} %reduce-scatter.5.cloned.1.call-done), channel_id=1, replica_groups=mesh['dp'=64,'replica'=4] {'dp'}, use_global_device_ids=true, to_apply=%region_13.14 | all-reduce | flops 1048576 | bytes 6291456 | tf_op jit(solution)/shard_map/psum | solution.py:110
  (121 shorter events, 60.6 us)
Async XLA Ops:
  7.2 1.6 copy-start
  15.0 0.8 copy-start.3
  32.7 198.4 %all-to-all-start = ((bf16[64,64,1024]{2,1,0:T(8,128)(2,1)}), bf16[64,64,1024]{2,1,0:T(8,128)(2,1)}, u32[]{:S(2)}, u32[]{:S(2)}) async-start(bf16[64,64,1024]{2,1,0:T(8,128)(2,1)} %copy.33), calls=%async_computation | async-start | bytes 16777216 | tf_op jit(solution)/shard_map/all_to_all | solution.py:48
  235.6 6.2 copy-start.2
  248.9 6.2 copy-start.2
  262.2 6.2 copy-start.2
  275.4 6.2 copy-start.2
  288.7 6.2 copy-start.2
  301.9 6.2 copy-start.2
  315.2 6.2 copy-start.2
  328.5 6.2 copy-start.2
  337.3 8.1 copy-start.4
  337.3 192.8 %all-to-all-start.1 = ((bf16[64,64,1024]{2,1,0:T(8,128)(2,1)}), bf16[64,64,1024]{2,1,0:T(8,128)(2,1)}, u32[]{:S(2)}, u32[]{:S(2)}) async-start(bf16[64,64,1024]{2,1,0:T(8,128)(2,1)} %bitcast.68), calls=%async_computation.1 | async-start | bytes 16777216 | tf_op jit(solution)/shard_map/all_to_all | solution.py:80
  344.0 205.7 %reduce-scatter.7.cloned.1.call-start = ((), (), s32[]{:S(2)}) async-start(), calls=%async_computation.5 | async-start | bytes 163840
  348.9 279.6 %reduce-scatter.5.cloned.1.call-start = ((), (), s32[]{:S(2)}) async-start(), calls=%async_computation.4 | async-start | bytes 10485760 | tf_op jit(solution)/shard_map/reduce_scatter | solution.py:101
  530.1 12.4 %copy-start.1 = (bf16[4,256,1024]{2,1,0:T(8,128)(2,1)S(1)}, bf16[4,256,1024]{2,1,0:T(8,128)(2,1)}, u32[]{:S(2)}) copy-start(bf16[4,256,1024]{2,1,0:T(8,128)(2,1)} %get-tuple-element.235) | copy-start | bytes 6291460
Sparse Core Ops, SparseCore 0:
  349.0 22.4 reduce-scatter.6
  549.8 78.6 reduce-scatter.4
where the time goes:
time: 934 us; the launch traced here: 933 us
  waiting for transfers between devices  438 us (47%)
  blocking collectives  296 us (32%)
  matrix products  101 us (11%)
  local copies, waits for them, and re-layouts  51.2 us (5%)
  starting transfers between devices  19.3 us (2%)
  between operations  15.5 us (2%)
  other arithmetic  11.5 us (1%)
    psum x1, blocking collectives, on_device(): summed = lax.psum(head_part, 'dp')  296 us
    all_to_all x1, waiting for transfers between devices, on_device(): lax.all_to_all(sent_grads, 'dp', split_axis=0, concat_axis=0, tiled=True)  181 us
    all_to_all x1, waiting for transfers between devices, on_device(): lax.all_to_all(outgoing, 'dp', split_axis=0, concat_axis=0, tiled=True)  180 us
    reduce_scatter x1, waiting for transfers between devices, on_device(): lax.psum_scatter(lax.dot_general(text_rows, proj_grad, (((0,), (0,)), (()...  77.3 us
    dot_general x8, matrix products, visit_group(): jnp.einsum('gik,gjk->gij', image_rows, text_units, preferred_element_type...  44.6 us
    gather x8, local copies, waits for them, and re-layouts, visit_group(): image_rows = jnp.take(image_unit, which_block, axis=0)  35 us
    dot_general x8, matrix products, visit_group(): jnp.einsum('gij,gik->gjk', weights, image_rows, preferred_element_type=jn...  21 us
  transfers between devices with their start and end apart: 4, of which 3 were waited for; matrix products, arithmetic and copies ran while one was open for 3% of the time, Pallas kernels for 0%

commit v1 on v0

v1 whole, which is shorter than its diff:
```python
import functools

import jax
import jax.numpy as jnp
from jax import lax
from jax.experimental import pallas as pl
from jax.experimental.pallas import tpu as pltpu
from jax.sharding import Mesh, PartitionSpec as P

EPSILON = 1e-06
DP = ("z", "y", "c")
GROUP = 4
F32 = jnp.float32
BF16 = jnp.bfloat16


def dot(a, b, contract):
    return lax.dot_general(a, b, ((contract[:1], contract[1:]), ((), ())), preferred_element_type=F32)


def unit_rows(values):
    inverse = lax.rsqrt(jnp.sum(values * values, axis=-1, keepdims=True) + EPSILON)
    return (values * inverse, inverse)


def shifted(size, shift):
    return [(i, (i + shift) % size) for i in range(size)]


def loss_and_weight(logits):
    small = jnp.exp(-jnp.abs(logits))
    share = 1.0 / (1.0 + small)
    weight = jnp.where(logits >= 0, share, small * share)
    return (jnp.maximum(logits, 0.0) + jnp.log1p(small), weight)


def pair_kernel(
    sources, counts, place, scale_bias, text_0, text_1, text_2, text_3, inverse, own_images,
    image_docs, text_docs, arrived, chunks, pair_loss, own_loss, text_all, acc
):
    blocks, piece_rows, width = text_0.shape
    pieces = (text_0, text_1, text_2, text_3)
    quarters = len(pieces)
    block_rows = quarters * piece_rows
    part = width // quarters
    scale, bias = scale_bias[0], scale_bias[1]
    for k in range(quarters):
        text_all[:, k * piece_rows : (k + 1) * piece_rows, :] = pieces[k][...]
    pair_loss[...] = jnp.zeros_like(pair_loss)

    def each_block(t, carry):
        text = text_all[t]
        images = own_images[t]
        logits = scale * dot(text, images, (1, 1)) + bias
        same = text_docs[t] == image_docs[t]
        sign = jnp.where(same, 1.0, -1.0)
        loss, weight = loss_and_weight(-sign * logits)
        own_loss[pl.ds(t, 1)] = jnp.sum(loss, axis=0, keepdims=True)[None]
        acc[...] = dot((-sign * weight).astype(BF16), images, (1, 0))
        count = counts[t]

        def each_group(g, inner):
            ids = [sources[t, g * GROUP + i] for i in range(GROUP)]
            rows = jnp.concatenate([arrived[ids[i]] for i in range(GROUP)], axis=0)
            values = scale * dot(text, rows, (1, 1)) + bias
            terms, shares = loss_and_weight(values)
            sums = jnp.sum(terms, axis=0, keepdims=True)
            left = (count - g * GROUP) * piece_rows
            live = lax.broadcasted_iota(jnp.int32, shares.shape, 1) < left
            shares = jnp.where(live, shares, 0.0).astype(BF16)
            acc[...] += dot(shares, rows, (1, 0))
            for i in range(GROUP):

                @pl.when(g * GROUP + i < count)
                def _():
                    pair_loss[pl.ds(ids[i], 1)] = sums[:, i * piece_rows : (i + 1) * piece_rows][None]

            return inner

        lax.fori_loop(0, (count + GROUP - 1) // GROUP, each_group, 0)
        unit = text.astype(F32)
        grad = scale * acc[...]
        along = jnp.sum(unit * grad, axis=-1, keepdims=True)
        acc[...] = (grad - unit * along) * inverse[t]
        for k in range(quarters):
            start = pl.multiple_of(lax.rem(place[0] + k, quarters) * part, part)
            values = acc[:, pl.ds(start, part)].astype(BF16)
            for j in range(quarters):
                chunks[k, j, pl.ds(t, 1)] = values[j * piece_rows : (j + 1) * piece_rows][None]
        return carry

    lax.fori_loop(0, blocks, each_block, 0)


def head_kernel(
    place, grad_0, grad_1, grad_2, grad_3, feat_0, feat_1, feat_2, feat_3, keep, give, turned,
    *, sizes, strip
):
    z_part, y_size, c_size = sizes
    feats = (feat_0, feat_1, feat_2, feat_3)
    rows = feat_0.shape[0]

    @pl.when(pl.program_id(0) == 0)
    def _():
        for j in range(len(feats)):
            at = slice(j * rows, (j + 1) * rows)
            total = 0.0
            for k, grad in enumerate((grad_0, grad_1, grad_2, grad_3)):
                piece = (j - k) % len(feats)
                total += grad[piece * rows : (piece + 1) * rows].astype(F32)
            flipped = total.T.astype(BF16)
            for zz in range(z_part):
                for y in range(y_size):
                    for c in range(c_size):
                        block = flipped[((zz * y_size + y) * c_size + c) * strip :][:strip]
                        y_rel = lax.rem(y - place[1] + y_size, y_size)
                        c_rel = lax.rem(c - place[2] + c_size, c_size)
                        to = ((c_rel * y_size + y_rel) * z_part + zz) * strip
                        turned[pl.ds(pl.multiple_of(to, strip), strip), at] = block

    half = keep.shape[0]
    for part, out in enumerate((keep, give)):
        total = None
        for j, feat in enumerate(feats):
            term = dot(turned[part * half : (part + 1) * half, j * rows : (j + 1) * rows], feat[...], (1, 0))
            total = term if total is None else total + term
        out[...] = total.astype(BF16)


def whole(memory=pltpu.VMEM):
    return pl.BlockSpec(memory_space=memory)


def on_device(
    text_features, head_weight, image_embeds, doc_ids, hard_lists, logit_scale, logit_bias
):
    z_size, y_size, c_size, x_size = (lax.axis_size(name) for name in ("z", "y", "c", "x"))
    z, y, c, x = (lax.axis_index(name) for name in ("z", "y", "c", "x"))
    dp_count = z_size * y_size * c_size
    dp_index = (z * y_size + y) * c_size + c
    blocks, _, piece_rows, feat_width = text_features.shape
    block_rows = image_embeds.shape[1]
    emb_width = head_weight.shape[1]
    rows = blocks * piece_rows
    part = emb_width // x_size
    strip = emb_width // dp_count
    block_iota = jnp.arange(blocks, dtype=jnp.int32)
    peer_iota = jnp.arange(dp_count, dtype=jnp.int32)

    owners = jnp.where(hard_lists >= 0, hard_lists // blocks, -1).reshape(dp_count, blocks, -1)
    my_owners = lax.dynamic_index_in_dim(owners, dp_index, 0, keepdims=False)
    asked = jnp.any(my_owners[None] == peer_iota[:, None, None], axis=2)
    asker_block = jnp.sum(asked.astype(jnp.int32) * block_iota, axis=1)

    own_images = lax.dynamic_slice_in_dim(image_embeds, x * piece_rows, piece_rows, 1)
    own_images = unit_rows(own_images.astype(F32))[0].astype(BF16)
    arrived = exchange_images(own_images, asker_block)

    features = text_features.reshape(rows, feat_width)
    unit_text, inverse = unit_rows(dot(features, head_weight, (1, 0)))
    text_emb = unit_text.astype(BF16).reshape(blocks, piece_rows, emb_width)
    inverse = inverse.reshape(blocks, piece_rows)

    def around(value):
        return [value] + [lax.ppermute(value, "x", shifted(x_size, k)) for k in range(1, x_size)]

    texts = around(text_emb)
    inverses = jnp.stack(around(inverse), axis=1).reshape(blocks, block_rows, 1)
    feats = around(features)

    hit = (owners == dp_index)
    listed = jnp.any(hit, axis=(1, 2))
    which = jnp.sum(hit * (hard_lists % blocks).reshape(owners.shape), axis=(1, 2))
    mine = listed[None] & (which[None] == block_iota[:, None])
    before = peer_iota[None] < peer_iota[:, None]
    order = jnp.sum((mine[:, None] & before).astype(jnp.int32), axis=2)
    counts = jnp.sum(mine.astype(jnp.int32), axis=1)
    slots = jnp.arange(dp_count, dtype=jnp.int32)
    sources = jnp.sum(
        jnp.where(mine[:, None] & (order[:, None] == slots[:, None]), peer_iota, 0), axis=2
    )

    docs = doc_ids.reshape(blocks, x_size, piece_rows)
    twice = jnp.concatenate([docs[:, ::-1], docs[:, ::-1]], axis=1)
    text_docs = lax.dynamic_slice_in_dim(twice, x_size - 1 - x, x_size, 1)
    text_docs = text_docs.reshape(blocks, block_rows, 1)
    image_docs = lax.dynamic_index_in_dim(docs, x, 1, keepdims=True)
    place = jnp.stack([x, y, c]).astype(jnp.int32)
    scale_bias = jnp.stack([logit_scale, logit_bias])

    chunks, pair_loss, own_loss = pl.pallas_call(
        pair_kernel,
        out_shape=(
            jax.ShapeDtypeStruct((x_size, x_size, blocks, piece_rows, part), BF16),
            jax.ShapeDtypeStruct((dp_count, 1, piece_rows), F32),
            jax.ShapeDtypeStruct((blocks, 1, piece_rows), F32),
        ),
        in_specs=[whole(pltpu.SMEM)] * 4 + [whole()] * 9,
        out_specs=(whole(), whole(), whole()),
        scratch_shapes=[
            pltpu.VMEM((blocks, block_rows, emb_width), BF16),
            pltpu.VMEM((block_rows, emb_width), F32),
        ],
        compiler_params=pltpu.CompilerParams(vmem_limit_bytes=48 << 20),
        name="pairs",
    )(sources, counts, place, scale_bias, *texts, inverses, own_images, image_docs, text_docs, arrived)

    returned = lax.all_to_all(
        pair_loss.reshape(dp_count, piece_rows), DP, split_axis=0, concat_axis=0, tiled=True
    )
    pick = (jnp.any(asked, axis=1)[:, None] & (asker_block[:, None] == block_iota))[..., None]
    remote_loss = jnp.sum(jnp.where(pick, returned[:, None], 0.0), axis=0)
    row_loss = (own_loss.reshape(blocks, piece_rows) + remote_loss) / block_rows

    grads = [chunks[0].reshape(x_size * rows, part)]
    for k in range(1, x_size):
        grads.append(
            lax.ppermute(chunks[k].reshape(x_size * rows, part), "x", shifted(x_size, k))
        )
    z_part = z_size // x_size
    tile = min(1024, feat_width)
    half = part // c_size
    keep, give = pl.pallas_call(
        functools.partial(head_kernel, sizes=(z_part, y_size, c_size), strip=strip),
        grid=(feat_width // tile,),
        out_shape=(
            jax.ShapeDtypeStruct((half, feat_width), BF16),
            jax.ShapeDtypeStruct((half, feat_width), BF16),
        ),
        in_specs=[whole(pltpu.SMEM)]
        + [whole()] * 4
        + [pl.BlockSpec((rows, tile), lambda i: (0, i))] * 4,
        out_specs=(
            pl.BlockSpec((half, tile), lambda i: (0, i)),
            pl.BlockSpec((half, tile), lambda i: (0, i)),
        ),
        scratch_shapes=[pltpu.VMEM((part, x_size * rows), BF16)],
        compiler_params=pltpu.CompilerParams(vmem_limit_bytes=48 << 20),
        name="head",
    )(place, *grads, *feats)

    taken = lax.ppermute(give, "c", shifted(c_size, 1))
    total = (keep.astype(F32) + taken.astype(F32)).astype(BF16)
    total = total.reshape(y_size, z_part * strip, feat_width)
    moved = [total[0]] + [
        lax.ppermute(total[k], "y", shifted(y_size, k)) for k in range(1, y_size)
    ]
    total = sum(m.astype(F32) for m in moved).astype(BF16)
    total = total.reshape(z_part, strip, x_size, feat_width // x_size)
    final = None
    for k in range(z_size):
        goes = lax.rem(z + k, z_size)
        chunk = lax.dynamic_slice(
            total, (goes // x_size, 0, goes % x_size, 0), (1, strip, 1, feat_width // x_size)
        ).reshape(strip, feat_width // x_size)
        pairs = []
        for z_from in range(z_size):
            for x_from in range(x_size):
                to = (z_from + k) % z_size
                pairs.append(
                    (z_from * x_size + x_from, (z_part * x_from + to // x_size) * x_size + to % x_size)
                )
        got = lax.ppermute(chunk, ("z", "x"), pairs).astype(F32)
        final = got if final is None else final + got
    return (row_loss, final.T)


def copy_kernel(picked, from_ref, to_ref):
    to_ref[...] = from_ref[...]


def pick_blocks(values, picked):
    count, shape = picked.shape[0], values.shape[1:]
    spec = pltpu.PrefetchScalarGridSpec(
        num_scalar_prefetch=1,
        grid=(count,),
        in_specs=[pl.BlockSpec((1,) + shape, lambda i, ref: (ref[i], 0, 0))],
        out_specs=pl.BlockSpec((1,) + shape, lambda i, ref: (i, 0, 0)),
    )
    return pl.pallas_call(
        copy_kernel,
        grid_spec=spec,
        out_shape=jax.ShapeDtypeStruct((count,) + shape, values.dtype),
        name="pick",
    )(picked, values)


def exchange_images(own_images, asker_block):
    outgoing = pick_blocks(own_images, asker_block)
    return lax.all_to_all(outgoing, DP, split_axis=0, concat_axis=0, tiled=True)


def solution(mesh):
    x_size = mesh.shape["replica"]
    c_size = 2
    z_size = 2 * x_size
    y_size = mesh.shape["dp"] // (z_size * c_size)
    fine = Mesh(mesh.devices.reshape(z_size, y_size, c_size, x_size), ("z", "y", "c", "x"))
    placed = (P(DP, "x", None, None), P(), P(DP, None, None), P(DP, None), P(), P(), P())
    return jax.shard_map(
        on_device,
        mesh=fine,
        in_specs=placed,
        out_specs=(P(DP, "x"), P("x", DP)),
        check_vma=False,
    )
```

time: 934 us -> 353 us (0.38)
  blocking collectives: 296 us -> 0 us
  waiting for transfers between devices: 438 us -> 199 us
  matrix products: 101 us -> 6.42 us
  starting transfers between devices: 19.3 us -> 82.6 us
  local copies, waits for them, and re-layouts: 51.2 us -> 2.85 us
  Pallas kernels: 0 us -> 46.2 us
  between operations: 15.5 us -> 2.31 us
    all_to_all x2, waiting for transfers between devices: 361 us -> 55.4 us  [the longest x1 55.4 us: exchange_images(): return lax.all_to_all(outgoing, DP, split_axis=0, concat_axis=0, tiled=True)]
    psum x1 -> x0, blocking collectives: 296 us -> none  [on_device(): summed = lax.psum(head_part, 'dp')]
    ppermute x0 -> x24, waiting for transfers between devices: none -> 144 us  [the longest x9 111 us: around(): lax.ppermute(value, 'x', shifted(x_size, k))]
    dot_general x30 -> x1, matrix products: 101 us -> 6.42 us  [dot(): lax.dot_general(a, b, ((contract[:1], contract[1:]), ((), ())), preferred...]
    reduce_scatter x1 -> x0, waiting for transfers between devices: 77.3 us -> none  [on_device(): lax.psum_scatter(lax.dot_general(text_rows, proj_grad, (((0,), (0,)), (()...]
    ppermute x0 -> x24, starting transfers between devices: none -> 53.5 us  [the longest x8 31.6 us: on_device(): got = lax.ppermute(chunk, ('z', 'x'), pairs).astype(F32)]
    pallas_call x0 -> x3, Pallas kernels: none -> 46.2 us  [the longest x1 23.8 us: pick_blocks(): pl.pallas_call(copy_kernel, grid_spec=spec, out_shape=jax.ShapeDtypeStruc...]
    gather x8 -> x0, local copies, waits for them, and re-layouts: 35 us -> none  [visit_group(): image_rows = jnp.take(image_unit, which_block, axis=0)]
  transfers between devices with their start and end apart: 4 -> 26, of which waited for: 3 -> 14; matrix products, arithmetic and copies ran while one was open for 3% -> 3% of each run, Pallas kernels for 0% -> 5%
where the time goes in v1:
time: 353 us; the launch traced here: 347 us
  waiting for transfers between devices  199 us (56%)
  starting transfers between devices  82.6 us (23%)
  Pallas kernels  46.2 us (13%)
  other arithmetic  7.64 us (2%)
  matrix products  6.42 us (2%)
    ppermute x9, waiting for transfers between devices, around(): lax.ppermute(value, 'x', shifted(x_size, k))  111 us
    all_to_all x1, waiting for transfers between devices, exchange_images(): return lax.all_to_all(outgoing, DP, split_axis=0, concat_axis=0, tiled=True)  55.4 us
    ppermute x8, starting transfers between devices, on_device(): got = lax.ppermute(chunk, ('z', 'x'), pairs).astype(F32)  31.6 us
    pallas_call x1, Pallas kernels, pick_blocks(): pl.pallas_call(copy_kernel, grid_spec=spec, out_shape=jax.ShapeDtypeStruc...  23.8 us
    all_to_all x1, starting transfers between devices, exchange_images(): return lax.all_to_all(outgoing, DP, split_axis=0, concat_axis=0, tiled=True)  23.5 us
    ppermute x3, waiting for transfers between devices, on_device(): lax.ppermute(chunks[k].reshape(x_size * rows, part), 'x', shifted(x_size,...  19 us
    pallas_call x1, Pallas kernels, on_device(): pl.pallas_call(pair_kernel, out_shape=(jax.ShapeDtypeStruct((x_size, x_si...  16.4 us
    ppermute x3, starting transfers between devices, on_device(): lax.ppermute(total[k], 'y', shifted(y_size, k))  9.65 us
  transfers between devices with their start and end apart: 26, of which 14 were waited for; matrix products, arithmetic and copies ran while one was open for 3% of the time, Pallas kernels for 5%

profile of v1, /device:TPU:4, one launch (start us, length us, event | category | flops | bytes accessed | tf_op | source)
XLA Modules:
  0.0 347.0 jit_solution(2954482148976472606)
XLA Ops:
  5.7 23.8 %pick.1 = bf16[64,64,1024]{2,1,0:T(8,128)(2,1)} custom-call(s32[64]{0:T(128)} %select_reduce_fusion.2.picked, bf16[4,64,1024]{2,1,0:T(8,128)(2,1)} %fusion.1.from_ref.own_images), custom_call_target="tpu_custom_call" | custom-call | tf_op jit(solution)/shard_map/pick/pallas_call | solution.py:280
  29.5 23.5 %all-to-all-start = ((bf16[64,64,1024]{2,1,0:T(8,128)(2,1)}), bf16[64,64,1024]{2,1,0:T(8,128)(2,1)}, u32[]{:S(2)}, u32[]{:S(2)}) async-start(bf16[64,64,1024]{2,1,0:T(8,128)(2,1)} %pick.1), calls=%async_computation | async-start | bytes 16777216 | tf_op jit(solution)/shard_map/all_to_all | solution.py:290
  55.8 6.4 %multiply_reduce_fusion = (f32[256]{0:T(256)S(1)}, f32[256,1024]{1,0:T(8,128)S(1)}) fusion(bf16[256,4096]{1,0:T(8,128)(2,1)} %bitcast.5.feat_0, bf16[4096,1024]{1,0:T(8,128)(2,1)} %param.8), kind=kOutput, calls=%fused_computation.6 | convolution fusion | flops 2148007680 | bytes 11535360 | tf_op jit(solution)/shard_map/dot_general | solution.py:18
  62.3 2.9 collective-permute-start.4
  68.1 80.2 %collective-permute-done.4 = f32[4,64]{1,0:T(4,128)S(1)} collective-permute-done((f32[4,64]{1,0:T(4,128)S(1)}, f32[4,64]{1,0:T(4,128)S(1)}, u32[]{:S(2)}, u32[]{:S(2)}) %collective-permute-start.4) | collective-permute-done | bytes 1056 | tf_op jit(solution)/shard_map/ppermute | solution.py:165
  148.4 3.5 %collective-permute-done.5 = f32[4,64]{1,0:T(4,128)S(1)} collective-permute-done((f32[4,64]{1,0:T(4,128)S(1)}, f32[4,64]{1,0:T(4,128)S(1)}, u32[]{:S(2)}, u32[]{:S(2)}) %collective-permute-start.5) | collective-permute-done | bytes 1056 | tf_op jit(solution)/shard_map/ppermute | solution.py:165
  154.4 4.1 %collective-permute-done.3 = f32[4,64]{1,0:T(4,128)S(1)} collective-permute-done((f32[4,64]{1,0:T(4,128)S(1)}, f32[4,64]{1,0:T(4,128)S(1)}, u32[]{:S(2)}, u32[]{:S(2)}) %collective-permute-start.3) | collective-permute-done | bytes 1056 | tf_op jit(solution)/shard_map/ppermute | solution.py:165
  160.1 13.9 %collective-permute-done.1.text_2 = bf16[4,64,1024]{2,1,0:T(8,128)(2,1)S(1)} collective-permute-done((bf16[4,64,1024]{2,1,0:T(8,128)(2,1)S(1)}, bf16[4,64,1024]{2,1,0:T(8,128)(2,1)S(1)}, u32[]{:S(2)}, u32[]{:S(2)}) %collective-permute-start.1) | collective-permute-done | bytes 524320 | tf_op jit(solution)/shard_map/ppermute | solution.py:165
  174.0 9.6 %collective-permute-done.2.text_3 = bf16[4,64,1024]{2,1,0:T(8,128)(2,1)} collective-permute-done((bf16[4,64,1024]{2,1,0:T(8,128)(2,1)S(1)}, bf16[4,64,1024]{2,1,0:T(8,128)(2,1)}, u32[]{:S(2)}, u32[]{:S(2)}) %collective-permute-start.2) | collective-permute-done | bytes 524320 | tf_op jit(solution)/shard_map/ppermute | solution.py:165
  183.7 55.4 %all-to-all-done.arrived = bf16[64,64,1024]{2,1,0:T(8,128)(2,1)} async-done(((bf16[64,64,1024]{2,1,0:T(8,128)(2,1)}), bf16[64,64,1024]{2,1,0:T(8,128)(2,1)}, u32[]{:S(2)}, u32[]{:S(2)}) %all-to-all-start) | async-done | bytes 8388640 | tf_op jit(solution)/shard_map/all_to_all | solution.py:290
  239.1 16.4 %pairs.1 = (bf16[4,4,4,64,256]{4,3,2,1,0:T(8,128)(2,1)S(1)}, f32[64,1,64]{2,1,0:T(1,128)}, f32[4,1,64]{2,1,0:T(1,128)S(1)}) custom-call(s32[4,64]{1,0:T(4,128)S(1)} %select_reduce_fusion.1.sources, s32[4]{0:T(128)S(1)} %get-tuple-element.14.counts, s32[3]{0:T(128)S(1)} %pad_add_fusion.place, f32[2]{0:T(128)S(1)} %pad_maximum_fusion.1.scale_bias, ...), custom_call_target="tpu_custom_call" | custom-call | tf_op jit(solution)/shard_map/pairs/pallas_call | solution.py:191
  259.0 11.7 %collective-permute-done.6.grad_1 = bf16[1024,256]{1,0:T(8,128)(2,1)S(1)} collective-permute-done((bf16[1024,256]{1,0:T(8,128)(2,1)S(1)}, bf16[1024,256]{1,0:T(8,128)(2,1)S(1)}, u32[]{:S(2)}, u32[]{:S(2)}) %collective-permute-start.6) | collective-permute-done | bytes 524320 | tf_op jit(solution)/shard_map/ppermute | solution.py:218
  270.7 5.4 %collective-permute-done.7.grad_2 = bf16[1024,256]{1,0:T(8,128)(2,1)S(1)} collective-permute-done((bf16[1024,256]{1,0:T(8,128)(2,1)S(1)}, bf16[1024,256]{1,0:T(8,128)(2,1)S(1)}, u32[]{:S(2)}, u32[]{:S(2)}) %collective-permute-start.7) | collective-permute-done | bytes 524320 | tf_op jit(solution)/shard_map/ppermute | solution.py:218
  277.9 6.0 %head.1 = (bf16[128,4096]{1,0:T(8,128)(2,1)S(1)}, bf16[128,4096]{1,0:T(8,128)(2,1)S(1)}) custom-call(s32[3]{0:T(128)S(1)} %pad_add_fusion.place, bf16[1024,256]{1,0:T(8,128)(2,1)S(1)} %bitcast.57, bf16[1024,256]{1,0:T(8,128)(2,1)S(1)} %collective-permute-done.6.grad_1, bf16[1024,256]{1,0:T(8,128)(2,1)S(1)} %collective-permute-done.7.grad_2, ...), custom_call_target="tpu_custom_call" | custom-call | tf_op jit(solution)/shard_map/head/pallas_call | solution.py:223
  287.0 4.1 %collective-permute-start.13 = (bf16[32,4096]{1,0:T(8,128)(2,1)S(1)}, bf16[32,4096]{1,0:T(8,128)(2,1)S(1)}, u32[]{:S(2)}, u32[]{:S(2)}) collective-permute-start(bf16[32,4096]{1,0:T(8,128)(2,1)S(1)} %get-tuple-element.23), channel_id=1, source_target_pairs={{0,8},{8,16},{16,24},{24,0},{1,9},{9,17},{17,25},{25,1},{2,10},{10... | collective-permute-start | bytes 786440 | tf_op jit(solution)/shard_map/ppermute | solution.py:246
  291.1 3.0 collective-permute-start.14
  296.7 5.6 %all-to-all-start.1 = ((f32[64,1,64]{2,1,0:T(1,128)}), f32[64,1,64]{2,1,0:T(1,128)S(1)}, u32[]{:S(2)}, u32[]{:S(2)}) async-start(f32[64,1,64]{2,1,0:T(1,128)} %get-tuple-element.8), calls=%async_computation.1 | async-start | bytes 65536 | tf_op jit(solution)/shard_map/all_to_all | solution.py:208
  302.3 4.0 %collective-permute-done.14 = bf16[32,4096]{1,0:T(8,128)(2,1)S(1)} collective-permute-done((bf16[32,4096]{1,0:T(8,128)(2,1)S(1)}, bf16[32,4096]{1,0:T(8,128)(2,1)S(1)}, u32[]{:S(2)}, u32[]{:S(2)}) %collective-permute-start.14) | collective-permute-done | bytes 262176 | tf_op jit(solution)/shard_map/ppermute | solution.py:246
  307.2 5.5 %collective-permute-start.16 = (bf16[16,1024]{1,0:T(8,128)(2,1)S(1)}, bf16[16,1024]{1,0:T(8,128)(2,1)S(1)}, u32[]{:S(2)}, u32[]{:S(2)}) collective-permute-start(bf16[16,1024]{1,0:T(8,128)(2,1)S(1)} %bitcast.68), channel_id=1, source_target_pairs={{0,0},{1,64},{2,128},{3,192},{32,1},{33,65},{34,129},{35,193},{64,... | collective-permute-start | bytes 98312 | tf_op jit(solution)/shard_map/ppermute | solution.py:263
  312.7 2.9 collective-permute-start.17
  315.6 3.3 collective-permute-start.18
  319.1 9.5 %collective-permute-start.19 = (bf16[16,1024]{1,0:T(8,128)(2,1)S(1)}, bf16[16,1024]{1,0:T(8,128)(2,1)S(1)}, u32[]{:S(2)}, u32[]{:S(2)}) collective-permute-start(bf16[16,1024]{1,0:T(8,128)(2,1)S(1)} %bitcast.66), channel_id=1, source_target_pairs={{0,3},{1,67},{2,131},{3,195},{32,32},{33,96},{34,160},{35,224},{64... | collective-permute-start | bytes 98312 | tf_op jit(solution)/shard_map/ppermute | solution.py:263
  328.7 5.1 %collective-permute-start.21 = (bf16[16,1024]{1,0:T(8,128)(2,1)S(1)}, bf16[16,1024]{1,0:T(8,128)(2,1)S(1)}, u32[]{:S(2)}, u32[]{:S(2)}) collective-permute-start(bf16[16,1024]{1,0:T(8,128)(2,1)S(1)} %bitcast.71), channel_id=1, source_target_pairs={{0,33},{1,97},{2,161},{3,225},{32,34},{33,98},{34,162},{35,226},{6... | collective-permute-start | bytes 98312 | tf_op jit(solution)/shard_map/ppermute | solution.py:263
  340.0 6.0 %collective-permute-done.22 = bf16[16,1024]{1,0:T(8,128)(2,1)S(1)} collective-permute-done((bf16[16,1024]{1,0:T(8,128)(2,1)S(1)}, bf16[16,1024]{1,0:T(8,128)(2,1)S(1)}, u32[]{:S(2)}, u32[]{:S(2)}) %collective-permute-start.22) | collective-permute-done | bytes 32800 | tf_op jit(solution)/shard_map/ppermute | solution.py:263
  (89 shorter events, 32.9 us)
Async XLA Ops:
  29.5 209.5 %all-to-all-start = ((bf16[64,64,1024]{2,1,0:T(8,128)(2,1)}), bf16[64,64,1024]{2,1,0:T(8,128)(2,1)}, u32[]{:S(2)}, u32[]{:S(2)}) async-start(bf16[64,64,1024]{2,1,0:T(8,128)(2,1)} %pick.1), calls=%async_computation | async-start | bytes 16777216 | tf_op jit(solution)/shard_map/all_to_all | solution.py:290
  53.0 204.8 %collective-permute-start.10 = (bf16[256,4096]{1,0:T(8,128)(2,1)}, bf16[256,4096]{1,0:T(8,128)(2,1)}, u32[]{:S(2)}, u32[]{:S(2)}) collective-permute-start(bf16[256,4096]{1,0:T(8,128)(2,1)} %bitcast.5.feat_0), channel_id=1, source_target_pairs={{0,2},{1,3},{2,0},{3,1},{4,6},{5,7},{6,4},{7,5},{8,10},{9,11},{10,... | collective-permute-start | bytes 6291464 | tf_op jit(solution)/shard_map/ppermute | solution.py:165
  53.6 205.3 %collective-permute-start.11 = (bf16[256,4096]{1,0:T(8,128)(2,1)}, bf16[256,4096]{1,0:T(8,128)(2,1)}, u32[]{:S(2)}, u32[]{:S(2)}) collective-permute-start(bf16[256,4096]{1,0:T(8,128)(2,1)} %bitcast.5.feat_0), channel_id=1, source_target_pairs={{0,3},{1,0},{2,1},{3,2},{4,7},{5,4},{6,5},{7,6},{8,11},{9,8},{10,9... | collective-permute-start | bytes 6291464 | tf_op jit(solution)/shard_map/ppermute | solution.py:165
  55.8 203.2 %collective-permute-start.9 = (bf16[256,4096]{1,0:T(8,128)(2,1)}, bf16[256,4096]{1,0:T(8,128)(2,1)}, u32[]{:S(2)}, u32[]{:S(2)}) collective-permute-start(bf16[256,4096]{1,0:T(8,128)(2,1)} %bitcast.5.feat_0), channel_id=1, source_target_pairs={{0,1},{1,2},{2,3},{3,0},{4,5},{5,6},{6,7},{7,4},{8,9},{9,10},{10,1... | collective-permute-start | bytes 6291464 | tf_op jit(solution)/shard_map/ppermute | solution.py:165
  62.3 86.1 %collective-permute-start.4 = (f32[4,64]{1,0:T(4,128)S(1)}, f32[4,64]{1,0:T(4,128)S(1)}, u32[]{:S(2)}, u32[]{:S(2)}) collective-permute-start(f32[4,64]{1,0:T(4,128)S(1)} %rsqrt.32), channel_id=1, source_target_pairs={{0,2},{1,3},{2,0},{3,1},{4,6},{5,7},{6,4},{7,5},{8,10},{9,11},{10,... | collective-permute-start | bytes 3080 | tf_op jit(solution)/shard_map/ppermute | solution.py:165
  65.3 93.8 %collective-permute-start = (bf16[4,64,1024]{2,1,0:T(8,128)(2,1)S(1)}, bf16[4,64,1024]{2,1,0:T(8,128)(2,1)S(1)}, u32[]{:S(2)}, u32[]{:S(2)}) collective-permute-start(bf16[4,64,1024]{2,1,0:T(8,128)(2,1)S(1)} %bitcast.53), channel_id=1, source_target_pairs={{0,1},{1,2},{2,3},{3,0},{4,5},{5,6},{6,7},{7,4},{8,9},{9,10},{10,1... | collective-permute-start | bytes 1572872 | tf_op jit(solution)/shard_map/ppermute | solution.py:165
  151.9 6.7 %collective-permute-start.3 = (f32[4,64]{1,0:T(4,128)S(1)}, f32[4,64]{1,0:T(4,128)S(1)}, u32[]{:S(2)}, u32[]{:S(2)}) collective-permute-start(f32[4,64]{1,0:T(4,128)S(1)} %rsqrt.32), channel_id=1, source_target_pairs={{0,1},{1,2},{2,3},{3,0},{4,5},{5,6},{6,7},{7,4},{8,9},{9,10},{10,1... | collective-permute-start | bytes 3080 | tf_op jit(solution)/shard_map/ppermute | solution.py:165
  158.6 15.5 %collective-permute-start.1 = (bf16[4,64,1024]{2,1,0:T(8,128)(2,1)S(1)}, bf16[4,64,1024]{2,1,0:T(8,128)(2,1)S(1)}, u32[]{:S(2)}, u32[]{:S(2)}) collective-permute-start(bf16[4,64,1024]{2,1,0:T(8,128)(2,1)S(1)} %bitcast.54), channel_id=1, source_target_pairs={{0,2},{1,3},{2,0},{3,1},{4,6},{5,7},{6,4},{7,5},{8,10},{9,11},{10,... | collective-permute-start | bytes 1572872 | tf_op jit(solution)/shard_map/ppermute | solution.py:165
  159.1 24.6 %collective-permute-start.2 = (bf16[4,64,1024]{2,1,0:T(8,128)(2,1)S(1)}, bf16[4,64,1024]{2,1,0:T(8,128)(2,1)}, u32[]{:S(2)}, u32[]{:S(2)}) collective-permute-start(bf16[4,64,1024]{2,1,0:T(8,128)(2,1)S(1)} %bitcast.55), channel_id=1, source_target_pairs={{0,3},{1,0},{2,1},{3,2},{4,7},{5,4},{6,5},{7,6},{8,11},{9,8},{10,9... | collective-permute-start | bytes 1572872 | tf_op jit(solution)/shard_map/ppermute | solution.py:165
  255.7 15.0 %collective-permute-start.6 = (bf16[1024,256]{1,0:T(8,128)(2,1)S(1)}, bf16[1024,256]{1,0:T(8,128)(2,1)S(1)}, u32[]{:S(2)}, u32[]{:S(2)}) collective-permute-start(bf16[1024,256]{1,0:T(8,128)(2,1)S(1)} %bitcast.61), channel_id=1, source_target_pairs={{0,1},{1,2},{2,3},{3,0},{4,5},{5,6},{6,7},{7,4},{8,9},{9,10},{10,1... | collective-permute-start | bytes 1572872 | tf_op jit(solution)/shard_map/ppermute | solution.py:218
  257.0 19.1 %collective-permute-start.7 = (bf16[1024,256]{1,0:T(8,128)(2,1)S(1)}, bf16[1024,256]{1,0:T(8,128)(2,1)S(1)}, u32[]{:S(2)}, u32[]{:S(2)}) collective-permute-start(bf16[1024,256]{1,0:T(8,128)(2,1)S(1)} %bitcast.60), channel_id=1, source_target_pairs={{0,2},{1,3},{2,0},{3,1},{4,6},{5,7},{6,4},{7,5},{8,10},{9,11},{10,... | collective-permute-start | bytes 1572872 | tf_op jit(solution)/shard_map/ppermute | solution.py:218
  257.8 20.1 %collective-permute-start.8 = (bf16[1024,256]{1,0:T(8,128)(2,1)S(1)}, bf16[1024,256]{1,0:T(8,128)(2,1)S(1)}, u32[]{:S(2)}, u32[]{:S(2)}) collective-permute-start(bf16[1024,256]{1,0:T(8,128)(2,1)S(1)} %bitcast.59), channel_id=1, source_target_pairs={{0,3},{1,0},{2,1},{3,2},{4,7},{5,4},{6,5},{7,6},{8,11},{9,8},{10,9... | collective-permute-start | bytes 1572872 | tf_op jit(solution)/shard_map/ppermute | solution.py:218
  287.0 15.3 %collective-permute-start.13 = (bf16[32,4096]{1,0:T(8,128)(2,1)S(1)}, bf16[32,4096]{1,0:T(8,128)(2,1)S(1)}, u32[]{:S(2)}, u32[]{:S(2)}) collective-permute-start(bf16[32,4096]{1,0:T(8,128)(2,1)S(1)} %get-tuple-element.23), channel_id=1, source_target_pairs={{0,8},{8,16},{16,24},{24,0},{1,9},{9,17},{17,25},{25,1},{2,10},{10... | collective-permute-start | bytes 786440 | tf_op jit(solution)/shard_map/ppermute | solution.py:246
  291.1 15.2 %collective-permute-start.14 = (bf16[32,4096]{1,0:T(8,128)(2,1)S(1)}, bf16[32,4096]{1,0:T(8,128)(2,1)S(1)}, u32[]{:S(2)}, u32[]{:S(2)}) collective-permute-start(bf16[32,4096]{1,0:T(8,128)(2,1)S(1)} %get-tuple-element.25), channel_id=1, source_target_pairs={{0,16},{8,24},{16,0},{24,8},{1,17},{9,25},{17,1},{25,9},{2,18},{10... | collective-permute-start | bytes 786440 | tf_op jit(solution)/shard_map/ppermute | solution.py:246
  294.1 12.1 %collective-permute-start.15 = (bf16[32,4096]{1,0:T(8,128)(2,1)S(1)}, bf16[32,4096]{1,0:T(8,128)(2,1)S(1)}, u32[]{:S(2)}, u32[]{:S(2)}) collective-permute-start(bf16[32,4096]{1,0:T(8,128)(2,1)S(1)} %get-tuple-element.24), channel_id=1, source_target_pairs={{0,24},{8,0},{16,8},{24,16},{1,25},{9,1},{17,9},{25,17},{2,26},{10... | collective-permute-start | bytes 786440 | tf_op jit(solution)/shard_map/ppermute | solution.py:246
  296.7 22.2 %all-to-all-start.1 = ((f32[64,1,64]{2,1,0:T(1,128)}), f32[64,1,64]{2,1,0:T(1,128)S(1)}, u32[]{:S(2)}, u32[]{:S(2)}) async-start(f32[64,1,64]{2,1,0:T(1,128)} %get-tuple-element.8), calls=%async_computation.1 | async-start | bytes 65536 | tf_op jit(solution)/shard_map/all_to_all | solution.py:208
  307.2 21.5 %collective-permute-start.16 = (bf16[16,1024]{1,0:T(8,128)(2,1)S(1)}, bf16[16,1024]{1,0:T(8,128)(2,1)S(1)}, u32[]{:S(2)}, u32[]{:S(2)}) collective-permute-start(bf16[16,1024]{1,0:T(8,128)(2,1)S(1)} %bitcast.68), channel_id=1, source_target_pairs={{0,0},{1,64},{2,128},{3,192},{32,1},{33,65},{34,129},{35,193},{64,... | collective-permute-start | bytes 98312 | tf_op jit(solution)/shard_map/ppermute | solution.py:263
  312.7 21.2 %collective-permute-start.17 = (bf16[16,1024]{1,0:T(8,128)(2,1)S(1)}, bf16[16,1024]{1,0:T(8,128)(2,1)S(1)}, u32[]{:S(2)}, u32[]{:S(2)}) collective-permute-start(bf16[16,1024]{1,0:T(8,128)(2,1)S(1)} %bitcast.65), channel_id=1, source_target_pairs={{0,1},{1,65},{2,129},{3,193},{32,2},{33,66},{34,130},{35,194},{64,... | collective-permute-start | bytes 98312 | tf_op jit(solution)/shard_map/ppermute | solution.py:263
  315.6 20.7 %collective-permute-start.18 = (bf16[16,1024]{1,0:T(8,128)(2,1)S(1)}, bf16[16,1024]{1,0:T(8,128)(2,1)S(1)}, u32[]{:S(2)}, u32[]{:S(2)}) collective-permute-start(bf16[16,1024]{1,0:T(8,128)(2,1)S(1)} %bitcast.64), channel_id=1, source_target_pairs={{0,2},{1,66},{2,130},{3,194},{32,3},{33,67},{34,131},{35,195},{64,... | collective-permute-start | bytes 98312 | tf_op jit(solution)/shard_map/ppermute | solution.py:263
  319.1 20.7 %collective-permute-start.19 = (bf16[16,1024]{1,0:T(8,128)(2,1)S(1)}, bf16[16,1024]{1,0:T(8,128)(2,1)S(1)}, u32[]{:S(2)}, u32[]{:S(2)}) collective-permute-start(bf16[16,1024]{1,0:T(8,128)(2,1)S(1)} %bitcast.66), channel_id=1, source_target_pairs={{0,3},{1,67},{2,131},{3,195},{32,32},{33,96},{34,160},{35,224},{64... | collective-permute-start | bytes 98312 | tf_op jit(solution)/shard_map/ppermute | solution.py:263
  328.6 11.2 %collective-permute-start.20 = (bf16[16,1024]{1,0:T(8,128)(2,1)S(1)}, bf16[16,1024]{1,0:T(8,128)(2,1)S(1)}, u32[]{:S(2)}, u32[]{:S(2)}) collective-permute-start(bf16[16,1024]{1,0:T(8,128)(2,1)S(1)} %bitcast.69), channel_id=1, source_target_pairs={{0,32},{1,96},{2,160},{3,224},{32,33},{33,97},{34,161},{35,225},{6... | collective-permute-start | bytes 98312 | tf_op jit(solution)/shard_map/ppermute | solution.py:263
  328.7 11.2 %collective-permute-start.21 = (bf16[16,1024]{1,0:T(8,128)(2,1)S(1)}, bf16[16,1024]{1,0:T(8,128)(2,1)S(1)}, u32[]{:S(2)}, u32[]{:S(2)}) collective-permute-start(bf16[16,1024]{1,0:T(8,128)(2,1)S(1)} %bitcast.71), channel_id=1, source_target_pairs={{0,33},{1,97},{2,161},{3,225},{32,34},{33,98},{34,162},{35,226},{6... | collective-permute-start | bytes 98312 | tf_op jit(solution)/shard_map/ppermute | solution.py:263
  333.9 12.1 %collective-permute-start.22 = (bf16[16,1024]{1,0:T(8,128)(2,1)S(1)}, bf16[16,1024]{1,0:T(8,128)(2,1)S(1)}, u32[]{:S(2)}, u32[]{:S(2)}) collective-permute-start(bf16[16,1024]{1,0:T(8,128)(2,1)S(1)} %bitcast.70), channel_id=1, source_target_pairs={{0,34},{1,98},{2,162},{3,226},{32,35},{33,99},{34,163},{35,227},{6... | collective-permute-start | bytes 98312 | tf_op jit(solution)/shard_map/ppermute | solution.py:263
  336.3 10.0 %collective-permute-start.23 = (bf16[16,1024]{1,0:T(8,128)(2,1)S(1)}, bf16[16,1024]{1,0:T(8,128)(2,1)S(1)}, u32[]{:S(2)}, u32[]{:S(2)}) collective-permute-start(bf16[16,1024]{1,0:T(8,128)(2,1)S(1)} %bitcast.67), channel_id=1, source_target_pairs={{0,35},{1,99},{2,163},{3,227},{32,0},{33,64},{34,128},{35,192},{64... | collective-permute-start | bytes 98312 | tf_op jit(solution)/shard_map/ppermute | solution.py:263
  (6 other events, 220.6 us)

commit v2 on v1

v2 whole, which is shorter than its diff:
```python
import functools

import jax
import jax.numpy as jnp
from jax import lax
from jax.experimental import pallas as pl
from jax.experimental.pallas import tpu as pltpu
from jax.sharding import Mesh, PartitionSpec as P

EPSILON = 1e-06
DP = ("z", "y", "c")
GROUP = 4
EXTRA = 128
F32 = jnp.float32
BF16 = jnp.bfloat16


def dot(a, b, contract):
    return lax.dot_general(a, b, ((contract[:1], contract[1:]), ((), ())), preferred_element_type=F32)


def unit_rows(values):
    inverse = lax.rsqrt(jnp.sum(values * values, axis=-1, keepdims=True) + EPSILON)
    return (values * inverse, inverse)


def shifted(size, shift):
    return [(i, (i + shift) % size) for i in range(size)]


def loss_and_weight(logits):
    small = jnp.exp(-jnp.abs(logits))
    share = 1.0 / (1.0 + small)
    weight = jnp.where(logits >= 0, share, small * share)
    return (jnp.maximum(logits, 0.0) + jnp.log1p(small), weight)


def project_kernel(features, weight, out, acc):
    step = pl.program_id(0)

    @pl.when(step == 0)
    def _():
        acc[...] = jnp.zeros_like(acc)

    acc[...] += dot(features[...], weight[...], (1, 0))

    @pl.when(step == pl.num_programs(0) - 1)
    def _():
        unit, inverse = unit_rows(acc[...])
        width = unit.shape[1]
        out[:, :width] = unit.astype(BF16)
        first = inverse.astype(BF16).astype(F32)
        second = (inverse - first).astype(BF16).astype(F32)
        third = inverse - first - second
        lane = lax.broadcasted_iota(jnp.int32, (unit.shape[0], EXTRA), 1)
        terms = jnp.where(lane == 0, first, jnp.where(lane == 1, second, jnp.where(lane == 2, third, 0.0)))
        out[:, width:] = terms.astype(BF16)


def pair_kernel(sources, slots, counts, place, scale_bias, *refs, starts):
    quarters = 4
    texts, refs = refs[:quarters], refs[quarters:]
    own_images, image_docs, text_docs, *arriving = refs[:-7]
    chunks, pair_loss, own_loss, text_all, arrived, acc, sems = refs[-7:]
    blocks, piece_rows, width = own_images.shape
    part = width // quarters
    scale, bias = scale_bias[0], scale_bias[1]
    copies = []
    for n, (ref, at) in enumerate(zip(arriving, starts)):
        copies.append(pltpu.make_async_copy(ref, arrived.at[pl.ds(at, ref.shape[0])], sems.at[n]))
        copies[-1].start()
    for k in range(quarters):
        to = pl.multiple_of(lax.rem(place[0] - k + quarters, quarters) * piece_rows, piece_rows)
        text_all[:, pl.ds(to, piece_rows), :] = texts[k][...].reshape(blocks, piece_rows, width + EXTRA)
    pair_loss[...] = jnp.zeros_like(pair_loss)
    for copy in copies:
        copy.wait()

    def each_block(t, carry):
        text = text_all[t, :, :width]
        images = own_images[t]
        logits = scale * dot(text, images, (1, 1)) + bias
        same = text_docs[t] == image_docs[t]
        sign = jnp.where(same, 1.0, -1.0)
        loss, weight = loss_and_weight(-sign * logits)
        own_loss[pl.ds(t, 1)] = jnp.sum(loss, axis=0, keepdims=True)[None]
        acc[...] = dot((-sign * weight).astype(BF16), images, (1, 0))
        count = counts[t]

        def each_group(g, inner):
            held = [slots[t, g * GROUP + i] for i in range(GROUP)]
            rows = jnp.concatenate([arrived[held[i]] for i in range(GROUP)], axis=0)
            values = scale * dot(text, rows, (1, 1)) + bias
            terms, shares = loss_and_weight(values)
            sums = jnp.sum(terms, axis=0, keepdims=True)
            left = (count - g * GROUP) * piece_rows
            live = lax.broadcasted_iota(jnp.int32, shares.shape, 1) < left
            shares = jnp.where(live, shares, 0.0).astype(BF16)
            acc[...] += dot(shares, rows, (1, 0))
            for i in range(GROUP):

                @pl.when(g * GROUP + i < count)
                def _():
                    source = sources[t, g * GROUP + i]
                    pair_loss[pl.ds(source, 1)] = sums[:, i * piece_rows : (i + 1) * piece_rows][None]

            return inner

        lax.fori_loop(0, (count + GROUP - 1) // GROUP, each_group, 0)
        inverse = jnp.sum(text_all[t, :, width:].astype(F32), axis=-1, keepdims=True)
        unit = text.astype(F32)
        grad = scale * acc[...]
        along = jnp.sum(unit * grad, axis=-1, keepdims=True)
        acc[...] = (grad - unit * along) * inverse
        for k in range(quarters):
            start = pl.multiple_of(lax.rem(place[0] + k, quarters) * part, part)
            values = acc[:, pl.ds(start, part)].astype(BF16)
            for j in range(quarters):
                chunks[k, j, pl.ds(t, 1)] = values[j * piece_rows : (j + 1) * piece_rows][None]
        return carry

    lax.fori_loop(0, blocks, each_block, 0)


def pick_kernel(table, place, *refs, steps, sizes):
    z_size, y_size, c_size = sizes
    count = len(steps)
    from_refs, to_refs, sems = refs[:count], refs[count:-1], refs[-1]
    copies = []
    for dy in range(y_size):
        for dc in range(c_size):
            y = lax.rem(place[1] + dy, y_size)
            c = lax.rem(place[2] + dc, c_size)
            for j, step in enumerate(steps):
                z = lax.rem(place[3] - step + z_size, z_size)
                block = table[z, y * c_size + c]
                n = dy * c_size + dc
                copies.append(
                    pltpu.make_async_copy(from_refs[j].at[block], to_refs[n].at[j], sems.at[n * count + j])
                )
    for copy in copies:
        copy.start()
    for copy in copies:
        copy.wait()


def head_kernel(place, grad_0, grad_1, grad_2, grad_3, feats, keep, give, turned, *, sizes, strip):
    z_part, y_size, c_size = sizes

    @pl.when(pl.program_id(0) == 0)
    def _():
        total = sum(g[...].astype(F32) for g in (grad_0, grad_1, grad_2, grad_3))
        flipped = total.T.astype(BF16)
        for zz in range(z_part):
            for y in range(y_size):
                for c in range(c_size):
                    block = flipped[((zz * y_size + y) * c_size + c) * strip :][:strip]
                    y_rel = lax.rem(y - place[1] + y_size, y_size)
                    c_rel = lax.rem(c - place[2] + c_size, c_size)
                    to = ((c_rel * y_size + y_rel) * z_part + zz) * strip
                    turned[pl.ds(pl.multiple_of(to, strip), strip)] = block

    half = keep.shape[0]
    total = dot(turned[...], feats[...], (1, 0)).astype(BF16)
    keep[...] = total[:half]
    give[...] = total[half:]


def whole(memory=pltpu.VMEM):
    return pl.BlockSpec(memory_space=memory)


def on_device(
    text_features, head_weight, image_embeds, doc_ids, hard_lists, logit_scale, logit_bias
):
    z_size, y_size, c_size, x_size = (lax.axis_size(name) for name in ("z", "y", "c", "x"))
    z, y, c, x = (lax.axis_index(name) for name in ("z", "y", "c", "x"))
    dp_count = z_size * y_size * c_size
    dp_index = (z * y_size + y) * c_size + c
    blocks, _, piece_rows, feat_width = text_features.shape
    block_rows = image_embeds.shape[1]
    emb_width = head_weight.shape[1]
    rows = blocks * piece_rows
    part = emb_width // x_size
    strip = emb_width // dp_count
    block_iota = jnp.arange(blocks, dtype=jnp.int32)
    peer_iota = jnp.arange(dp_count, dtype=jnp.int32)
    place = jnp.stack([x, y, c, z]).astype(jnp.int32)
    features = text_features.reshape(rows, feat_width)
    feats = lax.all_gather(features, "x", axis=0, tiled=False)

    owners = jnp.where(hard_lists >= 0, hard_lists // blocks, -1).reshape(dp_count, blocks, -1)
    line = owners.reshape(z_size, y_size * c_size, blocks, -1)
    line = lax.dynamic_index_in_dim(line, y * c_size + c, 1, keepdims=False)
    plane = z * y_size * c_size + jnp.arange(y_size * c_size, dtype=jnp.int32)
    wanted = jnp.any(line[:, None] == plane[:, None, None], axis=3)
    table = jnp.sum(wanted.astype(jnp.int32) * block_iota, axis=2)

    own_images = lax.dynamic_slice_in_dim(image_embeds, x * piece_rows, piece_rows, 1)
    own_images = unit_rows(own_images.astype(F32))[0].astype(BF16)
    groups = exchange_images(own_images, table, place, (z_size, y_size, c_size))

    tile = min(1024, feat_width)
    text_emb = pl.pallas_call(
        project_kernel,
        grid=(feat_width // tile,),
        out_shape=jax.ShapeDtypeStruct((rows, emb_width + EXTRA), BF16),
        in_specs=[
            pl.BlockSpec((rows, tile), lambda i: (0, i)),
            pl.BlockSpec((tile, emb_width), lambda i: (i, 0)),
        ],
        out_specs=pl.BlockSpec((rows, emb_width + EXTRA), lambda i: (0, 0)),
        scratch_shapes=[pltpu.VMEM((rows, emb_width), F32)],
        compiler_params=pltpu.CompilerParams(vmem_limit_bytes=32 << 20),
        cost_estimate=pl.CostEstimate(
            flops=2 * rows * feat_width * emb_width, bytes_accessed=12 << 20, transcendentals=0
        ),
        name="project",
    )(features, head_weight)
    texts = [text_emb] + [
        lax.ppermute(text_emb, "x", shifted(x_size, k)) for k in range(1, x_size)
    ]

    hit = owners == dp_index
    listed = jnp.any(hit, axis=(1, 2))
    which = jnp.sum(hit * (hard_lists % blocks).reshape(owners.shape), axis=(1, 2))
    mine = listed[None] & (which[None] == block_iota[:, None])
    before = peer_iota[None] < peer_iota[:, None]
    order = jnp.sum((mine[:, None] & before).astype(jnp.int32), axis=2)
    counts = jnp.sum(mine.astype(jnp.int32), axis=1)
    at = mine[:, None] & (order[:, None] == peer_iota[:, None])
    sources = jnp.sum(jnp.where(at, peer_iota, 0), axis=2)
    back = (z - peer_iota // (y_size * c_size)) % z_size
    turn = jnp.where(2 * back <= z_size, jnp.maximum(2 * back - 1, 0), 2 * (z_size - back))
    over_y = (y - peer_iota // c_size) % y_size
    over_c = (c - peer_iota) % c_size
    slots = jnp.sum(jnp.where(at, (over_y * c_size + over_c) * z_size + turn, 0), axis=2)

    text_docs = doc_ids.reshape(blocks, block_rows, 1)
    image_docs = lax.dynamic_slice_in_dim(doc_ids, x * piece_rows, piece_rows, 1)[:, None]
    scale_bias = jnp.stack([logit_scale, logit_bias])
    arriving, starts, turns = [], [], 0
    for group in groups:
        arriving += group
        starts += [n * z_size + turns for n in range(len(group))]
        turns += group[0].shape[0]

    chunks, pair_loss, own_loss = pl.pallas_call(
        functools.partial(pair_kernel, starts=starts),
        out_shape=(
            jax.ShapeDtypeStruct((x_size, x_size, blocks, piece_rows, part), BF16),
            jax.ShapeDtypeStruct((dp_count, 1, piece_rows), F32),
            jax.ShapeDtypeStruct((blocks, 1, piece_rows), F32),
        ),
        in_specs=[whole(pltpu.SMEM)] * 5 + [whole()] * 7 + [whole(pl.ANY)] * len(arriving),
        out_specs=(whole(), whole(), whole()),
        scratch_shapes=[
            pltpu.VMEM((blocks, block_rows, emb_width + EXTRA), BF16),
            pltpu.VMEM((dp_count, piece_rows, emb_width), BF16),
            pltpu.VMEM((block_rows, emb_width), F32),
            pltpu.SemaphoreType.DMA((len(arriving),)),
        ],
        compiler_params=pltpu.CompilerParams(vmem_limit_bytes=48 << 20),
        cost_estimate=pl.CostEstimate(flops=8 << 30, bytes_accessed=20 << 20, transcendentals=4 << 20),
        name="pairs",
    )(sources, slots, counts, place, scale_bias, *texts, own_images, image_docs, text_docs, *arriving)

    grads = [chunks[0].reshape(x_size * rows, part)]
    for k in range(1, x_size):
        grads.append(
            lax.ppermute(chunks[k].reshape(x_size * rows, part), "x", shifted(x_size, k))
        )
    z_part = z_size // x_size
    half = part // c_size
    keep, give = pl.pallas_call(
        functools.partial(head_kernel, sizes=(z_part, y_size, c_size), strip=strip),
        grid=(feat_width // tile,),
        out_shape=(
            jax.ShapeDtypeStruct((half, feat_width), BF16),
            jax.ShapeDtypeStruct((half, feat_width), BF16),
        ),
        in_specs=[whole(pltpu.SMEM)]
        + [whole()] * 4
        + [pl.BlockSpec((x_size * rows, tile), lambda i: (0, i))],
        out_specs=(
            pl.BlockSpec((half, tile), lambda i: (0, i)),
            pl.BlockSpec((half, tile), lambda i: (0, i)),
        ),
        scratch_shapes=[pltpu.VMEM((part, x_size * rows), BF16)],
        compiler_params=pltpu.CompilerParams(vmem_limit_bytes=48 << 20),
        cost_estimate=pl.CostEstimate(
            flops=2 * rows * feat_width * emb_width, bytes_accessed=16 << 20, transcendentals=0
        ),
        name="head",
    )(place, *grads, feats.reshape(x_size * rows, feat_width))

    asker = jnp.sum(jnp.any(hit, axis=2).astype(jnp.int32) * block_iota, axis=1)
    spread = jnp.where(asker[:, None, None] == block_iota[:, None], pair_loss, 0.0)
    remote_loss = lax.psum_scatter(spread.reshape(dp_count * blocks, piece_rows), DP, tiled=True)
    row_loss = (own_loss.reshape(blocks, piece_rows) + remote_loss) / block_rows
    return (row_loss, add_over_dp(keep, give, (z_size, y_size, c_size, x_size), z, strip))


def add_over_dp(keep, give, sizes, z, strip):
    z_size, y_size, c_size, x_size = sizes
    z_part = z_size // x_size
    width = keep.shape[1]

    def add(*values):
        return sum(v.astype(F32) for v in values).astype(BF16)

    total = add(keep, lax.ppermute(give, "c", shifted(c_size, 1)))
    total = total.reshape(y_size, z_part * strip, width)
    total = add(
        total[0], *(lax.ppermute(total[k], "y", shifted(y_size, k)) for k in range(1, y_size))
    ).reshape(z_part, strip, width)
    low, top = z % 2, z // (z_size // 2)
    given = lax.dynamic_index_in_dim(total, 1 - low, 0, keepdims=False)
    kept = lax.dynamic_index_in_dim(total, low, 0, keepdims=False)
    total = add(kept, lax.ppermute(given, "z", [(i, i ^ 1) for i in range(z_size)]))
    total = total.reshape(strip, 2, width // 2)
    given = lax.dynamic_index_in_dim(total, 1 - top, 1, keepdims=False)
    kept = lax.dynamic_index_in_dim(total, top, 1, keepdims=False)
    total = add(kept, lax.ppermute(given, "z", [(i, (i + z_size // 2) % z_size) for i in range(z_size)]))
    total = total.reshape(strip, 2, width // 4)
    final = 0.0
    for flip in range(2):
        pairs = []
        for z_from in range(z_size):
            bit = (z_from // 2 % 2) ^ flip
            for x_from in range(x_size):
                to_z, to_x = z_part * x_from + z_from % 2, z_from // (z_size // 2) * 2 + bit
                pairs.append((z_from * x_size + x_from, to_z * x_size + to_x))
        chunk = lax.dynamic_index_in_dim(total, (z // 2 % 2) ^ flip, 1, keepdims=False)
        final = final + lax.ppermute(chunk, ("z", "x"), pairs).astype(F32)
    return final.T


def exchange_images(own_images, table, place, sizes):
    z_size, y_size, c_size = sizes
    blocks = own_images.shape[0]
    up = down = own_images
    steps = [[(0, own_images)]]
    for k in range(1, z_size // 2):
        up = lax.ppermute(up, "z", shifted(z_size, 1))
        down = lax.ppermute(down, "z", shifted(z_size, -1))
        steps.append([(k, up), (-k, down)])
    up = lax.ppermute(up[: blocks // 2], "z", shifted(z_size, 1))
    down = lax.ppermute(down[blocks // 2 :], "z", shifted(z_size, -1))
    steps[-1].append((z_size // 2, jnp.concatenate([up, down], axis=0)))
    groups = []
    for group in steps:
        count = len(group)
        shape = (count,) + own_images.shape[1:]
        picked = pl.pallas_call(
            functools.partial(pick_kernel, steps=[k for k, _ in group], sizes=sizes),
            out_shape=[jax.ShapeDtypeStruct(shape, BF16)] * (y_size * c_size),
            in_specs=[whole(pltpu.SMEM)] * 2 + [whole(pl.ANY)] * count,
            out_specs=[whole(pl.ANY)] * (y_size * c_size),
            scratch_shapes=[pltpu.SemaphoreType.DMA((y_size * c_size * count,))],
            name="pick",
        )(table, place, *(v for _, v in group))
        got = [picked[0]]
        for n in range(1, y_size * c_size):
            dy, dc = n // c_size, n % c_size
            pairs = [
                (y * c_size + c, (y + dy) % y_size * c_size + (c + dc) % c_size)
                for y in range(y_size)
                for c in range(c_size)
            ]
            got.append(lax.ppermute(picked[n], ("y", "c"), pairs))
        groups.append(got)
    return groups


def solution(mesh):
    x_size = mesh.shape["replica"]
    c_size = 2
    z_size = 2 * x_size
    y_size = mesh.shape["dp"] // (z_size * c_size)
    fine = Mesh(mesh.devices.reshape(z_size, y_size, c_size, x_size), ("z", "y", "c", "x"))
    placed = (P(DP, "x", None, None), P(), P(DP, None, None), P(DP, None), P(), P(), P())
    return jax.shard_map(
        on_device,
        mesh=fine,
        in_specs=placed,
        out_specs=(P(DP, "x"), P("x", DP)),
        check_vma=False,
    )
```

time: 353 us -> 697 us (1.97)
  Pallas kernels: 46.2 us -> 292 us
  waiting for transfers between devices: 199 us -> 270 us
  local copies, waits for them, and re-layouts: 2.85 us -> 23.7 us
  between operations: 2.31 us -> 18.4 us
  starting transfers between devices: 82.6 us -> 69.7 us
    pallas_call x2 -> x6, Pallas kernels: 40.2 us -> 286 us  [the longest x4 262 us: exchange_images(): pl.pallas_call(functools.partial(pick_kernel, steps=[k for k, _ in group]...]
    unnamed x0 -> x3, waiting for transfers between devices: none -> 158 us
    all_to_all x2 -> x0, waiting for transfers between devices: 55.4 us -> none  [the longest x1 55.4 us: exchange_images(): return lax.all_to_all(outgoing, DP, split_axis=0, concat_axis=0, tiled=True)]
    ppermute x21 -> x47, waiting for transfers between devices: 125 us -> 89.3 us  [the longest x28 68.1 us: exchange_images(): got.append(lax.ppermute(picked[n], ('y', 'c'), pairs))]
    all_to_all x2 -> x0, starting transfers between devices: 29.1 us -> none  [the longest x1 23.5 us: exchange_images(): return lax.all_to_all(outgoing, DP, split_axis=0, concat_axis=0, tiled=True)]
    unnamed x16 -> x67, local copies, waits for them, and re-layouts: 0.14 us -> 18.7 us
    ppermute x21 -> x47, starting transfers between devices: 50.3 us -> 63.8 us  [the longest x28 30.6 us: exchange_images(): got.append(lax.ppermute(picked[n], ('y', 'c'), pairs))]
  transfers between devices with their start and end apart: 26 -> 52, of which waited for: 14 -> 23; matrix products, arithmetic and copies ran while one was open for 3% -> 2% of each run, Pallas kernels for 5% -> 42%
where the time goes in v2:
time: 697 us; the launch traced here: 685 us
  Pallas kernels  292 us (42%)
  waiting for transfers between devices  270 us (39%)
  starting transfers between devices  69.7 us (10%)
  local copies, waits for them, and re-layouts  23.7 us (3%)
  between operations  18.4 us (3%)
  other arithmetic  11.9 us (2%)
    pallas_call x4, Pallas kernels, exchange_images(): pl.pallas_call(functools.partial(pick_kernel, steps=[k for k, _ in group]...  262 us
    unnamed x3, waiting for transfers between devices  158 us
    ppermute x28, waiting for transfers between devices, exchange_images(): got.append(lax.ppermute(picked[n], ('y', 'c'), pairs))  68.1 us
    ppermute x28, starting transfers between devices, exchange_images(): got.append(lax.ppermute(picked[n], ('y', 'c'), pairs))  30.6 us
    ppermute x3, waiting for transfers between devices, on_device(): lax.ppermute(chunks[k].reshape(x_size * rows, part), 'x', shifted(x_size,...  22.1 us
    pallas_call x1, Pallas kernels, on_device(): pl.pallas_call(functools.partial(pair_kernel, starts=starts), out_shape=(...  20.3 us
    unnamed x67, local copies, waits for them, and re-layouts  18.7 us
  transfers between devices with their start and end apart: 52, of which 23 were waited for; matrix products, arithmetic and copies ran while one was open for 2% of the time, Pallas kernels for 42%

profile of v2, /device:TPU:4, one launch (start us, length us, event | category | flops | bytes accessed | tf_op | source)
XLA Modules:
  0.0 685.2 jit_solution(15797207275587311281)
XLA Ops:
  13.3 4.0 collective-permute-start.11
  19.6 33.7 %pick.4 = (bf16[1,64,1024]{2,1,0:T(8,128)(2,1)}, bf16[1,64,1024]{2,1,0:T(8,128)(2,1)}, bf16[1,64,1024]{2,1,0:T(8,128)(2,1)}, bf16[1,64,1024]{2,1,0:T(8,128)(2,1)...) custom-call(s32[8,8]{1,0:T(8,128)} %select_reduce_fusion.3.table, ...), custom_call_target="tpu_custom_call" | custom-call | tf_op jit(solution)/shard_map/pick/pallas_call | solution.py:355
  68.7 3.9 collective-permute-start.9
  72.6 3.2 collective-permute-start.20
  75.8 3.5 copy-done
  79.3 3.3 project.1.refs_0_
  91.2 65.5 %pick.5 = (bf16[2,64,1024]{2,1,0:T(8,128)(2,1)}, bf16[2,64,1024]{2,1,0:T(8,128)(2,1)}, bf16[2,64,1024]{2,1,0:T(8,128)(2,1)}, bf16[2,64,1024]{2,1,0:T(8,128)(2,1)...) custom-call(s32[8,8]{1,0:T(8,128)} %select_reduce_fusion.3.table, ...), custom_call_target="tpu_custom_call" | custom-call | tf_op jit(solution)/shard_map/pick/pallas_call | solution.py:355
  162.1 6.1 collective-permute-done.13.refs_17_
  170.4 13.7 %collective-permute-done.14.refs_18_ = bf16[2,64,1024]{2,1,0:T(8,128)(2,1)S(1)} collective-permute-done((bf16[2,64,1024]{2,1,0:T(8,128)(2,1)}, bf16[2,64,1024]{2,1,0:T(8,128)(2,1)S(1)}, u32[]{:S(2)}, u32[]{:S(2)}) %collective-permute-start.14) | collective-permute-done | bytes 262176 | tf_op jit(solution)/shard_map/ppermute | solution.py:371
  184.1 65.5 %pick.6 = (bf16[2,64,1024]{2,1,0:T(8,128)(2,1)}, bf16[2,64,1024]{2,1,0:T(8,128)(2,1)}, bf16[2,64,1024]{2,1,0:T(8,128)(2,1)}, bf16[2,64,1024]{2,1,0:T(8,128)(2,1)...) custom-call(s32[8,8]{1,0:T(8,128)} %select_reduce_fusion.3.table, ...), custom_call_target="tpu_custom_call" | custom-call | tf_op jit(solution)/shard_map/pick/pallas_call | solution.py:355
  257.4 97.4 %pick.7 = (bf16[3,64,1024]{2,1,0:T(8,128)(2,1)}, bf16[3,64,1024]{2,1,0:T(8,128)(2,1)}, bf16[3,64,1024]{2,1,0:T(8,128)(2,1)}, bf16[3,64,1024]{2,1,0:T(8,128)(2,1)...) custom-call(s32[8,8]{1,0:T(8,128)} %select_reduce_fusion.3.table, ...), custom_call_target="tpu_custom_call" | custom-call | tf_op jit(solution)/shard_map/pick/pallas_call | solution.py:355
  362.1 9.4 %collective-permute-done.25.refs_28_ = bf16[2,64,1024]{2,1,0:T(8,128)(2,1)} collective-permute-done((bf16[2,64,1024]{2,1,0:T(8,128)(2,1)}, bf16[2,64,1024]{2,1,0:T(8,128)(2,1)}, u32[]{:S(2)}, u32[]{:S(2)}) %collective-permute-start.25) | collective-permute-done | bytes 262176 | tf_op jit(solution)/shard_map/ppermute | solution.py:371
  383.6 9.5 %collective-permute-done.35.refs_35_ = bf16[3,64,1024]{2,1,0:T(8,128)(2,1)} collective-permute-done((bf16[3,64,1024]{2,1,0:T(8,128)(2,1)}, bf16[3,64,1024]{2,1,0:T(8,128)(2,1)}, u32[]{:S(2)}, u32[]{:S(2)}) %collective-permute-start.35) | collective-permute-done | bytes 393248 | tf_op jit(solution)/shard_map/ppermute | solution.py:371
  393.1 8.0 %collective-permute-done.36.refs_36_ = bf16[3,64,1024]{2,1,0:T(8,128)(2,1)} collective-permute-done((bf16[3,64,1024]{2,1,0:T(8,128)(2,1)}, bf16[3,64,1024]{2,1,0:T(8,128)(2,1)}, u32[]{:S(2)}, u32[]{:S(2)}) %collective-permute-start.36) | collective-permute-done | bytes 393248 | tf_op jit(solution)/shard_map/ppermute | solution.py:371
  403.2 8.2 %collective-permute-done.38.refs_38_ = bf16[3,64,1024]{2,1,0:T(8,128)(2,1)} collective-permute-done((bf16[3,64,1024]{2,1,0:T(8,128)(2,1)}, bf16[3,64,1024]{2,1,0:T(8,128)(2,1)}, u32[]{:S(2)}, u32[]{:S(2)}) %collective-permute-start.38) | collective-permute-done | bytes 393248 | tf_op jit(solution)/shard_map/ppermute | solution.py:371
  419.6 20.3 %pairs.1 = (bf16[4,4,4,64,256]{4,3,2,1,0:T(8,128)(2,1)}, f32[64,1,64]{2,1,0:T(1,128)S(1)}, f32[4,1,64]{2,1,0:T(1,128)S(1)}) custom-call(s32[4,64]{1,0:T(4,128)S(1)} %get-tuple-element.77.sources, s32[4,64]{1,0:T(4,128)S(1)} %get-tuple-element.76.slots, s32[4]{0:T(128)S(1)} %get-tuple-element.78.counts, s32[4]{0:T(128)S(1)} %copy-done.3, ...), custom_call_target="tpu_custom_call" | custom-call | flops 8589934592 | bytes 20971520 | tf_op jit(solution)/shard_map/pairs/pallas_call | solution.py:248
  447.3 9.0 %collective-permute-done.39.grad_1 = bf16[1024,256]{1,0:T(8,128)(2,1)S(1)} collective-permute-done((bf16[1024,256]{1,0:T(8,128)(2,1)S(1)}, bf16[1024,256]{1,0:T(8,128)(2,1)S(1)}, u32[]{:S(2)}, u32[]{:S(2)}) %collective-permute-start.39) | collective-permute-done | bytes 524320 | tf_op jit(solution)/shard_map/ppermute | solution.py:271
  456.3 12.4 %collective-permute-done.40.grad_2 = bf16[1024,256]{1,0:T(8,128)(2,1)S(1)} collective-permute-done((bf16[1024,256]{1,0:T(8,128)(2,1)S(1)}, bf16[1024,256]{1,0:T(8,128)(2,1)S(1)}, u32[]{:S(2)}, u32[]{:S(2)}) %collective-permute-start.40) | collective-permute-done | bytes 524320 | tf_op jit(solution)/shard_map/ppermute | solution.py:271
  469.5 6.0 head.1
  482.2 11.8 %collective-permute-done.43 = bf16[32,4096]{1,0:T(8,128)(2,1)S(1)} collective-permute-done((bf16[32,4096]{1,0:T(8,128)(2,1)S(1)}, bf16[32,4096]{1,0:T(8,128)(2,1)S(1)}, u32[]{:S(2)}, u32[]{:S(2)}) %collective-permute-start.43) | collective-permute-done | bytes 262176 | tf_op jit(solution)/shard_map/ppermute | solution.py:315
  500.3 4.5 collective-permute-start.47
  505.6 3.7 collective-permute-done.47
  509.5 8.1 %collective-permute-start.48 = (bf16[16,1024]{1,0:T(8,128)(2,1)S(1)}, bf16[16,1024]{1,0:T(8,128)(2,1)S(1)}, u32[]{:S(2)}, u32[]{:S(2)}) collective-permute-start(bf16[16,1024]{1,0:T(8,128)(2,1)S(1)} %bitcast.60), channel_id=1, source_target_pairs={{0,0},{1,64},{2,128},{3,192},{32,32},{33,96},{34,160},{35,224},{64... | collective-permute-start | bytes 98312 | tf_op jit(solution)/shard_map/ppermute | solution.py:335
  517.7 157.6 %all-reduce.3.cloned.1.call-done = f32[256,64]{1,0:T(8,128)} async-done(((f32[256,64]{1,0:T(8,128)}), f32[256,64]{1,0:T(8,128)}) %all-reduce.3.cloned.1.call-update) | async-done | bytes 65552
  (199 shorter events, 98.4 us)
Async XLA Ops:
  8.0 461.5 %all-gather.2.cloned.1.call-start = ((), (), s32[]{:S(2)}) async-start(), calls=%async_computation | async-start | bytes 10485760 | tf_op jit(solution)/shard_map/all_gather | solution.py:190
  8.7 666.6 %all-reduce.3.cloned.1.call-start = ((), (), s32[]{:S(2)}) async-start(), calls=%async_computation.1 | async-start | bytes 262144
  11.3 61.3 %collective-permute-start.10 = (bf16[4,64,1024]{2,1,0:T(8,128)(2,1)S(1)}, bf16[4,64,1024]{2,1,0:T(8,128)(2,1)}, u32[]{:S(2)}, u32[]{:S(2)}) collective-permute-start(bf16[4,64,1024]{2,1,0:T(8,128)(2,1)S(1)} %fusion.1.refs_0_.refs_4_), channel_id=1, source_target_pairs={{0,32},{32,64},{64,96},{96,128},{128,160},{160,192},{192,224},{224... | collective-permute-start | bytes 1572872 | tf_op jit(solution)/shard_map/ppermute | solution.py:345
  13.3 59.3 %collective-permute-start.11 = (bf16[4,64,1024]{2,1,0:T(8,128)(2,1)S(1)}, bf16[4,64,1024]{2,1,0:T(8,128)(2,1)}, u32[]{:S(2)}, u32[]{:S(2)}) collective-permute-start(bf16[4,64,1024]{2,1,0:T(8,128)(2,1)S(1)} %fusion.1.refs_0_.refs_4_), channel_id=1, source_target_pairs={{0,224},{32,0},{64,32},{96,64},{128,96},{160,128},{192,160},{224,1... | collective-permute-start | bytes 1572872 | tf_op jit(solution)/shard_map/ppermute | solution.py:346
  83.3 73.4 %collective-permute-start = (bf16[256,1152]{1,0:T(8,128)(2,1)S(1)}, bf16[256,1152]{1,0:T(8,128)(2,1)S(1)}, u32[]{:S(2)}, u32[]{:S(2)}) collective-permute-start(bf16[256,1152]{1,0:T(8,128)(2,1)S(1)} %project.1.refs_0_), channel_id=1, source_target_pairs={{0,1},{1,2},{2,3},{3,0},{4,5},{5,6},{6,7},{7,4},{8,9},{9,10},{10,1... | collective-permute-start | bytes 1769480 | tf_op jit(solution)/shard_map/ppermute | solution.py:221
  85.2 72.3 %collective-permute-start.1 = (bf16[256,1152]{1,0:T(8,128)(2,1)S(1)}, bf16[256,1152]{1,0:T(8,128)(2,1)S(1)}, u32[]{:S(2)}, u32[]{:S(2)}) collective-permute-start(bf16[256,1152]{1,0:T(8,128)(2,1)S(1)} %project.1.refs_0_), channel_id=1, source_target_pairs={{0,2},{1,3},{2,0},{3,1},{4,6},{5,7},{6,4},{7,5},{8,10},{9,11},{10,... | collective-permute-start | bytes 1769480 | tf_op jit(solution)/shard_map/ppermute | solution.py:221
  86.7 71.0 %collective-permute-start.2 = (bf16[256,1152]{1,0:T(8,128)(2,1)S(1)}, bf16[256,1152]{1,0:T(8,128)(2,1)}, u32[]{:S(2)}, u32[]{:S(2)}) collective-permute-start(bf16[256,1152]{1,0:T(8,128)(2,1)S(1)} %project.1.refs_0_), channel_id=1, source_target_pairs={{0,3},{1,0},{2,1},{3,2},{4,7},{5,4},{6,5},{7,6},{8,11},{9,8},{10,9... | collective-permute-start | bytes 1769480 | tf_op jit(solution)/shard_map/ppermute | solution.py:221
  87.8 80.4 %collective-permute-start.28 = (bf16[4,64,1024]{2,1,0:T(8,128)(2,1)}, bf16[4,64,1024]{2,1,0:T(8,128)(2,1)S(1)}, u32[]{:S(2)}, u32[]{:S(2)}) collective-permute-start(bf16[4,64,1024]{2,1,0:T(8,128)(2,1)} %collective-permute-done.19.refs_0_), channel_id=1, source_target_pairs={{0,32},{32,64},{64,96},{96,128},{128,160},{160,192},{192,224},{224... | collective-permute-start | bytes 1572872 | tf_op jit(solution)/shard_map/ppermute | solution.py:345
  87.9 81.7 %collective-permute-start.29 = (bf16[4,64,1024]{2,1,0:T(8,128)(2,1)}, bf16[4,64,1024]{2,1,0:T(8,128)(2,1)S(1)}, u32[]{:S(2)}, u32[]{:S(2)}) collective-permute-start(bf16[4,64,1024]{2,1,0:T(8,128)(2,1)} %collective-permute-done.20.refs_1_), channel_id=1, source_target_pairs={{0,224},{32,0},{64,32},{96,64},{128,96},{160,128},{192,160},{224,1... | collective-permute-start | bytes 1572872 | tf_op jit(solution)/shard_map/ppermute | solution.py:346
  158.4 25.7 %collective-permute-start.14 = (bf16[2,64,1024]{2,1,0:T(8,128)(2,1)}, bf16[2,64,1024]{2,1,0:T(8,128)(2,1)S(1)}, u32[]{:S(2)}, u32[]{:S(2)}) collective-permute-start(bf16[2,64,1024]{2,1,0:T(8,128)(2,1)} %get-tuple-element.50), channel_id=1, source_target_pairs={{0,12},{4,8},{8,20},{12,16},{16,28},{20,24},{24,4},{28,0},{1,13},{... | collective-permute-start | bytes 786440 | tf_op jit(solution)/shard_map/ppermute | solution.py:371
  159.3 90.4 %collective-permute-start.15 = (bf16[2,64,1024]{2,1,0:T(8,128)(2,1)}, bf16[2,64,1024]{2,1,0:T(8,128)(2,1)S(1)}, u32[]{:S(2)}, u32[]{:S(2)}) collective-permute-start(bf16[2,64,1024]{2,1,0:T(8,128)(2,1)} %get-tuple-element.51), channel_id=1, source_target_pairs={{0,16},{4,20},{8,24},{12,28},{16,0},{20,4},{24,8},{28,12},{1,17},{... | collective-permute-start | bytes 786440 | tf_op jit(solution)/shard_map/ppermute | solution.py:371
  168.2 81.6 %collective-permute-start.16 = (bf16[2,64,1024]{2,1,0:T(8,128)(2,1)}, bf16[2,64,1024]{2,1,0:T(8,128)(2,1)S(1)}, u32[]{:S(2)}, u32[]{:S(2)}) collective-permute-start(bf16[2,64,1024]{2,1,0:T(8,128)(2,1)} %get-tuple-element.52), channel_id=1, source_target_pairs={{0,20},{4,16},{8,28},{12,24},{16,4},{20,0},{24,12},{28,8},{1,21},{... | collective-permute-start | bytes 786440 | tf_op jit(solution)/shard_map/ppermute | solution.py:371
  168.2 82.0 %collective-permute-start.17 = (bf16[2,64,1024]{2,1,0:T(8,128)(2,1)}, bf16[2,64,1024]{2,1,0:T(8,128)(2,1)S(1)}, u32[]{:S(2)}, u32[]{:S(2)}) collective-permute-start(bf16[2,64,1024]{2,1,0:T(8,128)(2,1)} %get-tuple-element.53), channel_id=1, source_target_pairs={{0,24},{4,28},{8,0},{12,4},{16,8},{20,12},{24,16},{28,20},{1,25},{... | collective-permute-start | bytes 786440 | tf_op jit(solution)/shard_map/ppermute | solution.py:371
  169.6 82.3 %collective-permute-start.30 = (bf16[2,64,1024]{2,1,0:T(8,128)(2,1)}, bf16[2,64,1024]{2,1,0:T(8,128)(2,1)}, u32[]{:S(2)}, u32[]{:S(2)}) collective-permute-start(bf16[2,64,1024]{2,1,0:T(8,128)(2,1)} %slice.44), channel_id=1, source_target_pairs={{0,32},{32,64},{64,96},{96,128},{128,160},{160,192},{192,224},{224... | collective-permute-start | bytes 786440 | tf_op jit(solution)/shard_map/ppermute | solution.py:348
  184.1 67.8 %collective-permute-start.31 = (bf16[2,64,1024]{2,1,0:T(8,128)(2,1)}, bf16[2,64,1024]{2,1,0:T(8,128)(2,1)}, u32[]{:S(2)}, u32[]{:S(2)}) collective-permute-start(bf16[2,64,1024]{2,1,0:T(8,128)(2,1)} %slice.45), channel_id=1, source_target_pairs={{0,224},{32,0},{64,32},{96,64},{128,96},{160,128},{192,160},{224,1... | collective-permute-start | bytes 786440 | tf_op jit(solution)/shard_map/ppermute | solution.py:349
  249.7 105.1 %collective-permute-start.18 = (bf16[2,64,1024]{2,1,0:T(8,128)(2,1)}, bf16[2,64,1024]{2,1,0:T(8,128)(2,1)S(1)}, u32[]{:S(2)}, u32[]{:S(2)}) collective-permute-start(bf16[2,64,1024]{2,1,0:T(8,128)(2,1)} %get-tuple-element.54), channel_id=1, source_target_pairs={{0,28},{4,24},{8,4},{12,0},{16,12},{20,8},{24,20},{28,16},{1,29},{... | collective-permute-start | bytes 786440 | tf_op jit(solution)/shard_map/ppermute | solution.py:371
  249.8 105.4 %collective-permute-start.21 = (bf16[2,64,1024]{2,1,0:T(8,128)(2,1)}, bf16[2,64,1024]{2,1,0:T(8,128)(2,1)S(1)}, u32[]{:S(2)}, u32[]{:S(2)}) collective-permute-start(bf16[2,64,1024]{2,1,0:T(8,128)(2,1)} %get-tuple-element.56), channel_id=1, source_target_pairs={{0,4},{4,0},{8,12},{12,8},{16,20},{20,16},{24,28},{28,24},{1,5},{5... | collective-permute-start | bytes 786440 | tf_op jit(solution)/shard_map/ppermute | solution.py:371
  250.2 106.2 %collective-permute-start.22 = (bf16[2,64,1024]{2,1,0:T(8,128)(2,1)}, bf16[2,64,1024]{2,1,0:T(8,128)(2,1)S(1)}, u32[]{:S(2)}, u32[]{:S(2)}) collective-permute-start(bf16[2,64,1024]{2,1,0:T(8,128)(2,1)} %get-tuple-element.57), channel_id=1, source_target_pairs={{0,8},{4,12},{8,16},{12,20},{16,24},{20,28},{24,0},{28,4},{1,9},{5... | collective-permute-start | bytes 786440 | tf_op jit(solution)/shard_map/ppermute | solution.py:371
  251.9 105.0 %collective-permute-start.23 = (bf16[2,64,1024]{2,1,0:T(8,128)(2,1)}, bf16[2,64,1024]{2,1,0:T(8,128)(2,1)}, u32[]{:S(2)}, u32[]{:S(2)}) collective-permute-start(bf16[2,64,1024]{2,1,0:T(8,128)(2,1)} %get-tuple-element.58), channel_id=1, source_target_pairs={{0,12},{4,8},{8,20},{12,16},{16,28},{20,24},{24,4},{28,0},{1,13},{... | collective-permute-start | bytes 786440 | tf_op jit(solution)/shard_map/ppermute | solution.py:371
  251.9 107.3 %collective-permute-start.24 = (bf16[2,64,1024]{2,1,0:T(8,128)(2,1)}, bf16[2,64,1024]{2,1,0:T(8,128)(2,1)}, u32[]{:S(2)}, u32[]{:S(2)}) collective-permute-start(bf16[2,64,1024]{2,1,0:T(8,128)(2,1)} %get-tuple-element.59), channel_id=1, source_target_pairs={{0,16},{4,20},{8,24},{12,28},{16,0},{20,4},{24,8},{28,12},{1,17},{... | collective-permute-start | bytes 786440 | tf_op jit(solution)/shard_map/ppermute | solution.py:371
  380.8 30.6 %collective-permute-start.38 = (bf16[3,64,1024]{2,1,0:T(8,128)(2,1)}, bf16[3,64,1024]{2,1,0:T(8,128)(2,1)}, u32[]{:S(2)}, u32[]{:S(2)}) collective-permute-start(bf16[3,64,1024]{2,1,0:T(8,128)(2,1)} %get-tuple-element.70), channel_id=1, source_target_pairs={{0,28},{4,24},{8,4},{12,0},{16,12},{20,8},{24,20},{28,16},{1,29},{... | collective-permute-start | bytes 1179656 | tf_op jit(solution)/shard_map/ppermute | solution.py:371
  442.7 26.0 %collective-permute-start.40 = (bf16[1024,256]{1,0:T(8,128)(2,1)S(1)}, bf16[1024,256]{1,0:T(8,128)(2,1)S(1)}, u32[]{:S(2)}, u32[]{:S(2)}) collective-permute-start(bf16[1024,256]{1,0:T(8,128)(2,1)S(1)} %bitcast.56), channel_id=1, source_target_pairs={{0,2},{1,3},{2,0},{3,1},{4,6},{5,7},{6,4},{7,5},{8,10},{9,11},{10,... | collective-permute-start | bytes 1572872 | tf_op jit(solution)/shard_map/ppermute | solution.py:271
  509.5 167.1 %collective-permute-start.48 = (bf16[16,1024]{1,0:T(8,128)(2,1)S(1)}, bf16[16,1024]{1,0:T(8,128)(2,1)S(1)}, u32[]{:S(2)}, u32[]{:S(2)}) collective-permute-start(bf16[16,1024]{1,0:T(8,128)(2,1)S(1)} %bitcast.60), channel_id=1, source_target_pairs={{0,0},{1,64},{2,128},{3,192},{32,32},{33,96},{34,160},{35,224},{64... | collective-permute-start | bytes 98312 | tf_op jit(solution)/shard_map/ppermute | solution.py:335
  517.6 159.0 %collective-permute-start.49 = (bf16[16,1024]{1,0:T(8,128)(2,1)S(1)}, bf16[16,1024]{1,0:T(8,128)(2,1)S(1)}, u32[]{:S(2)}, u32[]{:S(2)}) collective-permute-start(bf16[16,1024]{1,0:T(8,128)(2,1)S(1)} %bitcast.61), channel_id=1, source_target_pairs={{0,1},{1,65},{2,129},{3,193},{32,33},{33,97},{34,161},{35,225},{64... | collective-permute-start | bytes 98312 | tf_op jit(solution)/shard_map/ppermute | solution.py:335
  (59 other events, 1663.6 us)
Sparse Core Ops, SparseCore 0:
  10.7 111.4 all-gather.1
Sparse Core Ops, SparseCore 1:
  505.7 169.7 all-reduce.2

commit v3 on v2

--- a/solution.py
+++ b/solution.py
@@ -57,17 +57,26 @@
         out[:, width:] = terms.astype(BF16)
 
 
-def pair_kernel(sources, slots, counts, place, scale_bias, *refs, starts):
+def pair_kernel(sources, slots, counts, place, scale_bias, *refs, starts, own):
     quarters = 4
     texts, refs = refs[:quarters], refs[quarters:]
-    own_images, image_docs, text_docs, *arriving = refs[:-7]
-    chunks, pair_loss, own_loss, text_all, arrived, acc, sems = refs[-7:]
-    blocks, piece_rows, width = own_images.shape
+    if own:
+        own_images, image_docs, text_docs, *refs = refs
+    arriving, refs = refs[: len(starts)], refs[len(starts) :]
+    chunks, pair_loss, refs = refs[0], refs[1], refs[2:]
+    if own:
+        own_loss, *refs = refs
+    text_all, arrived, acc, sems = refs
+    blocks, block_rows, width = text_all.shape
+    width -= EXTRA
+    piece_rows = block_rows // quarters
     part = width // quarters
     scale, bias = scale_bias[0], scale_bias[1]
     copies = []
     for n, (ref, at) in enumerate(zip(arriving, starts)):
-        copies.append(pltpu.make_async_copy(ref, arrived.at[pl.ds(at, ref.shape[0])], sems.at[n]))
+        count = ref.shape[0] // 2
+        half = ref.at[pl.ds(0 if own else count, count)]
+        copies.append(pltpu.make_async_copy(half, arrived.at[pl.ds(at, count)], sems.at[n]))
         copies[-1].start()
     for k in range(quarters):
         to = pl.multiple_of(lax.rem(place[0] - k + quarters, quarters) * piece_rows, piece_rows)
@@ -78,13 +87,16 @@
 
     def each_block(t, carry):
         text = text_all[t, :, :width]
-        images = own_images[t]
-        logits = scale * dot(text, images, (1, 1)) + bias
-        same = text_docs[t] == image_docs[t]
-        sign = jnp.where(same, 1.0, -1.0)
-        loss, weight = loss_and_weight(-sign * logits)
-        own_loss[pl.ds(t, 1)] = jnp.sum(loss, axis=0, keepdims=True)[None]
-        acc[...] = dot((-sign * weight).astype(BF16), images, (1, 0))
+        if own:
+            images = own_images[t]
+            logits = scale * dot(text, images, (1, 1)) + bias
+            same = text_docs[t] == image_docs[t]
+            sign = jnp.where(same, 1.0, -1.0)
+            loss, weight = loss_and_weight(-sign * logits)
+            own_loss[pl.ds(t, 1)] = jnp.sum(loss, axis=0, keepdims=True)[None]
+            acc[...] = dot((-sign * weight).astype(BF16), images, (1, 0))
+        else:
+            acc[...] = jnp.zeros_like(acc)
         count = counts[t]
 
         def each_group(g, inner):
@@ -122,22 +134,23 @@
     lax.fori_loop(0, blocks, each_block, 0)
 
 
-def pick_kernel(table, place, *refs, steps, sizes):
+def pick_kernel(table, place, *refs, step, sizes):
     z_size, y_size, c_size = sizes
-    count = len(steps)
-    from_refs, to_refs, sems = refs[:count], refs[count:-1], refs[-1]
+    to_refs, sems = refs[-1 - y_size : -1], refs[-1]
+    from_ref = refs[0]
+    count = from_ref.shape[0]
+    back = jnp.where(place[2] == 0, step, z_size - step)
+    z = lax.rem(place[3] - back + z_size, z_size)
     copies = []
     for dy in range(y_size):
-        for dc in range(c_size):
-            y = lax.rem(place[1] + dy, y_size)
-            c = lax.rem(place[2] + dc, c_size)
-            for j, step in enumerate(steps):
-                z = lax.rem(place[3] - step + z_size, z_size)
-                block = table[z, y * c_size + c]
-                n = dy * c_size + dc
-                copies.append(
-                    pltpu.make_async_copy(from_refs[j].at[block], to_refs[n].at[j], sems.at[n * count + j])
-                )
+        y = lax.rem(place[1] + dy, y_size)
+        for to in range(c_size):
+            for j in range(count):
+                source = z * c_size + lax.rem(place[2] + j, c_size)
+                block = table[source, y * c_size + lax.rem(place[2] + to, c_size)]
+                n = to * count + j
+                sem = sems.at[dy * c_size * count + n]
+                copies.append(pltpu.make_async_copy(from_ref.at[j, block], to_refs[dy].at[n], sem))
     for copy in copies:
         copy.start()
     for copy in copies:
@@ -190,8 +203,8 @@
     feats = lax.all_gather(features, "x", axis=0, tiled=False)
 
     owners = jnp.where(hard_lists >= 0, hard_lists // blocks, -1).reshape(dp_count, blocks, -1)
-    line = owners.reshape(z_size, y_size * c_size, blocks, -1)
-    line = lax.dynamic_index_in_dim(line, y * c_size + c, 1, keepdims=False)
+    line = owners.reshape(z_size, y_size, c_size, blocks, -1)
+    line = lax.dynamic_index_in_dim(line, y, 1, keepdims=False).reshape(z_size * c_size, blocks, -1)
     plane = z * y_size * c_size + jnp.arange(y_size * c_size, dtype=jnp.int32)
     wanted = jnp.any(line[:, None] == plane[:, None, None], axis=3)
     table = jnp.sum(wanted.astype(jnp.int32) * block_iota, axis=2)
@@ -217,59 +230,70 @@
         ),
         name="project",
     )(features, head_weight)
-    texts = [text_emb] + [
-        lax.ppermute(text_emb, "x", shifted(x_size, k)) for k in range(1, x_size)
-    ]
-
-    hit = owners == dp_index
-    listed = jnp.any(hit, axis=(1, 2))
-    which = jnp.sum(hit * (hard_lists % blocks).reshape(owners.shape), axis=(1, 2))
-    mine = listed[None] & (which[None] == block_iota[:, None])
-    before = peer_iota[None] < peer_iota[:, None]
-    order = jnp.sum((mine[:, None] & before).astype(jnp.int32), axis=2)
-    counts = jnp.sum(mine.astype(jnp.int32), axis=1)
-    at = mine[:, None] & (order[:, None] == peer_iota[:, None])
-    sources = jnp.sum(jnp.where(at, peer_iota, 0), axis=2)
-    back = (z - peer_iota // (y_size * c_size)) % z_size
-    turn = jnp.where(2 * back <= z_size, jnp.maximum(2 * back - 1, 0), 2 * (z_size - back))
-    over_y = (y - peer_iota // c_size) % y_size
-    over_c = (c - peer_iota) % c_size
-    slots = jnp.sum(jnp.where(at, (over_y * c_size + over_c) * z_size + turn, 0), axis=2)
-
-    text_docs = doc_ids.reshape(blocks, block_rows, 1)
-    image_docs = lax.dynamic_slice_in_dim(doc_ids, x * piece_rows, piece_rows, 1)[:, None]
-    scale_bias = jnp.stack([logit_scale, logit_bias])
+    texts = [text_emb]
+    for _ in range(1, x_size):
+        texts.append(lax.ppermute(texts[-1], "x", shifted(x_size, 1)))
+
     arriving, starts, turns = [], [], 0
     for group in groups:
         arriving += group
         starts += [n * z_size + turns for n in range(len(group))]
-        turns += group[0].shape[0]
-
-    chunks, pair_loss, own_loss = pl.pallas_call(
-        functools.partial(pair_kernel, starts=starts),
-        out_shape=(
-            jax.ShapeDtypeStruct((x_size, x_size, blocks, piece_rows, part), BF16),
-            jax.ShapeDtypeStruct((dp_count, 1, piece_rows), F32),
-            jax.ShapeDtypeStruct((blocks, 1, piece_rows), F32),
-        ),
-        in_specs=[whole(pltpu.SMEM)] * 5 + [whole()] * 7 + [whole(pl.ANY)] * len(arriving),
-        out_specs=(whole(), whole(), whole()),
-        scratch_shapes=[
-            pltpu.VMEM((blocks, block_rows, emb_width + EXTRA), BF16),
-            pltpu.VMEM((dp_count, piece_rows, emb_width), BF16),
-            pltpu.VMEM((block_rows, emb_width), F32),
-            pltpu.SemaphoreType.DMA((len(arriving),)),
-        ],
-        compiler_params=pltpu.CompilerParams(vmem_limit_bytes=48 << 20),
-        cost_estimate=pl.CostEstimate(flops=8 << 30, bytes_accessed=20 << 20, transcendentals=4 << 20),
-        name="pairs",
-    )(sources, slots, counts, place, scale_bias, *texts, own_images, image_docs, text_docs, *arriving)
-
-    grads = [chunks[0].reshape(x_size * rows, part)]
-    for k in range(1, x_size):
-        grads.append(
-            lax.ppermute(chunks[k].reshape(x_size * rows, part), "x", shifted(x_size, k))
-        )
+        turns += group[0].shape[0] // c_size
+    away = jnp.where(c == 0, z - peer_iota // (y_size * c_size), peer_iota // (y_size * c_size) - z) % z_size
+    over_y = (y - peer_iota // c_size) % y_size
+    over_c = (c - peer_iota) % c_size
+    ends = (away == 0) | (away == z_size // 2)
+    have = jnp.where(ends, over_c == 0, away < z_size // 2)
+    turn = jnp.where(ends, away * 2 - (away > 0), 2 * away - 1 + over_c)
+    slot_of = over_y * z_size + turn
+
+    text_docs = doc_ids.reshape(blocks, block_rows, 1)
+    image_docs = lax.dynamic_slice_in_dim(doc_ids, x * piece_rows, piece_rows, 1)[:, None]
+    scale_bias = jnp.stack([logit_scale, logit_bias])
+
+    def pairs(holder, pieces, own):
+        hit = owners == holder
+        which = jnp.sum(hit * (hard_lists % blocks).reshape(owners.shape), axis=(1, 2))
+        mine = (jnp.any(hit, axis=(1, 2)) & have)[None] & (which[None] == block_iota[:, None])
+        before = peer_iota[None] < peer_iota[:, None]
+        order = jnp.sum((mine[:, None] & before).astype(jnp.int32), axis=2)
+        counts = jnp.sum(mine.astype(jnp.int32), axis=1)
+        at = mine[:, None] & (order[:, None] == peer_iota[:, None])
+        sources = jnp.sum(jnp.where(at, peer_iota, 0), axis=2)
+        slots = jnp.sum(jnp.where(at, slot_of, 0), axis=2)
+        extra = [own_images, image_docs, text_docs] if own else []
+        losses = [jax.ShapeDtypeStruct((blocks, 1, piece_rows), F32)] if own else []
+        return pl.pallas_call(
+            functools.partial(pair_kernel, starts=starts, own=own),
+            out_shape=[
+                jax.ShapeDtypeStruct((x_size, x_size, blocks, piece_rows, part), BF16),
+                jax.ShapeDtypeStruct((dp_count, 1, piece_rows), F32),
+            ]
+            + losses,
+            in_specs=[whole(pltpu.SMEM)] * 5
+            + [whole()] * (x_size + len(extra))
+            + [whole(pl.ANY)] * len(arriving),
+            out_specs=[whole()] * (2 + len(losses)),
+            scratch_shapes=[
+                pltpu.VMEM((blocks, block_rows, emb_width + EXTRA), BF16),
+                pltpu.VMEM((y_size * z_size, piece_rows, emb_width), BF16),
+                pltpu.VMEM((block_rows, emb_width), F32),
+                pltpu.SemaphoreType.DMA((len(arriving),)),
+            ],
+            compiler_params=pltpu.CompilerParams(vmem_limit_bytes=56 << 20),
+            cost_estimate=pl.CostEstimate(flops=4 << 30, bytes_accessed=10 << 20, transcendentals=2 << 20),
+            name="pairs",
+        )(sources, slots, counts, place, scale_bias, *pieces, *extra, *arriving)
+
+    other_texts = [lax.ppermute(piece, "c", shifted(c_size, 1)) for piece in texts]
+    other_chunks, other_loss = pairs(dp_index + 1 - 2 * c, other_texts, False)
+    chunks, pair_loss, own_loss = pairs(dp_index, texts, True)
+
+    taken = lax.ppermute(other_chunks, "c", shifted(c_size, 1))
+    grads = []
+    for k in range(x_size):
+        total = (chunks[k].astype(F32) + taken[k].astype(F32)).astype(BF16).reshape(x_size * rows, part)
+        grads.append(lax.ppermute(total, "x", shifted(x_size, k)) if k else total)
     z_part = z_size // x_size
     half = part // c_size
     keep, give = pl.pallas_call(
@@ -294,9 +318,14 @@
         name="head",
     )(place, *grads, feats.reshape(x_size * rows, feat_width))
 
-    asker = jnp.sum(jnp.any(hit, axis=2).astype(jnp.int32) * block_iota, axis=1)
-    spread = jnp.where(asker[:, None, None] == block_iota[:, None], pair_loss, 0.0)
-    remote_loss = lax.psum_scatter(spread.reshape(dp_count * blocks, piece_rows), DP, tiled=True)
+    returned = lax.all_to_all(
+        jnp.concatenate([pair_loss, other_loss], axis=1), DP, split_axis=0, concat_axis=0, tiled=True
+    )
+    swapped = returned.reshape(-1, c_size, 2, piece_rows)[:, ::-1, 1].reshape(dp_count, piece_rows)
+    returned = returned[:, 0] + swapped
+    my_owners = lax.dynamic_index_in_dim(owners, dp_index, 0, keepdims=False)
+    asked = jnp.any(my_owners[None] == peer_iota[:, None, None], axis=2)
+    remote_loss = jnp.sum(jnp.where(asked[..., None], returned[:, None], 0.0), axis=0)
     row_loss = (own_loss.reshape(blocks, piece_rows) + remote_loss) / block_rows
     return (row_loss, add_over_dp(keep, give, (z_size, y_size, c_size, x_size), z, strip))
 
@@ -338,38 +367,30 @@
 
 def exchange_images(own_images, table, place, sizes):
     z_size, y_size, c_size = sizes
-    blocks = own_images.shape[0]
-    up = down = own_images
-    steps = [[(0, own_images)]]
-    for k in range(1, z_size // 2):
-        up = lax.ppermute(up, "z", shifted(z_size, 1))
-        down = lax.ppermute(down, "z", shifted(z_size, -1))
-        steps.append([(k, up), (-k, down)])
-    up = lax.ppermute(up[: blocks // 2], "z", shifted(z_size, 1))
-    down = lax.ppermute(down[blocks // 2 :], "z", shifted(z_size, -1))
-    steps[-1].append((z_size // 2, jnp.concatenate([up, down], axis=0)))
+    onward = []
+    for z in range(z_size):
+        onward.append((z * c_size, (z + 1) % z_size * c_size))
+        onward.append((z * c_size + 1, (z - 1) % z_size * c_size + 1))
+    moving = jnp.stack([own_images, lax.ppermute(own_images, "c", shifted(c_size, 1))])
     groups = []
-    for group in steps:
-        count = len(group)
-        shape = (count,) + own_images.shape[1:]
+    for step in range(z_size // 2 + 1):
+        if step == 0:
+            here = own_images[None]
+        else:
+            moving = moving[:1] if step == z_size // 2 else moving
+            here = moving = lax.ppermute(moving, ("z", "c"), onward)
+        shape = (c_size * here.shape[0],) + own_images.shape[1:]
         picked = pl.pallas_call(
-            functools.partial(pick_kernel, steps=[k for k, _ in group], sizes=sizes),
-            out_shape=[jax.ShapeDtypeStruct(shape, BF16)] * (y_size * c_size),
-            in_specs=[whole(pltpu.SMEM)] * 2 + [whole(pl.ANY)] * count,
-            out_specs=[whole(pl.ANY)] * (y_size * c_size),
-            scratch_shapes=[pltpu.SemaphoreType.DMA((y_size * c_size * count,))],
+            functools.partial(pick_kernel, step=step, sizes=sizes),
+            out_shape=[jax.ShapeDtypeStruct(shape, BF16)] * y_size,
+            in_specs=[whole(pltpu.SMEM)] * 2 + [whole()],
+            out_specs=[whole(pl.ANY)] * y_size,
+            scratch_shapes=[pltpu.SemaphoreType.DMA((y_size * shape[0],))],
             name="pick",
-        )(table, place, *(v for _, v in group))
-        got = [picked[0]]
-        for n in range(1, y_size * c_size):
-            dy, dc = n // c_size, n % c_size
-            pairs = [
-                (y * c_size + c, (y + dy) % y_size * c_size + (c + dc) % c_size)
-                for y in range(y_size)
-                for c in range(c_size)
-            ]
-            got.append(lax.ppermute(picked[n], ("y", "c"), pairs))
-        groups.append(got)
+        )(table, place, here)
+        groups.append(
+            [picked[0]] + [lax.ppermute(picked[n], "y", shifted(y_size, n)) for n in range(1, y_size)]
+        )
     return groups
 
 

time: 697 us -> 345 us (0.49); the launches traced: 685 us -> 340 us
  Pallas kernels: 292 us -> 50.9 us
  waiting for transfers between devices: 270 us -> 174 us
  local copies, waits for them, and re-layouts: 23.7 us -> 8.36 us
    pallas_call x5 -> x7, Pallas kernels: 282 us -> 40.8 us  [the longest x2 28.2 us: pairs(): pl.pallas_call(functools.partial(pair_kernel, starts=starts, own=own), ou...]
    unnamed x3 -> x1, waiting for transfers between devices: 158 us -> 0.68 us
    ppermute x42 -> x31, waiting for transfers between devices: 90.3 us -> 148 us  [the longest x15 59.2 us: exchange_images(): lax.ppermute(picked[n], 'y', shifted(y_size, n))]
    unnamed x67 -> x52, local copies, waits for them, and re-layouts: 18.7 us -> 5.16 us
    ppermute x3, waiting for transfers between devices: 12.4 us -> 0.01 us  [add_over_dp(): lax.ppermute(total[k], 'y', shifted(y_size, k))]
    all_to_all x0 -> x1, waiting for transfers between devices: none -> 9.38 us  [on_device(): lax.all_to_all(jnp.concatenate([pair_loss, other_loss], axis=1), DP, spli...]
    all_to_all x0 -> x1, starting transfers between devices: none -> 8.26 us  [on_device(): lax.all_to_all(jnp.concatenate([pair_loss, other_loss], axis=1), DP, spli...]
    ppermute x42 -> x31, starting transfers between devices: 52.1 us -> 48.4 us  [the longest x15 25.6 us: exchange_images(): lax.ppermute(picked[n], 'y', shifted(y_size, n))]
  transfers between devices with their start and end apart: 52 -> 41, of which waited for: 23 -> 22; matrix products, arithmetic and copies ran while one was open for 2% -> 5% of each run, Pallas kernels for 42% -> 13%
where the time goes in v3:
time: 345 us; the launch traced here: 340 us
  waiting for transfers between devices  174 us (50%)
  starting transfers between devices  73.4 us (21%)
  Pallas kernels  50.9 us (15%)
  other arithmetic  17.2 us (5%)
  between operations  16.2 us (5%)
  local copies, waits for them, and re-layouts  8.36 us (2%)
    ppermute x15, waiting for transfers between devices, exchange_images(): lax.ppermute(picked[n], 'y', shifted(y_size, n))  59.2 us
    ppermute x3, waiting for transfers between devices, on_device(): texts.append(lax.ppermute(texts[-1], 'x', shifted(x_size, 1)))  49.2 us
    pallas_call x2, Pallas kernels, pairs(): pl.pallas_call(functools.partial(pair_kernel, starts=starts, own=own), ou...  28.2 us
    ppermute x15, starting transfers between devices, exchange_images(): lax.ppermute(picked[n], 'y', shifted(y_size, n))  25.6 us
    ppermute x3, waiting for transfers between devices, on_device(): grads.append(lax.ppermute(total, 'x', shifted(x_size, k)) if k else total)  22.1 us
    ppermute x4, waiting for transfers between devices, exchange_images(): here = moving = lax.ppermute(moving, ('z', 'c'), onward)  16.8 us
    pallas_call x5, Pallas kernels, exchange_images(): pl.pallas_call(functools.partial(pick_kernel, step=step, sizes=sizes), ou...  12.6 us
    ppermute x2, starting transfers between devices, add_over_dp(): final = final + lax.ppermute(chunk, ('z', 'x'), pairs).astype(F32)  11.8 us
  transfers between devices with their start and end apart: 41, of which 22 were waited for; matrix products, arithmetic and copies ran while one was open for 5% of the time, Pallas kernels for 13%

profile of v3, /device:TPU:4, one launch (start us, length us, event | category | flops | bytes accessed | tf_op | source)
XLA Modules:
  0.0 340.1 jit_solution(3477712158660252985)
XLA Ops:
  14.6 16.8 %collective-permute-done.7.refs_0_ = bf16[2,4,64,1024]{3,2,1,0:T(8,128)(2,1)} collective-permute-done((bf16[2,4,64,1024]{3,2,1,0:T(8,128)(2,1)S(1)}, bf16[2,4,64,1024]{3,2,1,0:T(8,128)(2,1)}, u32[]{:S(2)}, u32[]{:S(2)}) %collective-permute-start.7) | collective-permute-done | bytes 1048608 | tf_op jit(solution)/shard_map/ppermute | solution.py:381
  31.5 3.4 copy-done
  39.8 27.0 %collective-permute-done.refs_1_ = bf16[256,1152]{1,0:T(8,128)(2,1)S(1)} collective-permute-done((bf16[256,1152]{1,0:T(8,128)(2,1)S(1)}, bf16[256,1152]{1,0:T(8,128)(2,1)S(1)}, u32[]{:S(2)}, u32[]{:S(2)}) %collective-permute-start) | collective-permute-done | bytes 589856 | tf_op jit(solution)/shard_map/ppermute | solution.py:235
  77.8 5.8 %collective-permute-done.3.refs_8_.refs_5_ = bf16[2,64,1024]{2,1,0:T(8,128)(2,1)S(1)} collective-permute-done((bf16[2,64,1024]{2,1,0:T(8,128)(2,1)}, bf16[2,64,1024]{2,1,0:T(8,128)(2,1)S(1)}, u32[]{:S(2)}, u32[]{:S(2)}) %collective-permute-start.3) | collective-permute-done | bytes 262176 | tf_op jit(solution)/shard_map/ppermute | solution.py:392
  83.6 12.0 %collective-permute-done.1.refs_2_ = bf16[256,1152]{1,0:T(8,128)(2,1)} collective-permute-done((bf16[256,1152]{1,0:T(8,128)(2,1)S(1)}, bf16[256,1152]{1,0:T(8,128)(2,1)}, u32[]{:S(2)}, u32[]{:S(2)}) %collective-permute-start.1) | collective-permute-done | bytes 589856 | tf_op jit(solution)/shard_map/ppermute | solution.py:235
  99.6 6.5 %collective-permute-done.5.refs_10_.refs_7_ = bf16[2,64,1024]{2,1,0:T(8,128)(2,1)S(1)} collective-permute-done((bf16[2,64,1024]{2,1,0:T(8,128)(2,1)}, bf16[2,64,1024]{2,1,0:T(8,128)(2,1)S(1)}, u32[]{:S(2)}, u32[]{:S(2)}) %collective-permute-start.5) | collective-permute-done | bytes 262176 | tf_op jit(solution)/shard_map/ppermute | solution.py:392
  110.2 4.1 %collective-permute-start.9 = (bf16[4,64,1024]{2,1,0:T(8,128)(2,1)}, bf16[4,64,1024]{2,1,0:T(8,128)(2,1)}, u32[]{:S(2)}, u32[]{:S(2)}) collective-permute-start(bf16[4,64,1024]{2,1,0:T(8,128)(2,1)} %get-tuple-element.35), channel_id=1, source_target_pairs={{0,16},{8,24},{16,0},{24,8},{1,17},{9,25},{17,1},{25,9},{2,18},{10... | collective-permute-start | bytes 1572872 | tf_op jit(solution)/shard_map/ppermute | solution.py:392
  114.3 10.2 %collective-permute-done.2.refs_3_ = bf16[256,1152]{1,0:T(8,128)(2,1)} collective-permute-done((bf16[256,1152]{1,0:T(8,128)(2,1)}, bf16[256,1152]{1,0:T(8,128)(2,1)}, u32[]{:S(2)}, u32[]{:S(2)}) %collective-permute-start.2) | collective-permute-done | bytes 589856 | tf_op jit(solution)/shard_map/ppermute | solution.py:235
  143.3 17.1 %collective-permute-done.12.refs_16_.refs_13_ = bf16[4,64,1024]{2,1,0:T(8,128)(2,1)S(1)} collective-permute-done((bf16[4,64,1024]{2,1,0:T(8,128)(2,1)}, bf16[4,64,1024]{2,1,0:T(8,128)(2,1)S(1)}, u32[]{:S(2)}, u32[]{:S(2)}) %collective-permute-start.12) | collective-permute-done | bytes 524320 | tf_op jit(solution)/shard_map/ppermute | solution.py:392
  165.4 3.4 %collective-permute-start.21 = (bf16[2,64,1024]{2,1,0:T(8,128)(2,1)}, bf16[2,64,1024]{2,1,0:T(8,128)(2,1)S(1)}, u32[]{:S(2)}, u32[]{:S(2)}) collective-permute-start(bf16[2,64,1024]{2,1,0:T(8,128)(2,1)} %get-tuple-element.47), channel_id=1, source_target_pairs={{0,16},{8,24},{16,0},{24,8},{1,17},{9,25},{17,1},{25,9},{2,18},{10... | collective-permute-start | bytes 786440 | tf_op jit(solution)/shard_map/ppermute | solution.py:392
  168.8 14.1 %collective-permute-done.16.refs_20_.refs_17_ = bf16[4,64,1024]{2,1,0:T(8,128)(2,1)} collective-permute-done((bf16[4,64,1024]{2,1,0:T(8,128)(2,1)}, bf16[4,64,1024]{2,1,0:T(8,128)(2,1)}, u32[]{:S(2)}, u32[]{:S(2)}) %collective-permute-start.16) | collective-permute-done | bytes 524320 | tf_op jit(solution)/shard_map/ppermute | solution.py:392
  188.9 5.3 %collective-permute-done.21.refs_25_.refs_22_ = bf16[2,64,1024]{2,1,0:T(8,128)(2,1)S(1)} collective-permute-done((bf16[2,64,1024]{2,1,0:T(8,128)(2,1)}, bf16[2,64,1024]{2,1,0:T(8,128)(2,1)S(1)}, u32[]{:S(2)}, u32[]{:S(2)}) %collective-permute-start.21) | collective-permute-done | bytes 262176 | tf_op jit(solution)/shard_map/ppermute | solution.py:392
  194.2 3.8 %collective-permute-done.22.refs_26_.refs_23_ = bf16[2,64,1024]{2,1,0:T(8,128)(2,1)S(1)} collective-permute-done((bf16[2,64,1024]{2,1,0:T(8,128)(2,1)}, bf16[2,64,1024]{2,1,0:T(8,128)(2,1)S(1)}, u32[]{:S(2)}, u32[]{:S(2)}) %collective-permute-start.22) | collective-permute-done | bytes 262176 | tf_op jit(solution)/shard_map/ppermute | solution.py:392
  198.7 13.6 %pairs.3 = (bf16[4,4,4,64,256]{4,3,2,1,0:T(8,128)(2,1)}, f32[64,1,64]{2,1,0:T(1,128)}) custom-call(s32[4,64]{1,0:T(4,128)} %get-tuple-element.61.sources, s32[4,64]{1,0:T(4,128)} %get-tuple-element.60.slots, s32[4]{0:T(128)} %get-tuple-element.66.counts, s32[4]{0:T(128)} %pad_add_fusion.place, f32[2]{0:T(128)} %pad_maximum_fusion.2.scale_bias, ...), custom_call_target="tpu_custom_call" | custom-call | flops 4294967296 | bytes 10485760 | tf_op jit(solution)/shard_map/pairs/pallas_call | solution.py:266
  212.3 9.8 %collective-permute-start.27 = (bf16[4,4,4,64,256]{4,3,2,1,0:T(8,128)(2,1)}, bf16[4,4,4,64,256]{4,3,2,1,0:T(8,128)(2,1)S(1)}, u32[]{:S(2)}, u32[]{:S(2)}) collective-permute-start(bf16[4,4,4,64,256]{4,3,2,1,0:T(8,128)(2,1)} %get-tuple-element.53), channel_id=1, source_target_pairs={{0,4},{4,0},{1,5},{5,1},{2,6},{6,2},{3,7},{7,3},{8,12},{12,8},{9,1... | collective-permute-start | bytes 6291464 | tf_op jit(solution)/shard_map/ppermute | solution.py:292
  223.8 14.6 %pairs.2 = (bf16[4,4,4,64,256]{4,3,2,1,0:T(8,128)(2,1)}, f32[64,1,64]{2,1,0:T(1,128)}, f32[4,1,64]{2,1,0:T(1,128)}) custom-call(s32[4,64]{1,0:T(4,128)} %get-tuple-element.64.sources, s32[4,64]{1,0:T(4,128)} %get-tuple-element.65.slots, s32[4]{0:T(128)} %get-tuple-element.68.counts, s32[4]{0:T(128)} %pad_add_fusion.place, f32[2]{0:T(128)} %pad_maximum_fusion.2.scale_bias, ...), custom_call_target="tpu_custom_call" | custom-call | flops 4294967296 | bytes 10485760 | tf_op jit(solution)/shard_map/pairs/pallas_call | solution.py:266
  247.3 7.7 %collective-permute-done.28.grad_1 = bf16[1024,256]{1,0:T(8,128)(2,1)S(1)} collective-permute-done((bf16[1024,256]{1,0:T(8,128)(2,1)S(1)}, bf16[1024,256]{1,0:T(8,128)(2,1)S(1)}, u32[]{:S(2)}, u32[]{:S(2)}) %collective-permute-start.28) | collective-permute-done | bytes 524320 | tf_op jit(solution)/shard_map/ppermute | solution.py:296
  255.1 12.8 %collective-permute-done.29.grad_2 = bf16[1024,256]{1,0:T(8,128)(2,1)S(1)} collective-permute-done((bf16[1024,256]{1,0:T(8,128)(2,1)S(1)}, bf16[1024,256]{1,0:T(8,128)(2,1)S(1)}, u32[]{:S(2)}, u32[]{:S(2)}) %collective-permute-start.29) | collective-permute-done | bytes 524320 | tf_op jit(solution)/shard_map/ppermute | solution.py:296
  269.4 6.7 %head.1 = (bf16[128,4096]{1,0:T(8,128)(2,1)S(1)}, bf16[128,4096]{1,0:T(8,128)(2,1)}) custom-call(s32[4]{0:T(128)S(1)} %copy-done.3, bf16[1024,256]{1,0:T(8,128)(2,1)S(1)} %bitcast.53, bf16[1024,256]{1,0:T(8,128)(2,1)S(1)} %collective-permute-done.28.grad_1, bf16[1024,256]{1,0:T(8,128)(2,1)S(1)} %collective-permute-done.29.grad_2, ...), custom_call_target="tpu_custom_call" | custom-call | flops 2147483648 | bytes 16777216 | tf_op jit(solution)/shard_map/head/pallas_call | solution.py:299
  285.0 8.3 %all-to-all-start = ((f32[64,1,128]{2,1,0:T(1,128)}), f32[64,1,128]{2,1,0:T(1,128)S(1)}, u32[]{:S(2)}, u32[]{:S(2)}) async-start(f32[64,1,128]{2,1,0:T(1,128)} %reshape.229), calls=%async_computation | async-start | bytes 65536 | tf_op jit(solution)/shard_map/all_to_all | solution.py:321
  293.4 9.4 %all-to-all-done = f32[64,1,128]{2,1,0:T(1,128)S(1)} async-done(((f32[64,1,128]{2,1,0:T(1,128)}), f32[64,1,128]{2,1,0:T(1,128)S(1)}, u32[]{:S(2)}, u32[]{:S(2)}) %all-to-all-start) | async-done | bytes 32800 | tf_op jit(solution)/shard_map/all_to_all | solution.py:321
  305.1 4.6 %collective-permute-done.35 = bf16[16,4096]{1,0:T(8,128)(2,1)S(1)} collective-permute-done((bf16[16,4096]{1,0:T(8,128)(2,1)S(1)}, bf16[16,4096]{1,0:T(8,128)(2,1)S(1)}, u32[]{:S(2)}, u32[]{:S(2)}) %collective-permute-start.35) | collective-permute-done | bytes 131104 | tf_op jit(solution)/shard_map/ppermute | solution.py:349
  310.9 7.6 %collective-permute-done.36 = bf16[16,2048]{1,0:T(8,128)(2,1)S(1)} collective-permute-done((bf16[16,2048]{1,0:T(8,128)(2,1)S(1)}, bf16[16,2048]{1,0:T(8,128)(2,1)S(1)}, u32[]{:S(2)}, u32[]{:S(2)}) %collective-permute-start.36) | collective-permute-done | bytes 65568 | tf_op jit(solution)/shard_map/ppermute | solution.py:353
  320.3 10.3 %collective-permute-start.37 = (bf16[16,1024]{1,0:T(8,128)(2,1)S(1)}, bf16[16,1024]{1,0:T(8,128)(2,1)S(1)}, u32[]{:S(2)}, u32[]{:S(2)}) collective-permute-start(bf16[16,1024]{1,0:T(8,128)(2,1)S(1)} %bitcast.68), channel_id=1, source_target_pairs={{0,0},{1,64},{2,128},{3,192},{32,32},{33,96},{34,160},{35,224},{64... | collective-permute-start | bytes 98312 | tf_op jit(solution)/shard_map/ppermute | solution.py:364
  (175 shorter events, 89.2 us)
Async XLA Ops:
  7.2 262.3 %all-gather.2.cloned.1.call-start = ((), (), s32[]{:S(2)}) async-start(), calls=%async_computation.1 | async-start | bytes 10485760 | tf_op jit(solution)/shard_map/all_gather | solution.py:203
  31.4 37.6 %collective-permute-start.11 = (bf16[2,4,64,1024]{3,2,1,0:T(8,128)(2,1)}, bf16[2,4,64,1024]{3,2,1,0:T(8,128)(2,1)}, u32[]{:S(2)}, u32[]{:S(2)}) collective-permute-start(bf16[2,4,64,1024]{3,2,1,0:T(8,128)(2,1)} %collective-permute-done.7.refs_0_), channel_id=1, source_target_pairs={{0,32},{4,228},{32,64},{36,4},{64,96},{68,36},{96,128},{100,68},{1... | collective-permute-start | bytes 3145736 | tf_op jit(solution)/shard_map/ppermute | solution.py:381
  38.2 28.6 %collective-permute-start = (bf16[256,1152]{1,0:T(8,128)(2,1)S(1)}, bf16[256,1152]{1,0:T(8,128)(2,1)S(1)}, u32[]{:S(2)}, u32[]{:S(2)}) collective-permute-start(bf16[256,1152]{1,0:T(8,128)(2,1)S(1)} %project.1.refs_0_), channel_id=1, source_target_pairs={{0,1},{1,2},{2,3},{3,0},{4,5},{5,6},{6,7},{7,4},{8,9},{9,10},{10,1... | collective-permute-start | bytes 1769480 | tf_op jit(solution)/shard_map/ppermute | solution.py:235
  66.7 28.8 %collective-permute-start.1 = (bf16[256,1152]{1,0:T(8,128)(2,1)S(1)}, bf16[256,1152]{1,0:T(8,128)(2,1)}, u32[]{:S(2)}, u32[]{:S(2)}) collective-permute-start(bf16[256,1152]{1,0:T(8,128)(2,1)S(1)} %collective-permute-done.refs_1_), channel_id=1, source_target_pairs={{0,1},{1,2},{2,3},{3,0},{4,5},{5,6},{6,7},{7,4},{8,9},{9,10},{10,1... | collective-permute-start | bytes 1769480 | tf_op jit(solution)/shard_map/ppermute | solution.py:235
  69.1 58.4 %collective-permute-start.15 = (bf16[2,4,64,1024]{3,2,1,0:T(8,128)(2,1)}, bf16[2,4,64,1024]{3,2,1,0:T(8,128)(2,1)S(1)}, u32[]{:S(2)}, u32[]{:S(2)}) collective-permute-start(bf16[2,4,64,1024]{3,2,1,0:T(8,128)(2,1)} %collective-permute-done.11.refs_0_), channel_id=1, source_target_pairs={{0,32},{4,228},{32,64},{36,4},{64,96},{68,36},{96,128},{100,68},{1... | collective-permute-start | bytes 3145736 | tf_op jit(solution)/shard_map/ppermute | solution.py:381
  77.5 31.4 %collective-permute-start.23 = (bf16[256,1152]{1,0:T(8,128)(2,1)S(1)}, bf16[256,1152]{1,0:T(8,128)(2,1)}, u32[]{:S(2)}, u32[]{:S(2)}) collective-permute-start(bf16[256,1152]{1,0:T(8,128)(2,1)S(1)} %project.1.refs_0_), channel_id=1, source_target_pairs={{0,4},{4,0},{1,5},{5,1},{2,6},{6,2},{3,7},{7,3},{8,12},{12,8},{9,1... | collective-permute-start | bytes 1769480 | tf_op jit(solution)/shard_map/ppermute | solution.py:288
  83.6 26.6 %collective-permute-start.24 = (bf16[256,1152]{1,0:T(8,128)(2,1)S(1)}, bf16[256,1152]{1,0:T(8,128)(2,1)}, u32[]{:S(2)}, u32[]{:S(2)}) collective-permute-start(bf16[256,1152]{1,0:T(8,128)(2,1)S(1)} %collective-permute-done.refs_1_), channel_id=1, source_target_pairs={{0,4},{4,0},{1,5},{5,1},{2,6},{6,2},{3,7},{7,3},{8,12},{12,8},{9,1... | collective-permute-start | bytes 1769480 | tf_op jit(solution)/shard_map/ppermute | solution.py:288
  95.6 28.9 %collective-permute-start.2 = (bf16[256,1152]{1,0:T(8,128)(2,1)}, bf16[256,1152]{1,0:T(8,128)(2,1)}, u32[]{:S(2)}, u32[]{:S(2)}) collective-permute-start(bf16[256,1152]{1,0:T(8,128)(2,1)} %collective-permute-done.1.refs_2_), channel_id=1, source_target_pairs={{0,1},{1,2},{2,3},{3,0},{4,5},{5,6},{6,7},{7,4},{8,9},{9,10},{10,1... | collective-permute-start | bytes 1769480 | tf_op jit(solution)/shard_map/ppermute | solution.py:235
  106.0 26.9 %collective-permute-start.25 = (bf16[256,1152]{1,0:T(8,128)(2,1)}, bf16[256,1152]{1,0:T(8,128)(2,1)}, u32[]{:S(2)}, u32[]{:S(2)}) collective-permute-start(bf16[256,1152]{1,0:T(8,128)(2,1)} %collective-permute-done.1.refs_2_), channel_id=1, source_target_pairs={{0,4},{4,0},{1,5},{5,1},{2,6},{6,2},{3,7},{7,3},{8,12},{12,8},{9,1... | collective-permute-start | bytes 1769480 | tf_op jit(solution)/shard_map/ppermute | solution.py:288
  108.9 24.1 %collective-permute-start.8 = (bf16[4,64,1024]{2,1,0:T(8,128)(2,1)}, bf16[4,64,1024]{2,1,0:T(8,128)(2,1)}, u32[]{:S(2)}, u32[]{:S(2)}) collective-permute-start(bf16[4,64,1024]{2,1,0:T(8,128)(2,1)} %get-tuple-element.34), channel_id=1, source_target_pairs={{0,8},{8,16},{16,24},{24,0},{1,9},{9,17},{17,25},{25,1},{2,10},{10... | collective-permute-start | bytes 1572872 | tf_op jit(solution)/shard_map/ppermute | solution.py:392
  110.2 28.4 %collective-permute-start.9 = (bf16[4,64,1024]{2,1,0:T(8,128)(2,1)}, bf16[4,64,1024]{2,1,0:T(8,128)(2,1)}, u32[]{:S(2)}, u32[]{:S(2)}) collective-permute-start(bf16[4,64,1024]{2,1,0:T(8,128)(2,1)} %get-tuple-element.35), channel_id=1, source_target_pairs={{0,16},{8,24},{16,0},{24,8},{1,17},{9,25},{17,1},{25,9},{2,18},{10... | collective-permute-start | bytes 1572872 | tf_op jit(solution)/shard_map/ppermute | solution.py:392
  132.9 27.5 %collective-permute-start.12 = (bf16[4,64,1024]{2,1,0:T(8,128)(2,1)}, bf16[4,64,1024]{2,1,0:T(8,128)(2,1)S(1)}, u32[]{:S(2)}, u32[]{:S(2)}) collective-permute-start(bf16[4,64,1024]{2,1,0:T(8,128)(2,1)} %get-tuple-element.38), channel_id=1, source_target_pairs={{0,8},{8,16},{16,24},{24,0},{1,9},{9,17},{17,25},{25,1},{2,10},{10... | collective-permute-start | bytes 1572872 | tf_op jit(solution)/shard_map/ppermute | solution.py:392
  133.0 27.4 %collective-permute-start.19 = (bf16[1,4,64,1024]{3,2,1,0:T(8,128)(2,1)S(1)}, bf16[1,4,64,1024]{3,2,1,0:T(8,128)(2,1)S(1)}, u32[]{:S(2)}, u32[]{:S(2)}) collective-permute-start(bf16[1,4,64,1024]{3,2,1,0:T(8,128)(2,1)S(1)} %slice.64), channel_id=1, source_target_pairs={{0,32},{4,228},{32,64},{36,4},{64,96},{68,36},{96,128},{100,68},{1... | collective-permute-start | bytes 1572872 | tf_op jit(solution)/shard_map/ppermute | solution.py:381
  138.5 24.9 %collective-permute-start.13 = (bf16[4,64,1024]{2,1,0:T(8,128)(2,1)}, bf16[4,64,1024]{2,1,0:T(8,128)(2,1)S(1)}, u32[]{:S(2)}, u32[]{:S(2)}) collective-permute-start(bf16[4,64,1024]{2,1,0:T(8,128)(2,1)} %get-tuple-element.39), channel_id=1, source_target_pairs={{0,16},{8,24},{16,0},{24,8},{1,17},{9,25},{17,1},{25,9},{2,18},{10... | collective-permute-start | bytes 1572872 | tf_op jit(solution)/shard_map/ppermute | solution.py:392
  140.6 24.8 %collective-permute-start.14 = (bf16[4,64,1024]{2,1,0:T(8,128)(2,1)}, bf16[4,64,1024]{2,1,0:T(8,128)(2,1)}, u32[]{:S(2)}, u32[]{:S(2)}) collective-permute-start(bf16[4,64,1024]{2,1,0:T(8,128)(2,1)} %get-tuple-element.40), channel_id=1, source_target_pairs={{0,24},{8,0},{16,8},{24,16},{1,25},{9,1},{17,9},{25,17},{2,26},{10... | collective-permute-start | bytes 1572872 | tf_op jit(solution)/shard_map/ppermute | solution.py:392
  142.4 40.6 %collective-permute-start.16 = (bf16[4,64,1024]{2,1,0:T(8,128)(2,1)}, bf16[4,64,1024]{2,1,0:T(8,128)(2,1)}, u32[]{:S(2)}, u32[]{:S(2)}) collective-permute-start(bf16[4,64,1024]{2,1,0:T(8,128)(2,1)} %get-tuple-element.42), channel_id=1, source_target_pairs={{0,8},{8,16},{16,24},{24,0},{1,9},{9,17},{17,25},{25,1},{2,10},{10... | collective-permute-start | bytes 1572872 | tf_op jit(solution)/shard_map/ppermute | solution.py:392
  160.4 24.4 %collective-permute-start.17 = (bf16[4,64,1024]{2,1,0:T(8,128)(2,1)}, bf16[4,64,1024]{2,1,0:T(8,128)(2,1)}, u32[]{:S(2)}, u32[]{:S(2)}) collective-permute-start(bf16[4,64,1024]{2,1,0:T(8,128)(2,1)} %get-tuple-element.43), channel_id=1, source_target_pairs={{0,16},{8,24},{16,0},{24,8},{1,17},{9,25},{17,1},{25,9},{2,18},{10... | collective-permute-start | bytes 1572872 | tf_op jit(solution)/shard_map/ppermute | solution.py:392
  160.4 26.3 %collective-permute-start.18 = (bf16[4,64,1024]{2,1,0:T(8,128)(2,1)}, bf16[4,64,1024]{2,1,0:T(8,128)(2,1)S(1)}, u32[]{:S(2)}, u32[]{:S(2)}) collective-permute-start(bf16[4,64,1024]{2,1,0:T(8,128)(2,1)} %get-tuple-element.44), channel_id=1, source_target_pairs={{0,24},{8,0},{16,8},{24,16},{1,25},{9,1},{17,9},{25,17},{2,26},{10... | collective-permute-start | bytes 1572872 | tf_op jit(solution)/shard_map/ppermute | solution.py:392
  163.4 25.5 %collective-permute-start.20 = (bf16[2,64,1024]{2,1,0:T(8,128)(2,1)}, bf16[2,64,1024]{2,1,0:T(8,128)(2,1)S(1)}, u32[]{:S(2)}, u32[]{:S(2)}) collective-permute-start(bf16[2,64,1024]{2,1,0:T(8,128)(2,1)} %get-tuple-element.46), channel_id=1, source_target_pairs={{0,8},{8,16},{16,24},{24,0},{1,9},{9,17},{17,25},{25,1},{2,10},{10... | collective-permute-start | bytes 786440 | tf_op jit(solution)/shard_map/ppermute | solution.py:392
  165.4 28.8 %collective-permute-start.21 = (bf16[2,64,1024]{2,1,0:T(8,128)(2,1)}, bf16[2,64,1024]{2,1,0:T(8,128)(2,1)S(1)}, u32[]{:S(2)}, u32[]{:S(2)}) collective-permute-start(bf16[2,64,1024]{2,1,0:T(8,128)(2,1)} %get-tuple-element.47), channel_id=1, source_target_pairs={{0,16},{8,24},{16,0},{24,8},{1,17},{9,25},{17,1},{25,9},{2,18},{10... | collective-permute-start | bytes 786440 | tf_op jit(solution)/shard_map/ppermute | solution.py:392
  212.3 26.1 %collective-permute-start.27 = (bf16[4,4,4,64,256]{4,3,2,1,0:T(8,128)(2,1)}, bf16[4,4,4,64,256]{4,3,2,1,0:T(8,128)(2,1)S(1)}, u32[]{:S(2)}, u32[]{:S(2)}) collective-permute-start(bf16[4,4,4,64,256]{4,3,2,1,0:T(8,128)(2,1)} %get-tuple-element.53), channel_id=1, source_target_pairs={{0,4},{4,0},{1,5},{5,1},{2,6},{6,2},{3,7},{7,3},{8,12},{12,8},{9,1... | collective-permute-start | bytes 6291464 | tf_op jit(solution)/shard_map/ppermute | solution.py:292
  242.2 25.7 %collective-permute-start.29 = (bf16[1024,256]{1,0:T(8,128)(2,1)S(1)}, bf16[1024,256]{1,0:T(8,128)(2,1)S(1)}, u32[]{:S(2)}, u32[]{:S(2)}) collective-permute-start(bf16[1024,256]{1,0:T(8,128)(2,1)S(1)} %bitcast.60), channel_id=1, source_target_pairs={{0,2},{1,3},{2,0},{3,1},{4,6},{5,7},{6,4},{7,5},{8,10},{9,11},{10,... | collective-permute-start | bytes 1572872 | tf_op jit(solution)/shard_map/ppermute | solution.py:296
  244.8 24.6 %collective-permute-start.30 = (bf16[1024,256]{1,0:T(8,128)(2,1)S(1)}, bf16[1024,256]{1,0:T(8,128)(2,1)S(1)}, u32[]{:S(2)}, u32[]{:S(2)}) collective-permute-start(bf16[1024,256]{1,0:T(8,128)(2,1)S(1)} %bitcast.59), channel_id=1, source_target_pairs={{0,3},{1,0},{2,1},{3,2},{4,7},{5,4},{6,5},{7,6},{8,11},{9,8},{10,9... | collective-permute-start | bytes 1572872 | tf_op jit(solution)/shard_map/ppermute | solution.py:296
  280.7 23.5 %collective-permute-start.34 = (bf16[32,4096]{1,0:T(8,128)(2,1)S(1)}, bf16[32,4096]{1,0:T(8,128)(2,1)S(1)}, u32[]{:S(2)}, u32[]{:S(2)}) collective-permute-start(bf16[32,4096]{1,0:T(8,128)(2,1)S(1)} %get-tuple-element.80), channel_id=1, source_target_pairs={{0,24},{8,0},{16,8},{24,16},{1,25},{9,1},{17,9},{25,17},{2,26},{10... | collective-permute-start | bytes 786440 | tf_op jit(solution)/shard_map/ppermute | solution.py:344
  (40 other events, 770.5 us)
Sparse Core Ops, SparseCore 0:
  9.8 124.3 all-gather.1

commit v4 on v3

v4 whole, which is shorter than its diff:
```python
import functools

import jax
import jax.numpy as jnp
from jax import lax
from jax.experimental import pallas as pl
from jax.experimental.pallas import tpu as pltpu
from jax.sharding import Mesh, PartitionSpec as P

EPSILON = 1e-06
DP = ("z", "y", "c")
GROUP = 2
EXTRA = 128
F32 = jnp.float32
BF16 = jnp.bfloat16


def dot(a, b, contract):
    return lax.dot_general(a, b, ((contract[:1], contract[1:]), ((), ())), preferred_element_type=F32)


def unit_rows(values):
    inverse = lax.rsqrt(jnp.sum(values * values, axis=-1, keepdims=True) + EPSILON)
    return (values * inverse, inverse)


def shifted(size, shift):
    return [(i, (i + shift) % size) for i in range(size)]


def loss_and_weight(logits):
    small = jnp.exp(-jnp.abs(logits))
    share = 1.0 / (1.0 + small)
    weight = jnp.where(logits >= 0, share, small * share)
    return (jnp.maximum(logits, 0.0) + jnp.log1p(small), weight)


def project_kernel(features, weight, *refs):
    out, acc = refs[-2:]
    step = pl.program_id(0)

    @pl.when(step == 0)
    def _():
        acc[...] = jnp.zeros_like(acc)

    acc[...] += dot(features[...], weight[...], (1, 0))

    @pl.when(step == pl.num_programs(0) - 1)
    def _():
        unit, inverse = unit_rows(acc[...])
        width = unit.shape[1]
        text = unit.astype(BF16)
        first = inverse.astype(BF16).astype(F32)
        second = (inverse - first).astype(BF16).astype(F32)
        third = inverse - first - second
        lane = lax.broadcasted_iota(jnp.int32, (unit.shape[0], EXTRA), 1)
        terms = jnp.where(lane == 0, first, jnp.where(lane == 1, second, jnp.where(lane == 2, third, 0.0)))
        terms = terms.astype(BF16)
        for k in range(out.shape[0]):
            out[k, :, :width] = text
            out[k, :, width:] = terms


def add_tiles(t, text, acc, sources, slots, counts, scale_bias, arrived, pair_loss):
    scale, bias = scale_bias[0], scale_bias[1]
    piece_rows = arrived.shape[1]
    count = counts[t]

    def each_group(g, carry):
        held = [slots[t, g * GROUP + i] for i in range(GROUP)]
        rows = jnp.concatenate([arrived[held[i]] for i in range(GROUP)], axis=0)
        values = scale * dot(text, rows, (1, 1)) + bias
        terms, shares = loss_and_weight(values)
        sums = jnp.sum(terms, axis=0, keepdims=True)
        left = (count - g * GROUP) * piece_rows
        live = lax.broadcasted_iota(jnp.int32, shares.shape, 1) < left
        shares = jnp.where(live, shares, 0.0).astype(BF16)
        acc[...] += dot(shares, rows, (1, 0))
        for i in range(GROUP):

            @pl.when(g * GROUP + i < count)
            def _():
                source = sources[t, g * GROUP + i]
                pair_loss[pl.ds(source, 1)] = sums[:, i * piece_rows : (i + 1) * piece_rows][None]

        return carry

    lax.fori_loop(0, (count + GROUP - 1) // GROUP, each_group, 0)


def bring(arriving, arrived, starts, sems, half):
    copies = []
    for n, (ref, at) in enumerate(zip(arriving, starts)):
        count = ref.shape[0] // 2
        rows = ref.at[pl.ds(half * count, count)]
        copies.append(pltpu.make_async_copy(rows, arrived.at[pl.ds(at, count)], sems.at[n]))
    return copies


def pair_kernel(sources, slots, counts, place, scale_bias, texts, *refs, starts, own):
    if own:
        own_images, image_docs, text_docs, *refs = refs
    arriving, refs = refs[: len(starts)], refs[len(starts) :]
    chunks, pair_loss, *refs = refs
    if own:
        own_loss, *refs = refs
    acc, arrived, sems = refs
    t = pl.program_id(0)
    quarters, _, _, piece_rows, part = chunks.shape
    width = quarters * part
    copies = bring(arriving, arrived, starts, sems, 0 if own else 1)

    @pl.when(t == 0)
    def _():
        for copy in copies:
            copy.start()
        pair_loss[...] = jnp.zeros_like(pair_loss)

    scale, bias = scale_bias[0], scale_bias[1]
    block = texts[...].reshape(quarters * piece_rows, width + EXTRA)
    text = block[:, :width]
    if own:
        images = own_images[0]
        logits = scale * dot(text, images, (1, 1)) + bias
        same = text_docs[0] == image_docs[0]
        sign = jnp.where(same, 1.0, -1.0)
        loss, weight = loss_and_weight(-sign * logits)
        own_loss[0] = jnp.sum(loss, axis=0, keepdims=True)
        acc[...] = dot((-sign * weight).astype(BF16), images, (1, 0))
    else:
        acc[...] = jnp.zeros_like(acc)

    @pl.when(t == 0)
    def _():
        for copy in copies:
            copy.wait()

    add_tiles(t, text, acc, sources, slots, counts, scale_bias, arrived, pair_loss)
    inverse = jnp.sum(block[:, width:].astype(F32), axis=-1, keepdims=True)
    unit = text.astype(F32)
    grad = scale * acc[...]
    along = jnp.sum(unit * grad, axis=-1, keepdims=True)
    acc[...] = (grad - unit * along) * inverse
    for k in range(quarters):
        start = pl.multiple_of(lax.rem(place[0] + k, quarters) * part, part)
        values = acc[:, pl.ds(start, part)].astype(BF16)
        for j in range(quarters):
            chunks[k, j, 0] = values[j * piece_rows : (j + 1) * piece_rows]


def pick_kernel(table, place, from_ref, *refs, step, sizes, onward):
    z_size, y_size, c_size = sizes
    sems = refs[-1]
    outs = y_size + (onward > 0)
    to_refs = refs[-1 - outs : -1]
    count = from_ref.shape[0]
    back = jnp.where(place[2] == 0, step, z_size - step)
    z = lax.rem(place[3] - back + z_size, z_size)
    copies = []
    if onward:
        copies.append(pltpu.make_async_copy(from_ref.at[pl.ds(0, onward)], to_refs[-1], sems.at[0]))
    for dy in range(y_size):
        y = lax.rem(place[1] + dy, y_size)
        for to in range(c_size):
            for j in range(count):
                source = z * c_size + lax.rem(place[2] + j, c_size)
                block = table[source, y * c_size + lax.rem(place[2] + to, c_size)]
                n = to * count + j
                sem = sems.at[1 + dy * c_size * count + n]
                copies.append(pltpu.make_async_copy(from_ref.at[j, block], to_refs[dy].at[n], sem))
    for copy in copies:
        copy.start()
    for copy in copies:
        copy.wait()


def head_kernel(place, grad_0, grad_1, grad_2, grad_3, feats, first_done, keep, give, turned, *, sizes, strip):
    z_part, y_size, c_size = sizes

    @pl.when(pl.program_id(0) == 0)
    def _():
        total = sum(g[...].astype(F32) for g in (grad_0, grad_1, grad_2, grad_3))
        flipped = total.T.astype(BF16)
        for zz in range(z_part):
            for y in range(y_size):
                for c in range(c_size):
                    block = flipped[((zz * y_size + y) * c_size + c) * strip :][:strip]
                    y_rel = lax.rem(y - place[1] + y_size, y_size)
                    c_rel = lax.rem(c - place[2] + c_size, c_size)
                    to = ((c_rel * y_size + y_rel) * z_part + zz) * strip
                    turned[pl.ds(pl.multiple_of(to, strip), strip)] = block

    half = keep.shape[0]
    total = dot(turned[...], feats[...], (1, 0)).astype(BF16)
    keep[...] = total[:half]
    give[...] = total[half:]


def whole(memory=pltpu.VMEM):
    return pl.BlockSpec(memory_space=memory)


def on_device(
    text_features, head_weight, image_embeds, doc_ids, hard_lists, logit_scale, logit_bias
):
    z_size, y_size, c_size, x_size = (lax.axis_size(name) for name in ("z", "y", "c", "x"))
    z, y, c, x = (lax.axis_index(name) for name in ("z", "y", "c", "x"))
    dp_count = z_size * y_size * c_size
    dp_index = (z * y_size + y) * c_size + c
    blocks, _, piece_rows, feat_width = text_features.shape
    block_rows = image_embeds.shape[1]
    emb_width = head_weight.shape[1]
    rows = blocks * piece_rows
    part = emb_width // x_size
    strip = emb_width // dp_count
    block_iota = jnp.arange(blocks, dtype=jnp.int32)
    peer_iota = jnp.arange(dp_count, dtype=jnp.int32)
    place = jnp.stack([x, y, c, z]).astype(jnp.int32)
    features = text_features.reshape(rows, feat_width)
    feats = lax.all_gather(features, "x", axis=0, tiled=False)

    owners = jnp.where(hard_lists >= 0, hard_lists // blocks, -1).reshape(dp_count, blocks, -1)
    line = owners.reshape(z_size, y_size, c_size, blocks, -1)
    line = lax.dynamic_index_in_dim(line, y, 1, keepdims=False).reshape(z_size * c_size, blocks, -1)
    plane = z * y_size * c_size + jnp.arange(y_size * c_size, dtype=jnp.int32)
    wanted = jnp.any(line[:, None] == plane[:, None, None], axis=3)
    table = jnp.sum(wanted.astype(jnp.int32) * block_iota, axis=2)

    own_images = lax.dynamic_slice_in_dim(image_embeds, x * piece_rows, piece_rows, 1)
    own_images = unit_rows(own_images.astype(F32))[0].astype(BF16)
    groups = exchange_images(own_images, table, place, (z_size, y_size, c_size))

    tile = min(1024, feat_width)
    text_emb = pl.pallas_call(
        project_kernel,
        grid=(feat_width // tile,),
        out_shape=jax.ShapeDtypeStruct((x_size * c_size, rows, emb_width + EXTRA), BF16),
        in_specs=[
            pl.BlockSpec((rows, tile), lambda i: (0, i)),
            pl.BlockSpec((tile, emb_width), lambda i: (i, 0)),
        ]
        + [whole(pl.ANY)],
        out_specs=pl.BlockSpec((x_size * c_size, rows, emb_width + EXTRA), lambda i: (0, 0, 0)),
        scratch_shapes=[pltpu.VMEM((rows, emb_width), F32)],
        compiler_params=pltpu.CompilerParams(vmem_limit_bytes=60 << 20),
        cost_estimate=pl.CostEstimate(flops=1, bytes_accessed=1, transcendentals=0),
        name="project",
    )(features, head_weight, groups[0][0])
    texts = lax.all_to_all(text_emb, ("x", "c"), split_axis=0, concat_axis=0, tiled=True)
    texts = texts.reshape(x_size, c_size, rows, emb_width + EXTRA)

    arrays, starts, slot_base, turns = [], [], [], 0
    for group in groups:
        count = group[0].shape[0] // c_size
        slot_base.append(turns)
        for array in group:
            arrays.append(array)
            starts.append(turns)
            turns += count
    away = jnp.where(c == 0, z - peer_iota // (y_size * c_size), peer_iota // (y_size * c_size) - z) % z_size
    over_y = (y - peer_iota // c_size) % y_size
    over_c = (c - peer_iota) % c_size
    ends = (away == 0) | (away == z_size // 2)
    have = jnp.where(ends, over_c == 0, away < z_size // 2)
    base = sum(jnp.where(away == k, b, 0) for k, b in enumerate(slot_base))
    slot_of = base + jnp.where(ends, over_y, over_y * c_size + over_c)

    text_docs = doc_ids.reshape(blocks, block_rows, 1)
    image_docs = lax.dynamic_slice_in_dim(doc_ids, x * piece_rows, piece_rows, 1)[:, None]
    scale_bias = jnp.stack([logit_scale, logit_bias])

    def lists(holder, here):
        hit = owners == holder
        which = jnp.sum(hit * (hard_lists % blocks).reshape(owners.shape), axis=(1, 2))
        mine = (jnp.any(hit, axis=(1, 2)) & here)[None] & (which[None] == block_iota[:, None])
        before = peer_iota[None] < peer_iota[:, None]
        order = jnp.sum((mine[:, None] & before).astype(jnp.int32), axis=2)
        at = mine[:, None] & (order[:, None] == peer_iota[:, None])
        sources = jnp.sum(jnp.where(at, peer_iota, 0), axis=2)
        return sources, jnp.sum(jnp.where(at, slot_of, 0), axis=2), jnp.sum(mine.astype(jnp.int32), axis=1)

    loss_shape = jax.ShapeDtypeStruct((dp_count, 1, piece_rows), F32)

    def pairs(holder, pieces, own):
        extra, extra_specs, losses, loss_specs = [], [], [], []
        if own:
            extra = [own_images, image_docs, text_docs]
            extra_specs = [pl.BlockSpec((1,) + v.shape[1:], lambda t: (t, 0, 0)) for v in extra]
            losses = [jax.ShapeDtypeStruct((blocks, 1, piece_rows), F32)]
            loss_specs = [pl.BlockSpec((1, 1, piece_rows), lambda t: (t, 0, 0))]
        return pl.pallas_call(
            functools.partial(pair_kernel, starts=starts, own=own),
            grid=(blocks,),
            out_shape=[
                jax.ShapeDtypeStruct((x_size, x_size, blocks, piece_rows, part), BF16),
                loss_shape,
            ]
            + losses,
            in_specs=[whole(pltpu.SMEM)] * 5
            + [pl.BlockSpec((x_size, 1, piece_rows, emb_width + EXTRA), lambda t: (0, t, 0, 0))]
            + extra_specs
            + [whole(pl.ANY)] * len(arrays),
            out_specs=[
                pl.BlockSpec((x_size, x_size, 1, piece_rows, part), lambda t: (0, 0, t, 0, 0)),
                pl.BlockSpec(loss_shape.shape, lambda t: (0, 0, 0)),
            ]
            + loss_specs,
            scratch_shapes=[
                pltpu.VMEM((block_rows, emb_width), F32),
                pltpu.VMEM((turns, piece_rows, emb_width), BF16),
                pltpu.SemaphoreType.DMA((len(arrays),)),
            ],
            compiler_params=pltpu.CompilerParams(vmem_limit_bytes=32 << 20),
            cost_estimate=pl.CostEstimate(flops=1, bytes_accessed=1, transcendentals=0),
            name="pairs",
        )(
            *lists(holder, have),
            place,
            scale_bias,
            pieces.reshape(x_size, blocks, piece_rows, emb_width + EXTRA),
            *extra,
            *arrays,
        )

    other_texts = lax.dynamic_index_in_dim(texts, 1 - c, 1, keepdims=False)
    other_chunks, other_loss = pairs(dp_index + 1 - 2 * c, other_texts, False)
    own_texts = lax.dynamic_index_in_dim(texts, c, 1, keepdims=False)
    chunks, pair_loss, own_loss = pairs(dp_index, own_texts, True)

    returned = lax.all_to_all(
        jnp.concatenate([pair_loss, other_loss], axis=1), DP, split_axis=0, concat_axis=0, tiled=True
    )

    taken = lax.ppermute(other_chunks, "c", shifted(c_size, 1))
    grads = []
    for k in range(x_size):
        total = (chunks[k].astype(F32) + taken[k].astype(F32)).astype(BF16).reshape(x_size * rows, part)
        grads.append(lax.ppermute(total, "x", shifted(x_size, k)) if k else total)
    z_part = z_size // x_size
    half = part // c_size
    keep, give = pl.pallas_call(
        functools.partial(head_kernel, sizes=(z_part, y_size, c_size), strip=strip),
        grid=(feat_width // tile,),
        out_shape=(
            jax.ShapeDtypeStruct((half, feat_width), BF16),
            jax.ShapeDtypeStruct((half, feat_width), BF16),
        ),
        in_specs=[whole(pltpu.SMEM)]
        + [whole()] * 4
        + [pl.BlockSpec((x_size * rows, tile), lambda i: (0, i)), whole(pl.ANY)],
        out_specs=(
            pl.BlockSpec((half, tile), lambda i: (0, i)),
            pl.BlockSpec((half, tile), lambda i: (0, i)),
        ),
        scratch_shapes=[pltpu.VMEM((part, x_size * rows), BF16)],
        compiler_params=pltpu.CompilerParams(vmem_limit_bytes=60 << 20),
        cost_estimate=pl.CostEstimate(
            flops=2 * rows * feat_width * emb_width, bytes_accessed=16 << 20, transcendentals=0
        ),
        name="head",
    )(place, *grads, feats.reshape(x_size * rows, feat_width), returned)

    swapped = returned.reshape(-1, c_size, 2, piece_rows)[:, ::-1, 1].reshape(dp_count, piece_rows)
    returned = returned[:, 0] + swapped
    my_owners = lax.dynamic_index_in_dim(owners, dp_index, 0, keepdims=False)
    asked = jnp.any(my_owners[None] == peer_iota[:, None, None], axis=2)
    remote_loss = jnp.sum(jnp.where(asked[..., None], returned[:, None], 0.0), axis=0)
    row_loss = (own_loss.reshape(blocks, piece_rows) + remote_loss) / block_rows
    return (row_loss, add_over_dp(keep, give, (z_size, y_size, c_size, x_size), z, strip))


def add_over_dp(keep, give, sizes, z, strip):
    z_size, y_size, c_size, x_size = sizes
    z_part = z_size // x_size
    width = keep.shape[1]

    def add(*values):
        return sum(v.astype(F32) for v in values).astype(BF16)

    total = add(keep, lax.ppermute(give, "c", shifted(c_size, 1)))
    total = total.reshape(y_size, z_part * strip, width)
    total = add(
        total[0], *(lax.ppermute(total[k], "y", shifted(y_size, k)) for k in range(1, y_size))
    ).reshape(z_part, strip, width)
    low, top = z % 2, z // (z_size // 2)
    given = lax.dynamic_index_in_dim(total, 1 - low, 0, keepdims=False)
    kept = lax.dynamic_index_in_dim(total, low, 0, keepdims=False)
    total = add(kept, lax.ppermute(given, "z", [(i, i ^ 1) for i in range(z_size)]))
    total = total.reshape(strip, 2, width // 2)
    given = lax.dynamic_index_in_dim(total, 1 - top, 1, keepdims=False)
    kept = lax.dynamic_index_in_dim(total, top, 1, keepdims=False)
    total = add(kept, lax.ppermute(given, "z", [(i, (i + z_size // 2) % z_size) for i in range(z_size)]))
    total = total.reshape(strip, 2, width // 4)
    final = 0.0
    for flip in range(2):
        pairs = []
        for z_from in range(z_size):
            bit = (z_from // 2 % 2) ^ flip
            for x_from in range(x_size):
                to_z, to_x = z_part * x_from + z_from % 2, z_from // (z_size // 2) * 2 + bit
                pairs.append((z_from * x_size + x_from, to_z * x_size + to_x))
        chunk = lax.dynamic_index_in_dim(total, (z // 2 % 2) ^ flip, 1, keepdims=False)
        final = final + lax.ppermute(chunk, ("z", "x"), pairs).astype(F32)
    return final.T


def exchange_images(own_images, table, place, sizes):
    z_size, y_size, c_size = sizes
    onward = []
    for z in range(z_size):
        onward.append((z * c_size, (z + 1) % z_size * c_size))
        onward.append((z * c_size + 1, (z - 1) % z_size * c_size + 1))
    moving = jnp.stack([own_images, lax.ppermute(own_images, "c", shifted(c_size, 1))])
    groups = []
    last = z_size // 2
    for step in range(last + 1):
        here = own_images[None] if step == 0 else lax.ppermute(moving, ("z", "c"), onward)
        keeps = 0 if step in (0, last) else 1 if step == last - 1 else c_size
        shape = (c_size * here.shape[0],) + own_images.shape[1:]
        outs = [jax.ShapeDtypeStruct(shape, BF16)] * y_size
        if keeps:
            outs.append(jax.ShapeDtypeStruct((keeps,) + own_images.shape, BF16))
        before = [groups[step - 1][1], groups[step - 1][-1]] if step in (1, 2) else []
        picked = pl.pallas_call(
            functools.partial(pick_kernel, step=step, sizes=sizes, onward=keeps),
            out_shape=outs,
            in_specs=[whole(pltpu.SMEM)] * 2 + [whole()] + [whole(pl.ANY)] * len(before),
            out_specs=[whole(pl.ANY)] * len(outs),
            scratch_shapes=[pltpu.SemaphoreType.DMA((1 + y_size * shape[0],))],
            cost_estimate=pl.CostEstimate(flops=1, bytes_accessed=1, transcendentals=0),
            name="pick",
        )(table, place, here, *before)
        if keeps:
            moving = picked[-1]
        groups.append(
            [picked[0]] + [lax.ppermute(picked[n], "y", shifted(y_size, n)) for n in range(1, y_size)]
        )
    return groups


def solution(mesh):
    x_size = mesh.shape["replica"]
    c_size = 2
    z_size = 2 * x_size
    y_size = mesh.shape["dp"] // (z_size * c_size)
    fine = Mesh(mesh.devices.reshape(z_size, y_size, c_size, x_size), ("z", "y", "c", "x"))
    placed = (P(DP, "x", None, None), P(), P(DP, None, None), P(DP, None), P(), P(), P())
    return jax.shard_map(
        on_device,
        mesh=fine,
        in_specs=placed,
        out_specs=(P(DP, "x"), P("x", DP)),
        check_vma=False,
    )
```

time: 345 us -> 296 us (0.86); the launches traced: 340 us -> 295 us
  waiting for transfers between devices: 174 us -> 110 us
  local copies, waits for them, and re-layouts: 8.36 us -> 31.5 us
  starting transfers between devices: 73.4 us -> 54 us
  blocking collectives: 0 us -> 18 us
    ppermute x11 -> x4, waiting for transfers between devices: 66 us -> 17.3 us  [exchange_images(): lax.ppermute(moving, ('z', 'c'), onward)]
    unnamed x52 -> x120, local copies, waits for them, and re-layouts: 5.16 us -> 25.3 us
    ppermute x3, waiting for transfers between devices: 22.1 us -> 3.83 us  [on_device(): grads.append(lax.ppermute(total, 'x', shifted(x_size, k)) if k else total)]
    all_to_all x0 -> x1, blocking collectives: none -> 18 us  [on_device(): lax.all_to_all(jnp.concatenate([pair_loss, other_loss], axis=1), DP, spli...]
    ppermute x3, waiting for transfers between devices: 0.01 us -> 12.7 us  [add_over_dp(): lax.ppermute(total[k], 'y', shifted(y_size, k))]
    ppermute x1, starting transfers between devices: 9.78 us -> 1.29 us  [on_device(): taken = lax.ppermute(other_chunks, 'c', shifted(c_size, 1))]
    all_to_all x1, waiting for transfers between devices: 9.38 us -> 2.21 us  [on_device(): lax.all_to_all(text_emb, ('x', 'c'), split_axis=0, concat_axis=0, tiled=T...]
    ppermute x11 -> x4, starting transfers between devices: 6.29 us -> 0.91 us  [exchange_images(): lax.ppermute(moving, ('z', 'c'), onward)]
  transfers between devices with their start and end apart: 41 -> 34, of which waited for: 22 -> 25; matrix products, arithmetic and copies ran while one was open for 5% -> 6% of each run, Pallas kernels for 13% -> 15%
where the time goes in v4:
time: 296 us; the launch traced here: 295 us
  waiting for transfers between devices  110 us (37%)
  starting transfers between devices  54 us (18%)
  Pallas kernels  51.6 us (17%)
  local copies, waits for them, and re-layouts  31.5 us (11%)
  blocking collectives  18 us (6%)
  between operations  16.1 us (5%)
  other arithmetic  14.2 us (5%)
    ppermute x15, waiting for transfers between devices, exchange_images(): lax.ppermute(picked[n], 'y', shifted(y_size, n))  54.7 us
    unnamed x120, local copies, waits for them, and re-layouts  25.3 us
    ppermute x15, starting transfers between devices, exchange_images(): lax.ppermute(picked[n], 'y', shifted(y_size, n))  23.3 us
    pallas_call x2, Pallas kernels, pairs(): pl.pallas_call(functools.partial(pair_kernel, starts=starts, own=own), gr...  22.3 us
    all_to_all x1, blocking collectives, on_device(): lax.all_to_all(jnp.concatenate([pair_loss, other_loss], axis=1), DP, spli...  18 us
    ppermute x4, waiting for transfers between devices, exchange_images(): lax.ppermute(moving, ('z', 'c'), onward)  17.3 us
    pallas_call x5, Pallas kernels, exchange_images(): pl.pallas_call(functools.partial(pick_kernel, step=step, sizes=sizes, onw...  13.3 us
    ppermute x3, waiting for transfers between devices, add_over_dp(): lax.ppermute(total[k], 'y', shifted(y_size, k))  12.7 us
  transfers between devices with their start and end apart: 34, of which 25 were waited for; matrix products, arithmetic and copies ran while one was open for 6% of the time, Pallas kernels for 15%

profile of v4, /device:TPU:4, one launch (start us, length us, event | category | flops | bytes accessed | tf_op | source)
XLA Modules:
  0.0 295.0 jit_solution(4015550254150719651)
XLA Ops:
  15.1 8.6 %project.1 = bf16[8,256,1152]{2,1,0:T(8,128)(2,1)} custom-call(bf16[256,4096]{1,0:T(8,128)(2,1)} %bitcast.64, bf16[4096,1024]{1,0:T(8,128)(2,1)} %weight.1, bf16[2,64,1024]{2,1,0:T(8,128)(2,1)} %get-tuple-element.32.refs_0_.refs_3_), custom_call_target="tpu_custom_call" | custom-call | flops 1 | bytes 1 | tf_op jit(solution)/shard_map/project/pallas_call | solution.py:234
  23.7 7.1 %all-to-all-start = ((bf16[8,256,1152]{2,1,0:T(8,128)(2,1)}), bf16[8,256,1152]{2,1,0:T(8,128)(2,1)}, u32[]{:S(2)}, u32[]{:S(2)}) async-start(bf16[8,256,1152]{2,1,0:T(8,128)(2,1)} %project.1), calls=%async_computation | async-start | bytes 9437184 | tf_op jit(solution)/shard_map/all_to_all | solution.py:249
  35.5 4.3 %collective-permute-done.refs_0_.refs_4_.refs_1_ = bf16[2,64,1024]{2,1,0:T(8,128)(2,1)S(1)} collective-permute-done((bf16[2,64,1024]{2,1,0:T(8,128)(2,1)S(1)}, bf16[2,64,1024]{2,1,0:T(8,128)(2,1)S(1)}, u32[]{:S(2)}, u32[]{:S(2)}) %collective-permute-start) | collective-permute-done | bytes 262176 | tf_op jit(solution)/shard_map/ppermute | solution.py:436
  40.3 8.7 %collective-permute-done.4.from_ref = bf16[2,4,64,1024]{3,2,1,0:T(8,128)(2,1)S(1)} collective-permute-done((bf16[2,4,64,1024]{3,2,1,0:T(8,128)(2,1)S(1)}, bf16[2,4,64,1024]{3,2,1,0:T(8,128)(2,1)S(1)}, u32[]{:S(2)}, u32[]{:S(2)}) %collective-permute-start.4) | collective-permute-done | bytes 1048608 | tf_op jit(solution)/shard_map/ppermute | solution.py:417
  56.5 11.7 %collective-permute-done.5.refs_0_.refs_8_.refs_5_ = bf16[4,64,1024]{2,1,0:T(8,128)(2,1)S(1)} collective-permute-done((bf16[4,64,1024]{2,1,0:T(8,128)(2,1)}, bf16[4,64,1024]{2,1,0:T(8,128)(2,1)S(1)}, u32[]{:S(2)}, u32[]{:S(2)}) %collective-permute-start.5) | collective-permute-done | bytes 524320 | tf_op jit(solution)/shard_map/ppermute | solution.py:436
  81.9 8.2 %collective-permute-done.12.from_ref = bf16[2,4,64,1024]{3,2,1,0:T(8,128)(2,1)S(1)} collective-permute-done((bf16[2,4,64,1024]{3,2,1,0:T(8,128)(2,1)}, bf16[2,4,64,1024]{3,2,1,0:T(8,128)(2,1)S(1)}, u32[]{:S(2)}, u32[]{:S(2)}) %collective-permute-start.12) | collective-permute-done | bytes 1048608 | tf_op jit(solution)/shard_map/ppermute | solution.py:417
  100.8 6.8 %collective-permute-done.9.refs_12_.refs_9_ = bf16[4,64,1024]{2,1,0:T(8,128)(2,1)S(1)} collective-permute-done((bf16[4,64,1024]{2,1,0:T(8,128)(2,1)}, bf16[4,64,1024]{2,1,0:T(8,128)(2,1)S(1)}, u32[]{:S(2)}, u32[]{:S(2)}) %collective-permute-start.9) | collective-permute-done | bytes 524320 | tf_op jit(solution)/shard_map/ppermute | solution.py:436
  114.4 4.4 %collective-permute-done.10.refs_13_.refs_10_ = bf16[4,64,1024]{2,1,0:T(8,128)(2,1)S(1)} collective-permute-done((bf16[4,64,1024]{2,1,0:T(8,128)(2,1)}, bf16[4,64,1024]{2,1,0:T(8,128)(2,1)S(1)}, u32[]{:S(2)}, u32[]{:S(2)}) %collective-permute-start.10) | collective-permute-done | bytes 524320 | tf_op jit(solution)/shard_map/ppermute | solution.py:436
  125.2 4.8 %collective-permute-done.13.refs_16_.refs_13_ = bf16[4,64,1024]{2,1,0:T(8,128)(2,1)S(1)} collective-permute-done((bf16[4,64,1024]{2,1,0:T(8,128)(2,1)}, bf16[4,64,1024]{2,1,0:T(8,128)(2,1)S(1)}, u32[]{:S(2)}, u32[]{:S(2)}) %collective-permute-start.13) | collective-permute-done | bytes 524320 | tf_op jit(solution)/shard_map/ppermute | solution.py:436
  136.8 4.7 %collective-permute-done.14.refs_17_.refs_14_ = bf16[4,64,1024]{2,1,0:T(8,128)(2,1)} collective-permute-done((bf16[4,64,1024]{2,1,0:T(8,128)(2,1)}, bf16[4,64,1024]{2,1,0:T(8,128)(2,1)}, u32[]{:S(2)}, u32[]{:S(2)}) %collective-permute-start.14) | collective-permute-done | bytes 524320 | tf_op jit(solution)/shard_map/ppermute | solution.py:436
  141.5 3.4 %collective-permute-done.15.refs_18_.refs_15_ = bf16[4,64,1024]{2,1,0:T(8,128)(2,1)} collective-permute-done((bf16[4,64,1024]{2,1,0:T(8,128)(2,1)}, bf16[4,64,1024]{2,1,0:T(8,128)(2,1)}, u32[]{:S(2)}, u32[]{:S(2)}) %collective-permute-start.15) | collective-permute-done | bytes 524320 | tf_op jit(solution)/shard_map/ppermute | solution.py:436
  146.9 5.7 %collective-permute-done.18.refs_21_.refs_18_ = bf16[2,64,1024]{2,1,0:T(8,128)(2,1)} collective-permute-done((bf16[2,64,1024]{2,1,0:T(8,128)(2,1)}, bf16[2,64,1024]{2,1,0:T(8,128)(2,1)}, u32[]{:S(2)}, u32[]{:S(2)}) %collective-permute-start.18) | collective-permute-done | bytes 262176 | tf_op jit(solution)/shard_map/ppermute | solution.py:436
  155.7 10.7 %pairs.3 = (bf16[4,4,4,64,256]{4,3,2,1,0:T(8,128)(2,1)}, f32[64,1,64]{2,1,0:T(1,128)S(1)}) custom-call(s32[4,64]{1,0:T(4,128)S(1)} %get-tuple-element.67.sources, s32[4,64]{1,0:T(4,128)S(1)} %get-tuple-element.66.slots, s32[4]{0:T(128)S(1)} %get-tuple-element.72.counts, s32[4]{0:T(128)S(1)} %copy-done.41, f32[2]{0:T(128)S(1)} %pad_maximum_fusion.2.scale_bias, ...), custom_call_target="tpu_custom_call" | custom-call | flops 1 | bytes 1 | tf_op jit(solution)/shard_map/pairs/pallas_call | solution.py:291
  184.0 11.6 %pairs.2 = (bf16[4,4,4,64,256]{4,3,2,1,0:T(8,128)(2,1)S(1)}, f32[64,1,64]{2,1,0:T(1,128)S(1)}, f32[4,1,64]{2,1,0:T(1,128)S(1)}) custom-call(s32[4,64]{1,0:T(4,128)S(1)} %get-tuple-element.70.sources, s32[4,64]{1,0:T(4,128)S(1)} %get-tuple-element.71.slots, s32[4]{0:T(128)S(1)} %get-tuple-element.94.counts, s32[4]{0:T(128)S(1)} %copy-done.41, ...), custom_call_target="tpu_custom_call" | custom-call | flops 1 | bytes 1 | tf_op jit(solution)/shard_map/pairs/pallas_call | solution.py:291
  195.7 3.1 %add_convert_fusion.1 = (bf16[1,4,4,64,256]{4,3,2,1,0:T(8,128)(2,1)S(1)}, bf16[1,4,4,64,256]{4,3,2,1,0:T(8,128)(2,1)S(1)}, bf16[1,4,4,64,256]{4,3,2,1,0:T(8,128)(2,1)S(1)}, bf16[1,4,4,64,256]{4,3,2,1,0:T(8,128)(2,1)}) fusion(bf16[4,4,4,64,256]{4,3,2,1,0:T(8,128)(2,1)} %collective-permute-done.20, bf16[4,4,4,64,256]{4,3,2,1,0:T(8,128)(2,1)S(1)} %get-tuple-element.58), kind=kLoop, calls=%fused_computation.6 | loop fusion | flops 4194304 | bytes 6291456 | tf_op jit(solution)/shard_map/convert_element_type | solution.py:337
  202.7 18.0 %all_to_all.10 = f32[64,1,128]{2,1,0:T(1,128)S(1)} all-to-all(f32[64,1,128]{2,1,0:T(1,128)S(1)} %reshape.243), channel_id=1, replica_groups=mesh['z'=8,'y'=4,'c'=2,'x'=4] {'z','y','c'}, dimensions={0} | all-to-all | bytes 65536 | tf_op jit(solution)/shard_map/all_to_all | solution.py:330
  227.3 7.4 %head.1 = (bf16[128,4096]{1,0:T(8,128)(2,1)}, bf16[128,4096]{1,0:T(8,128)(2,1)}) custom-call(s32[4]{0:T(128)} %pad_add_fusion.place, bf16[1024,256]{1,0:T(8,128)(2,1)} %bitcast.65, bf16[1024,256]{1,0:T(8,128)(2,1)} %copy-done.50, bf16[1024,256]{1,0:T(8,128)(2,1)} %copy-done.51, bf16[1024,256]{1,0:T(8,128)(2,1)} %copy-done.52, bf16[1024,4096]{1,0:T(8,128)(2,1)} %bitcast.62, ...), custom_call_target="tpu_custom_call" | custom-call | flops 2147483648 | bytes 16777216 | tf_op jit(solution)/shard_map/head/pallas_call | solution.py:341
  239.2 3.3 %collective-permute-start.27 = (bf16[32,4096]{1,0:T(8,128)(2,1)S(1)}, bf16[32,4096]{1,0:T(8,128)(2,1)S(1)}, u32[]{:S(2)}, u32[]{:S(2)}) collective-permute-start(bf16[32,4096]{1,0:T(8,128)(2,1)S(1)} %get-tuple-element.88), channel_id=1, source_target_pairs={{0,24},{8,0},{16,8},{24,16},{1,25},{9,1},{17,9},{25,17},{2,26},{10... | collective-permute-start | bytes 786440 | tf_op jit(solution)/shard_map/ppermute | solution.py:383
  245.0 9.0 %collective-permute-done.27 = bf16[32,4096]{1,0:T(8,128)(2,1)S(1)} collective-permute-done((bf16[32,4096]{1,0:T(8,128)(2,1)S(1)}, bf16[32,4096]{1,0:T(8,128)(2,1)S(1)}, u32[]{:S(2)}, u32[]{:S(2)}) %collective-permute-start.27) | collective-permute-done | bytes 262176 | tf_op jit(solution)/shard_map/ppermute | solution.py:383
  254.0 3.7 %collective-permute-done.25 = bf16[32,4096]{1,0:T(8,128)(2,1)S(1)} collective-permute-done((bf16[32,4096]{1,0:T(8,128)(2,1)S(1)}, bf16[32,4096]{1,0:T(8,128)(2,1)S(1)}, u32[]{:S(2)}, u32[]{:S(2)}) %collective-permute-start.25) | collective-permute-done | bytes 262176 | tf_op jit(solution)/shard_map/ppermute | solution.py:383
  258.0 5.4 %collective-permute-done.28 = bf16[16,4096]{1,0:T(8,128)(2,1)S(1)} collective-permute-done((bf16[16,4096]{1,0:T(8,128)(2,1)S(1)}, bf16[16,4096]{1,0:T(8,128)(2,1)S(1)}, u32[]{:S(2)}, u32[]{:S(2)}) %collective-permute-start.28) | collective-permute-done | bytes 131104 | tf_op jit(solution)/shard_map/ppermute | solution.py:388
  266.1 6.1 %collective-permute-done.29 = bf16[16,2048]{1,0:T(8,128)(2,1)S(1)} collective-permute-done((bf16[16,2048]{1,0:T(8,128)(2,1)S(1)}, bf16[16,2048]{1,0:T(8,128)(2,1)S(1)}, u32[]{:S(2)}, u32[]{:S(2)}) %collective-permute-start.29) | collective-permute-done | bytes 65568 | tf_op jit(solution)/shard_map/ppermute | solution.py:392
  275.4 7.4 %collective-permute-start.30 = (bf16[16,1024]{1,0:T(8,128)(2,1)S(1)}, bf16[16,1024]{1,0:T(8,128)(2,1)S(1)}, u32[]{:S(2)}, u32[]{:S(2)}) collective-permute-start(bf16[16,1024]{1,0:T(8,128)(2,1)S(1)} %bitcast.78), channel_id=1, source_target_pairs={{0,0},{1,64},{2,128},{3,192},{32,32},{33,96},{34,160},{35,224},{64... | collective-permute-start | bytes 98312 | tf_op jit(solution)/shard_map/ppermute | solution.py:403
  283.4 4.1 %collective-permute-done.30 = bf16[16,1024]{1,0:T(8,128)(2,1)S(1)} collective-permute-done((bf16[16,1024]{1,0:T(8,128)(2,1)S(1)}, bf16[16,1024]{1,0:T(8,128)(2,1)S(1)}, u32[]{:S(2)}, u32[]{:S(2)}) %collective-permute-start.30) | collective-permute-done | bytes 32800 | tf_op jit(solution)/shard_map/ppermute | solution.py:403
  (230 shorter events, 110.6 us)
Async XLA Ops:
  7.2 219.3 %all-gather.2.cloned.1.call-start = ((), (), s32[]{:S(2)}) async-start(), calls=%async_computation.2 | async-start | bytes 10485760 | tf_op jit(solution)/shard_map/all_gather | solution.py:220
  9.1 21.7 %collective-permute-start.3 = (bf16[4,64,1024]{2,1,0:T(8,128)(2,1)S(1)}, bf16[4,64,1024]{2,1,0:T(8,128)(2,1)}, u32[]{:S(2)}, u32[]{:S(2)}) collective-permute-start(bf16[4,64,1024]{2,1,0:T(8,128)(2,1)S(1)} %fusion.1.refs_0_), channel_id=1, source_target_pairs={{0,4},{4,0},{1,5},{5,1},{2,6},{6,2},{3,7},{7,3},{8,12},{12,8},{9,1... | collective-permute-start | bytes 1572872 | tf_op jit(solution)/shard_map/ppermute | solution.py:413
  23.7 110.0 %all-to-all-start = ((bf16[8,256,1152]{2,1,0:T(8,128)(2,1)}), bf16[8,256,1152]{2,1,0:T(8,128)(2,1)}, u32[]{:S(2)}, u32[]{:S(2)}) async-start(bf16[8,256,1152]{2,1,0:T(8,128)(2,1)} %project.1), calls=%async_computation | async-start | bytes 9437184 | tf_op jit(solution)/shard_map/all_to_all | solution.py:249
  32.0 17.0 %collective-permute-start.4 = (bf16[2,4,64,1024]{3,2,1,0:T(8,128)(2,1)S(1)}, bf16[2,4,64,1024]{3,2,1,0:T(8,128)(2,1)S(1)}, u32[]{:S(2)}, u32[]{:S(2)}) collective-permute-start(bf16[2,4,64,1024]{3,2,1,0:T(8,128)(2,1)S(1)} %pad_maximum_fusion), channel_id=1, source_target_pairs={{0,32},{4,228},{32,64},{36,4},{64,96},{68,36},{96,128},{100,68},{1... | collective-permute-start | bytes 3145736 | tf_op jit(solution)/shard_map/ppermute | solution.py:417
  53.1 16.3 %collective-permute-start.8 = (bf16[2,4,64,1024]{3,2,1,0:T(8,128)(2,1)}, bf16[2,4,64,1024]{3,2,1,0:T(8,128)(2,1)S(1)}, u32[]{:S(2)}, u32[]{:S(2)}) collective-permute-start(bf16[2,4,64,1024]{3,2,1,0:T(8,128)(2,1)} %get-tuple-element.40), channel_id=1, source_target_pairs={{0,32},{4,228},{32,64},{36,4},{64,96},{68,36},{96,128},{100,68},{1... | collective-permute-start | bytes 3145736 | tf_op jit(solution)/shard_map/ppermute | solution.py:417
  53.2 15.0 %collective-permute-start.5 = (bf16[4,64,1024]{2,1,0:T(8,128)(2,1)}, bf16[4,64,1024]{2,1,0:T(8,128)(2,1)S(1)}, u32[]{:S(2)}, u32[]{:S(2)}) collective-permute-start(bf16[4,64,1024]{2,1,0:T(8,128)(2,1)} %get-tuple-element.37), channel_id=1, source_target_pairs={{0,8},{8,16},{16,24},{24,0},{1,9},{9,17},{17,25},{25,1},{2,10},{10... | collective-permute-start | bytes 1572872 | tf_op jit(solution)/shard_map/ppermute | solution.py:436
  73.8 16.3 %collective-permute-start.12 = (bf16[2,4,64,1024]{3,2,1,0:T(8,128)(2,1)}, bf16[2,4,64,1024]{3,2,1,0:T(8,128)(2,1)S(1)}, u32[]{:S(2)}, u32[]{:S(2)}) collective-permute-start(bf16[2,4,64,1024]{3,2,1,0:T(8,128)(2,1)} %get-tuple-element.45), channel_id=1, source_target_pairs={{0,32},{4,228},{32,64},{36,4},{64,96},{68,36},{96,128},{100,68},{1... | collective-permute-start | bytes 3145736 | tf_op jit(solution)/shard_map/ppermute | solution.py:417
  74.2 23.2 %collective-permute-start.1 = (bf16[2,64,1024]{2,1,0:T(8,128)(2,1)}, bf16[2,64,1024]{2,1,0:T(8,128)(2,1)S(1)}, u32[]{:S(2)}, u32[]{:S(2)}) collective-permute-start(bf16[2,64,1024]{2,1,0:T(8,128)(2,1)} %get-tuple-element.34), channel_id=1, source_target_pairs={{0,16},{8,24},{16,0},{24,8},{1,17},{9,25},{17,1},{25,9},{2,18},{10... | collective-permute-start | bytes 786440 | tf_op jit(solution)/shard_map/ppermute | solution.py:436
  77.5 21.9 %collective-permute-start.6 = (bf16[4,64,1024]{2,1,0:T(8,128)(2,1)}, bf16[4,64,1024]{2,1,0:T(8,128)(2,1)S(1)}, u32[]{:S(2)}, u32[]{:S(2)}) collective-permute-start(bf16[4,64,1024]{2,1,0:T(8,128)(2,1)} %get-tuple-element.38), channel_id=1, source_target_pairs={{0,16},{8,24},{16,0},{24,8},{1,17},{9,25},{17,1},{25,9},{2,18},{10... | collective-permute-start | bytes 1572872 | tf_op jit(solution)/shard_map/ppermute | solution.py:436
  80.4 27.2 %collective-permute-start.9 = (bf16[4,64,1024]{2,1,0:T(8,128)(2,1)}, bf16[4,64,1024]{2,1,0:T(8,128)(2,1)S(1)}, u32[]{:S(2)}, u32[]{:S(2)}) collective-permute-start(bf16[4,64,1024]{2,1,0:T(8,128)(2,1)} %get-tuple-element.42), channel_id=1, source_target_pairs={{0,8},{8,16},{16,24},{24,0},{1,9},{9,17},{17,25},{25,1},{2,10},{10... | collective-permute-start | bytes 1572872 | tf_op jit(solution)/shard_map/ppermute | solution.py:436
  94.1 17.1 %collective-permute-start.16 = (bf16[1,4,64,1024]{3,2,1,0:T(8,128)(2,1)}, bf16[1,4,64,1024]{3,2,1,0:T(8,128)(2,1)S(1)}, u32[]{:S(2)}, u32[]{:S(2)}) collective-permute-start(bf16[1,4,64,1024]{3,2,1,0:T(8,128)(2,1)} %get-tuple-element.50), channel_id=1, source_target_pairs={{0,32},{4,228},{32,64},{36,4},{64,96},{68,36},{96,128},{100,68},{1... | collective-permute-start | bytes 1572872 | tf_op jit(solution)/shard_map/ppermute | solution.py:417
  94.4 24.5 %collective-permute-start.10 = (bf16[4,64,1024]{2,1,0:T(8,128)(2,1)}, bf16[4,64,1024]{2,1,0:T(8,128)(2,1)S(1)}, u32[]{:S(2)}, u32[]{:S(2)}) collective-permute-start(bf16[4,64,1024]{2,1,0:T(8,128)(2,1)} %get-tuple-element.43), channel_id=1, source_target_pairs={{0,16},{8,24},{16,0},{24,8},{1,17},{9,25},{17,1},{25,9},{2,18},{10... | collective-permute-start | bytes 1572872 | tf_op jit(solution)/shard_map/ppermute | solution.py:436
  98.0 24.2 %collective-permute-start.11 = (bf16[4,64,1024]{2,1,0:T(8,128)(2,1)}, bf16[4,64,1024]{2,1,0:T(8,128)(2,1)S(1)}, u32[]{:S(2)}, u32[]{:S(2)}) collective-permute-start(bf16[4,64,1024]{2,1,0:T(8,128)(2,1)} %get-tuple-element.44), channel_id=1, source_target_pairs={{0,24},{8,0},{16,8},{24,16},{1,25},{9,1},{17,9},{25,17},{2,26},{10... | collective-permute-start | bytes 1572872 | tf_op jit(solution)/shard_map/ppermute | solution.py:436
  99.4 30.6 %collective-permute-start.13 = (bf16[4,64,1024]{2,1,0:T(8,128)(2,1)}, bf16[4,64,1024]{2,1,0:T(8,128)(2,1)S(1)}, u32[]{:S(2)}, u32[]{:S(2)}) collective-permute-start(bf16[4,64,1024]{2,1,0:T(8,128)(2,1)} %get-tuple-element.47), channel_id=1, source_target_pairs={{0,8},{8,16},{16,24},{24,0},{1,9},{9,17},{17,25},{25,1},{2,10},{10... | collective-permute-start | bytes 1572872 | tf_op jit(solution)/shard_map/ppermute | solution.py:436
  108.4 33.1 %collective-permute-start.14 = (bf16[4,64,1024]{2,1,0:T(8,128)(2,1)}, bf16[4,64,1024]{2,1,0:T(8,128)(2,1)}, u32[]{:S(2)}, u32[]{:S(2)}) collective-permute-start(bf16[4,64,1024]{2,1,0:T(8,128)(2,1)} %get-tuple-element.48), channel_id=1, source_target_pairs={{0,16},{8,24},{16,0},{24,8},{1,17},{9,25},{17,1},{25,9},{2,18},{10... | collective-permute-start | bytes 1572872 | tf_op jit(solution)/shard_map/ppermute | solution.py:436
  111.2 33.7 %collective-permute-start.15 = (bf16[4,64,1024]{2,1,0:T(8,128)(2,1)}, bf16[4,64,1024]{2,1,0:T(8,128)(2,1)}, u32[]{:S(2)}, u32[]{:S(2)}) collective-permute-start(bf16[4,64,1024]{2,1,0:T(8,128)(2,1)} %get-tuple-element.49), channel_id=1, source_target_pairs={{0,24},{8,0},{16,8},{24,16},{1,25},{9,1},{17,9},{25,17},{2,26},{10... | collective-permute-start | bytes 1572872 | tf_op jit(solution)/shard_map/ppermute | solution.py:436
  119.7 27.2 %collective-permute-start.17 = (bf16[2,64,1024]{2,1,0:T(8,128)(2,1)}, bf16[2,64,1024]{2,1,0:T(8,128)(2,1)}, u32[]{:S(2)}, u32[]{:S(2)}) collective-permute-start(bf16[2,64,1024]{2,1,0:T(8,128)(2,1)} %get-tuple-element.52), channel_id=1, source_target_pairs={{0,8},{8,16},{16,24},{24,0},{1,9},{9,17},{17,25},{25,1},{2,10},{10... | collective-permute-start | bytes 786440 | tf_op jit(solution)/shard_map/ppermute | solution.py:436
  123.0 29.6 %collective-permute-start.18 = (bf16[2,64,1024]{2,1,0:T(8,128)(2,1)}, bf16[2,64,1024]{2,1,0:T(8,128)(2,1)}, u32[]{:S(2)}, u32[]{:S(2)}) collective-permute-start(bf16[2,64,1024]{2,1,0:T(8,128)(2,1)} %get-tuple-element.53), channel_id=1, source_target_pairs={{0,16},{8,24},{16,0},{24,8},{1,17},{9,25},{17,1},{25,9},{2,18},{10... | collective-permute-start | bytes 786440 | tf_op jit(solution)/shard_map/ppermute | solution.py:436
  130.8 24.7 %collective-permute-start.19 = (bf16[2,64,1024]{2,1,0:T(8,128)(2,1)}, bf16[2,64,1024]{2,1,0:T(8,128)(2,1)}, u32[]{:S(2)}, u32[]{:S(2)}) collective-permute-start(bf16[2,64,1024]{2,1,0:T(8,128)(2,1)} %get-tuple-element.54), channel_id=1, source_target_pairs={{0,24},{8,0},{16,8},{24,16},{1,25},{9,1},{17,9},{25,17},{2,26},{10... | collective-permute-start | bytes 786440 | tf_op jit(solution)/shard_map/ppermute | solution.py:436
  166.4 29.3 %collective-permute-start.20 = (bf16[4,4,4,64,256]{4,3,2,1,0:T(8,128)(2,1)}, bf16[4,4,4,64,256]{4,3,2,1,0:T(8,128)(2,1)}, u32[]{:S(2)}, u32[]{:S(2)}) collective-permute-start(bf16[4,4,4,64,256]{4,3,2,1,0:T(8,128)(2,1)} %get-tuple-element.59), channel_id=1, source_target_pairs={{0,4},{4,0},{1,5},{5,1},{2,6},{6,2},{3,7},{7,3},{8,12},{12,8},{9,1... | collective-permute-start | bytes 6291464 | tf_op jit(solution)/shard_map/ppermute | solution.py:334
  198.8 23.9 %collective-permute-start.21 = (bf16[1024,256]{1,0:T(8,128)(2,1)S(1)}, bf16[1024,256]{1,0:T(8,128)(2,1)S(1)}, u32[]{:S(2)}, u32[]{:S(2)}) collective-permute-start(bf16[1024,256]{1,0:T(8,128)(2,1)S(1)} %bitcast.73), channel_id=1, source_target_pairs={{0,1},{1,2},{2,3},{3,0},{4,5},{5,6},{6,7},{7,4},{8,9},{9,10},{10,1... | collective-permute-start | bytes 1572872 | tf_op jit(solution)/shard_map/ppermute | solution.py:338
  200.8 23.3 %collective-permute-start.22 = (bf16[1024,256]{1,0:T(8,128)(2,1)S(1)}, bf16[1024,256]{1,0:T(8,128)(2,1)S(1)}, u32[]{:S(2)}, u32[]{:S(2)}) collective-permute-start(bf16[1024,256]{1,0:T(8,128)(2,1)S(1)} %bitcast.72), channel_id=1, source_target_pairs={{0,2},{1,3},{2,0},{3,1},{4,6},{5,7},{6,4},{7,5},{8,10},{9,11},{10,... | collective-permute-start | bytes 1572872 | tf_op jit(solution)/shard_map/ppermute | solution.py:338
  200.8 25.7 %collective-permute-start.23 = (bf16[1024,256]{1,0:T(8,128)(2,1)S(1)}, bf16[1024,256]{1,0:T(8,128)(2,1)S(1)}, u32[]{:S(2)}, u32[]{:S(2)}) collective-permute-start(bf16[1024,256]{1,0:T(8,128)(2,1)S(1)} %bitcast.71), channel_id=1, source_target_pairs={{0,3},{1,0},{2,1},{3,2},{4,7},{5,4},{6,5},{7,6},{8,11},{9,8},{10,9... | collective-permute-start | bytes 1572872 | tf_op jit(solution)/shard_map/ppermute | solution.py:338
  239.2 14.8 %collective-permute-start.27 = (bf16[32,4096]{1,0:T(8,128)(2,1)S(1)}, bf16[32,4096]{1,0:T(8,128)(2,1)S(1)}, u32[]{:S(2)}, u32[]{:S(2)}) collective-permute-start(bf16[32,4096]{1,0:T(8,128)(2,1)S(1)} %get-tuple-element.88), channel_id=1, source_target_pairs={{0,24},{8,0},{16,8},{24,16},{1,25},{9,1},{17,9},{25,17},{2,26},{10... | collective-permute-start | bytes 786440 | tf_op jit(solution)/shard_map/ppermute | solution.py:383
  (67 other events, 644.6 us)
Sparse Core Ops, SparseCore 0:
  9.8 138.8 all-gather.1

commit v5 on v4

--- a/solution.py
+++ b/solution.py
@@ -228,10 +228,8 @@
 
     own_images = lax.dynamic_slice_in_dim(image_embeds, x * piece_rows, piece_rows, 1)
     own_images = unit_rows(own_images.astype(F32))[0].astype(BF16)
-    groups = exchange_images(own_images, table, place, (z_size, y_size, c_size))
-
     tile = min(1024, feat_width)
-    text_emb = pl.pallas_call(
+    project = pl.pallas_call(
         project_kernel,
         grid=(feat_width // tile,),
         out_shape=jax.ShapeDtypeStruct((x_size * c_size, rows, emb_width + EXTRA), BF16),
@@ -239,13 +237,21 @@
             pl.BlockSpec((rows, tile), lambda i: (0, i)),
             pl.BlockSpec((tile, emb_width), lambda i: (i, 0)),
         ]
-        + [whole(pl.ANY)],
+        + [whole(pl.ANY)] * (y_size + 1),
         out_specs=pl.BlockSpec((x_size * c_size, rows, emb_width + EXTRA), lambda i: (0, 0, 0)),
         scratch_shapes=[pltpu.VMEM((rows, emb_width), F32)],
         compiler_params=pltpu.CompilerParams(vmem_limit_bytes=60 << 20),
         cost_estimate=pl.CostEstimate(flops=1, bytes_accessed=1, transcendentals=0),
         name="project",
-    )(features, head_weight, groups[0][0])
+    )
+    groups, text_emb = exchange_images(
+        own_images,
+        table,
+        place,
+        (z_size, y_size, c_size),
+        lambda *first: project(features, head_weight, *first),
+    )
+
     texts = lax.all_to_all(text_emb, ("x", "c"), split_axis=0, concat_axis=0, tiled=True)
     texts = texts.reshape(x_size, c_size, rows, emb_width + EXTRA)
 
@@ -310,7 +316,7 @@
                 pltpu.VMEM((turns, piece_rows, emb_width), BF16),
                 pltpu.SemaphoreType.DMA((len(arrays),)),
             ],
-            compiler_params=pltpu.CompilerParams(vmem_limit_bytes=32 << 20),
+            compiler_params=pltpu.CompilerParams(vmem_limit_bytes=60 << 20),
             cost_estimate=pl.CostEstimate(flops=1, bytes_accessed=1, transcendentals=0),
             name="pairs",
         )(
@@ -404,7 +410,7 @@
     return final.T
 
 
-def exchange_images(own_images, table, place, sizes):
+def exchange_images(own_images, table, place, sizes, project):
     z_size, y_size, c_size = sizes
     onward = []
     for z in range(z_size):
@@ -421,6 +427,8 @@
         if keeps:
             outs.append(jax.ShapeDtypeStruct((keeps,) + own_images.shape, BF16))
         before = [groups[step - 1][1], groups[step - 1][-1]] if step in (1, 2) else []
+        if step == 1:
+            text_emb = project(*groups[0], here)
         picked = pl.pallas_call(
             functools.partial(pick_kernel, step=step, sizes=sizes, onward=keeps),
             out_shape=outs,
@@ -435,7 +443,7 @@
         groups.append(
             [picked[0]] + [lax.ppermute(picked[n], "y", shifted(y_size, n)) for n in range(1, y_size)]
         )
-    return groups
+    return groups, text_emb
 
 
 def solution(mesh):

time: 296 us -> 287 us (0.970)
  local copies, waits for them, and re-layouts: 31.5 us -> 14.1 us
  Pallas kernels: 51.6 us -> 58.1 us
  starting transfers between devices: 54 us -> 50.4 us
  blocking collectives: 18 us -> 21.5 us
    unnamed x120 -> x62, local copies, waits for them, and re-layouts: 25.3 us -> 6.07 us
    all_to_all x1, waiting for transfers between devices: 2.21 us -> 16.6 us  [on_device(): lax.all_to_all(text_emb, ('x', 'c'), split_axis=0, concat_axis=0, tiled=T...]
    ppermute x15, waiting for transfers between devices: 54.7 us -> 47.4 us  [exchange_images(): lax.ppermute(picked[n], 'y', shifted(y_size, n))]
    pallas_call x2, Pallas kernels: 22.3 us -> 28.8 us  [pairs(): pl.pallas_call(functools.partial(pair_kernel, starts=starts, own=own), gr...]
    ppermute x4, waiting for transfers between devices: 17.3 us -> 13.2 us  [exchange_images(): lax.ppermute(moving, ('z', 'c'), onward)]
    ppermute x3, waiting for transfers between devices: 3.83 us -> 0.01 us  [on_device(): grads.append(lax.ppermute(total, 'x', shifted(x_size, k)) if k else total)]
    all_to_all x1, blocking collectives: 18 us -> 21.5 us  [on_device(): lax.all_to_all(jnp.concatenate([pair_loss, other_loss], axis=1), DP, spli...]
    ppermute x15, starting transfers between devices: 23.3 us -> 19.9 us  [exchange_images(): lax.ppermute(picked[n], 'y', shifted(y_size, n))]
  transfers between devices with their start and end apart: 34 -> 34, of which waited for: 25 -> 20; matrix products, arithmetic and copies ran while one was open for 6% -> 7% of each run, Pallas kernels for 15% -> 18%
where the time goes in v5:
time: 287 us; the launch traced here: 286 us
  waiting for transfers between devices  111 us (39%)
  Pallas kernels  58.1 us (20%)
  starting transfers between devices  50.4 us (18%)
  blocking collectives  21.5 us (7%)
  between operations  15.9 us (6%)
  other arithmetic  15.2 us (5%)
  local copies, waits for them, and re-layouts  14.1 us (5%)
    ppermute x15, waiting for transfers between devices, exchange_images(): lax.ppermute(picked[n], 'y', shifted(y_size, n))  47.4 us
    pallas_call x2, Pallas kernels, pairs(): pl.pallas_call(functools.partial(pair_kernel, starts=starts, own=own), gr...  28.8 us
    all_to_all x1, blocking collectives, on_device(): lax.all_to_all(jnp.concatenate([pair_loss, other_loss], axis=1), DP, spli...  21.5 us
    ppermute x15, starting transfers between devices, exchange_images(): lax.ppermute(picked[n], 'y', shifted(y_size, n))  19.9 us
    all_to_all x1, waiting for transfers between devices, on_device(): lax.all_to_all(text_emb, ('x', 'c'), split_axis=0, concat_axis=0, tiled=T...  16.6 us
    pallas_call x5, Pallas kernels, exchange_images(): pl.pallas_call(functools.partial(pick_kernel, step=step, sizes=sizes, onw...  13.3 us
    ppermute x4, waiting for transfers between devices, exchange_images(): lax.ppermute(moving, ('z', 'c'), onward)  13.2 us
    ppermute x3, waiting for transfers between devices, add_over_dp(): lax.ppermute(total[k], 'y', shifted(y_size, k))  13.2 us
  transfers between devices with their start and end apart: 34, of which 20 were waited for; matrix products, arithmetic and copies ran while one was open for 7% of the time, Pallas kernels for 18%

profile of v5, /device:TPU:4, one launch (start us, length us, event | category | flops | bytes accessed | tf_op | source)
XLA Modules:
  0.0 286.1 jit_solution(4260654780474496119)
XLA Ops:
  25.9 6.8 %collective-permute-done.1.refs_2_.refs_5_ = bf16[2,64,1024]{2,1,0:T(8,128)(2,1)S(1)} collective-permute-done((bf16[2,64,1024]{2,1,0:T(8,128)(2,1)}, bf16[2,64,1024]{2,1,0:T(8,128)(2,1)S(1)}, u32[]{:S(2)}, u32[]{:S(2)}) %collective-permute-start.1) | collective-permute-done | bytes 262176 | tf_op jit(solution)/shard_map/ppermute | solution.py:444
  34.5 8.7 %project.1 = bf16[8,256,1152]{2,1,0:T(8,128)(2,1)} custom-call(bf16[256,4096]{1,0:T(8,128)(2,1)} %bitcast.61, bf16[4096,1024]{1,0:T(8,128)(2,1)} %weight.1, bf16[2,64,1024]{2,1,0:T(8,128)(2,1)} %get-tuple-element.32.refs_0_.refs_3_, bf16[2,64,1024]{2,1,0:T(8,128)(2,1)} %copy-done.4, bf16[2,64,1024]{2,1,0:T(8,128)(2,1)} %copy-done.6, ...), custom_call_target="tpu_custom_call" | custom-call | flops 1 | bytes 1 | tf_op jit(solution)/shard_map/project/pallas_call | solution.py:252
  43.1 6.5 %all-to-all-start = ((bf16[8,256,1152]{2,1,0:T(8,128)(2,1)}), bf16[8,256,1152]{2,1,0:T(8,128)(2,1)}, u32[]{:S(2)}, u32[]{:S(2)}) async-start(bf16[8,256,1152]{2,1,0:T(8,128)(2,1)} %project.1), calls=%async_computation | async-start | bytes 9437184 | tf_op jit(solution)/shard_map/all_to_all | solution.py:255
  56.9 10.3 %collective-permute-done.5.refs_0_.refs_8_.refs_5_ = bf16[4,64,1024]{2,1,0:T(8,128)(2,1)S(1)} collective-permute-done((bf16[4,64,1024]{2,1,0:T(8,128)(2,1)}, bf16[4,64,1024]{2,1,0:T(8,128)(2,1)S(1)}, u32[]{:S(2)}, u32[]{:S(2)}) %collective-permute-start.5) | collective-permute-done | bytes 524320 | tf_op jit(solution)/shard_map/ppermute | solution.py:444
  81.4 10.2 %collective-permute-done.12.from_ref = bf16[2,4,64,1024]{3,2,1,0:T(8,128)(2,1)S(1)} collective-permute-done((bf16[2,4,64,1024]{3,2,1,0:T(8,128)(2,1)}, bf16[2,4,64,1024]{3,2,1,0:T(8,128)(2,1)S(1)}, u32[]{:S(2)}, u32[]{:S(2)}) %collective-permute-start.12) | collective-permute-done | bytes 1048608 | tf_op jit(solution)/shard_map/ppermute | solution.py:423
  101.8 5.6 %collective-permute-done.9.refs_12_.refs_9_ = bf16[4,64,1024]{2,1,0:T(8,128)(2,1)S(1)} collective-permute-done((bf16[4,64,1024]{2,1,0:T(8,128)(2,1)}, bf16[4,64,1024]{2,1,0:T(8,128)(2,1)S(1)}, u32[]{:S(2)}, u32[]{:S(2)}) %collective-permute-start.9) | collective-permute-done | bytes 524320 | tf_op jit(solution)/shard_map/ppermute | solution.py:444
  114.8 8.3 %collective-permute-done.11.refs_14_.refs_11_ = bf16[4,64,1024]{2,1,0:T(8,128)(2,1)S(1)} collective-permute-done((bf16[4,64,1024]{2,1,0:T(8,128)(2,1)}, bf16[4,64,1024]{2,1,0:T(8,128)(2,1)S(1)}, u32[]{:S(2)}, u32[]{:S(2)}) %collective-permute-start.11) | collective-permute-done | bytes 524320 | tf_op jit(solution)/shard_map/ppermute | solution.py:444
  124.4 5.4 %collective-permute-done.13.refs_16_.refs_13_ = bf16[4,64,1024]{2,1,0:T(8,128)(2,1)S(1)} collective-permute-done((bf16[4,64,1024]{2,1,0:T(8,128)(2,1)}, bf16[4,64,1024]{2,1,0:T(8,128)(2,1)S(1)}, u32[]{:S(2)}, u32[]{:S(2)}) %collective-permute-start.13) | collective-permute-done | bytes 524320 | tf_op jit(solution)/shard_map/ppermute | solution.py:444
  129.8 16.6 %all-to-all-done = bf16[8,256,1152]{2,1,0:T(8,128)(2,1)} async-done(((bf16[8,256,1152]{2,1,0:T(8,128)(2,1)}), bf16[8,256,1152]{2,1,0:T(8,128)(2,1)}, u32[]{:S(2)}, u32[]{:S(2)}) %all-to-all-start) | async-done | bytes 4718624 | tf_op jit(solution)/shard_map/all_to_all | solution.py:255
  146.4 4.9 %constant_dynamic-slice_fusion.3 = (bf16[4,1,256,1152]{3,2,1,0:T(8,128)(2,1)}, bf16[4,1,256,1152]{3,2,1,0:T(8,128)(2,1)}) fusion(bf16[4,2,256,1152]{3,2,1,0:T(8,128)(2,1)} %bitcast.11, s32[]{:T(128)S(6)} %select_n.208, s32[]{:T(128)S(6)} %select_n.204), kind=kLoop, calls=%fused_computation.55 | loop fusion | bytes 9437192 | tf_op jit(solution)/shard_map/jit(dynamic_index_in_dim)/dynamic_slice | solution.py:331
  151.4 5.6 %collective-permute-done.19.refs_22_.refs_19_ = bf16[2,64,1024]{2,1,0:T(8,128)(2,1)} collective-permute-done((bf16[2,64,1024]{2,1,0:T(8,128)(2,1)}, bf16[2,64,1024]{2,1,0:T(8,128)(2,1)}, u32[]{:S(2)}, u32[]{:S(2)}) %collective-permute-start.19) | collective-permute-done | bytes 262176 | tf_op jit(solution)/shard_map/ppermute | solution.py:444
  157.0 12.5 %pairs.3 = (bf16[4,4,4,64,256]{4,3,2,1,0:T(8,128)(2,1)}, f32[64,1,64]{2,1,0:T(1,128)}) custom-call(s32[4,64]{1,0:T(4,128)} %get-tuple-element.67.sources, s32[4,64]{1,0:T(4,128)} %get-tuple-element.66.slots, s32[4]{0:T(128)} %get-tuple-element.72.counts, s32[4]{0:T(128)} %pad_add_fusion.place, f32[2]{0:T(128)} %pad_maximum_fusion.2.scale_bias, ...), custom_call_target="tpu_custom_call" | custom-call | flops 1 | bytes 1 | tf_op jit(solution)/shard_map/pairs/pallas_call | solution.py:297
  171.3 16.3 %pairs.2 = (bf16[4,4,4,64,256]{4,3,2,1,0:T(8,128)(2,1)}, f32[64,1,64]{2,1,0:T(1,128)}, f32[4,1,64]{2,1,0:T(1,128)}) custom-call(s32[4,64]{1,0:T(4,128)} %get-tuple-element.70.sources, s32[4,64]{1,0:T(4,128)} %get-tuple-element.71.slots, s32[4]{0:T(128)} %get-tuple-element.94.counts, s32[4]{0:T(128)} %pad_add_fusion.place, f32[2]{0:T(128)} %pad_maximum_fusion.2.scale_bias, ...), custom_call_target="tpu_custom_call" | custom-call | flops 1 | bytes 1 | tf_op jit(solution)/shard_map/pairs/pallas_call | solution.py:297
  187.6 3.3 %add_convert_fusion.1 = (bf16[1,4,4,64,256]{4,3,2,1,0:T(8,128)(2,1)S(1)}, bf16[1,4,4,64,256]{4,3,2,1,0:T(8,128)(2,1)S(1)}, bf16[1,4,4,64,256]{4,3,2,1,0:T(8,128)(2,1)}, bf16[1,4,4,64,256]{4,3,2,1,0:T(8,128)(2,1)}) fusion(bf16[4,4,4,64,256]{4,3,2,1,0:T(8,128)(2,1)S(1)} %collective-permute-done.20, bf16[4,4,4,64,256]{4,3,2,1,0:T(8,128)(2,1)} %get-tuple-element.58), kind=kLoop, calls=%fused_computation.6 | loop fusion | flops 4194304 | bytes 6291456 | tf_op jit(solution)/shard_map/convert_element_type | solution.py:343
  193.9 21.5 %all_to_all.10 = f32[64,1,128]{2,1,0:T(1,128)S(1)} all-to-all(f32[64,1,128]{2,1,0:T(1,128)S(1)} %reshape.243), channel_id=1, replica_groups=mesh['z'=8,'y'=4,'c'=2,'x'=4] {'z','y','c'}, dimensions={0} | all-to-all | bytes 65536 | tf_op jit(solution)/shard_map/all_to_all | solution.py:336
  218.5 7.4 %head.1 = (bf16[128,4096]{1,0:T(8,128)(2,1)}, bf16[128,4096]{1,0:T(8,128)(2,1)}) custom-call(s32[4]{0:T(128)} %pad_add_fusion.place, bf16[1024,256]{1,0:T(8,128)(2,1)} %bitcast.63, bf16[1024,256]{1,0:T(8,128)(2,1)} %copy-done.19, bf16[1024,256]{1,0:T(8,128)(2,1)} %copy-done.20, bf16[1024,256]{1,0:T(8,128)(2,1)} %copy-done.21, bf16[1024,4096]{1,0:T(8,128)(2,1)} %bitcast.62, ...), custom_call_target="tpu_custom_call" | custom-call | flops 2147483648 | bytes 16777216 | tf_op jit(solution)/shard_map/head/pallas_call | solution.py:347
  234.4 9.5 %collective-permute-done.27 = bf16[32,4096]{1,0:T(8,128)(2,1)S(1)} collective-permute-done((bf16[32,4096]{1,0:T(8,128)(2,1)S(1)}, bf16[32,4096]{1,0:T(8,128)(2,1)S(1)}, u32[]{:S(2)}, u32[]{:S(2)}) %collective-permute-start.27) | collective-permute-done | bytes 262176 | tf_op jit(solution)/shard_map/ppermute | solution.py:389
  243.9 3.7 %collective-permute-done.25 = bf16[32,4096]{1,0:T(8,128)(2,1)S(1)} collective-permute-done((bf16[32,4096]{1,0:T(8,128)(2,1)S(1)}, bf16[32,4096]{1,0:T(8,128)(2,1)S(1)}, u32[]{:S(2)}, u32[]{:S(2)}) %collective-permute-start.25) | collective-permute-done | bytes 262176 | tf_op jit(solution)/shard_map/ppermute | solution.py:389
  248.3 5.0 %collective-permute-done.28 = bf16[16,4096]{1,0:T(8,128)(2,1)S(1)} collective-permute-done((bf16[16,4096]{1,0:T(8,128)(2,1)S(1)}, bf16[16,4096]{1,0:T(8,128)(2,1)S(1)}, u32[]{:S(2)}, u32[]{:S(2)}) %collective-permute-start.28) | collective-permute-done | bytes 131104 | tf_op jit(solution)/shard_map/ppermute | solution.py:394
  253.7 3.4 %collective-permute-start.29 = (bf16[16,2048]{1,0:T(8,128)(2,1)S(1)}, bf16[16,2048]{1,0:T(8,128)(2,1)S(1)}, u32[]{:S(2)}, u32[]{:S(2)}) collective-permute-start(bf16[16,2048]{1,0:T(8,128)(2,1)S(1)} %bitcast.74), channel_id=1, source_target_pairs={{0,128},{32,160},{64,192},{96,224},{128,0},{160,32},{192,64},{224,... | collective-permute-start | bytes 196616 | tf_op jit(solution)/shard_map/ppermute | solution.py:398
  257.2 5.5 %collective-permute-done.29 = bf16[16,2048]{1,0:T(8,128)(2,1)S(1)} collective-permute-done((bf16[16,2048]{1,0:T(8,128)(2,1)S(1)}, bf16[16,2048]{1,0:T(8,128)(2,1)S(1)}, u32[]{:S(2)}, u32[]{:S(2)}) %collective-permute-start.29) | collective-permute-done | bytes 65568 | tf_op jit(solution)/shard_map/ppermute | solution.py:398
  262.9 3.5 %collective-permute-start.31 = (bf16[16,1024]{1,0:T(8,128)(2,1)S(1)}, bf16[16,1024]{1,0:T(8,128)(2,1)S(1)}, u32[]{:S(2)}, u32[]{:S(2)}) collective-permute-start(bf16[16,1024]{1,0:T(8,128)(2,1)S(1)} %bitcast.75), channel_id=1, source_target_pairs={{0,1},{1,65},{2,129},{3,193},{32,33},{33,97},{34,161},{35,225},{64... | collective-permute-start | bytes 98312 | tf_op jit(solution)/shard_map/ppermute | solution.py:409
  266.5 5.8 %collective-permute-start.30 = (bf16[16,1024]{1,0:T(8,128)(2,1)S(1)}, bf16[16,1024]{1,0:T(8,128)(2,1)S(1)}, u32[]{:S(2)}, u32[]{:S(2)}) collective-permute-start(bf16[16,1024]{1,0:T(8,128)(2,1)S(1)} %bitcast.76), channel_id=1, source_target_pairs={{0,0},{1,64},{2,128},{3,192},{32,32},{33,96},{34,160},{35,224},{64... | collective-permute-start | bytes 98312 | tf_op jit(solution)/shard_map/ppermute | solution.py:409
  272.9 5.7 %collective-permute-done.30 = bf16[16,1024]{1,0:T(8,128)(2,1)S(1)} collective-permute-done((bf16[16,1024]{1,0:T(8,128)(2,1)S(1)}, bf16[16,1024]{1,0:T(8,128)(2,1)S(1)}, u32[]{:S(2)}, u32[]{:S(2)}) %collective-permute-start.30) | collective-permute-done | bytes 32800 | tf_op jit(solution)/shard_map/ppermute | solution.py:409
  (172 shorter events, 78.3 us)
Async XLA Ops:
  7.2 210.2 %all-gather.2.cloned.1.call-start = ((), (), s32[]{:S(2)}) async-start(), calls=%async_computation.2 | async-start | bytes 10485760 | tf_op jit(solution)/shard_map/all_gather | solution.py:220
  11.2 22.2 %collective-permute-start.4 = (bf16[2,4,64,1024]{3,2,1,0:T(8,128)(2,1)S(1)}, bf16[2,4,64,1024]{3,2,1,0:T(8,128)(2,1)S(1)}, u32[]{:S(2)}, u32[]{:S(2)}) collective-permute-start(bf16[2,4,64,1024]{3,2,1,0:T(8,128)(2,1)S(1)} %pad_maximum_fusion), channel_id=1, source_target_pairs={{0,32},{4,228},{32,64},{36,4},{64,96},{68,36},{96,128},{100,68},{1... | collective-permute-start | bytes 3145736 | tf_op jit(solution)/shard_map/ppermute | solution.py:423
  19.7 13.0 %collective-permute-start.1 = (bf16[2,64,1024]{2,1,0:T(8,128)(2,1)}, bf16[2,64,1024]{2,1,0:T(8,128)(2,1)S(1)}, u32[]{:S(2)}, u32[]{:S(2)}) collective-permute-start(bf16[2,64,1024]{2,1,0:T(8,128)(2,1)} %get-tuple-element.34), channel_id=1, source_target_pairs={{0,16},{8,24},{16,0},{24,8},{1,17},{9,25},{17,1},{25,9},{2,18},{10... | collective-permute-start | bytes 786440 | tf_op jit(solution)/shard_map/ppermute | solution.py:444
  43.1 103.3 %all-to-all-start = ((bf16[8,256,1152]{2,1,0:T(8,128)(2,1)}), bf16[8,256,1152]{2,1,0:T(8,128)(2,1)}, u32[]{:S(2)}, u32[]{:S(2)}) async-start(bf16[8,256,1152]{2,1,0:T(8,128)(2,1)} %project.1), calls=%async_computation | async-start | bytes 9437184 | tf_op jit(solution)/shard_map/all_to_all | solution.py:255
  52.7 17.7 %collective-permute-start.8 = (bf16[2,4,64,1024]{3,2,1,0:T(8,128)(2,1)}, bf16[2,4,64,1024]{3,2,1,0:T(8,128)(2,1)S(1)}, u32[]{:S(2)}, u32[]{:S(2)}) collective-permute-start(bf16[2,4,64,1024]{3,2,1,0:T(8,128)(2,1)} %get-tuple-element.40), channel_id=1, source_target_pairs={{0,32},{4,228},{32,64},{36,4},{64,96},{68,36},{96,128},{100,68},{1... | collective-permute-start | bytes 3145736 | tf_op jit(solution)/shard_map/ppermute | solution.py:423
  53.7 13.5 %collective-permute-start.5 = (bf16[4,64,1024]{2,1,0:T(8,128)(2,1)}, bf16[4,64,1024]{2,1,0:T(8,128)(2,1)S(1)}, u32[]{:S(2)}, u32[]{:S(2)}) collective-permute-start(bf16[4,64,1024]{2,1,0:T(8,128)(2,1)} %get-tuple-element.37), channel_id=1, source_target_pairs={{0,8},{8,16},{16,24},{24,0},{1,9},{9,17},{17,25},{25,1},{2,10},{10... | collective-permute-start | bytes 1572872 | tf_op jit(solution)/shard_map/ppermute | solution.py:444
  74.5 17.2 %collective-permute-start.12 = (bf16[2,4,64,1024]{3,2,1,0:T(8,128)(2,1)}, bf16[2,4,64,1024]{3,2,1,0:T(8,128)(2,1)S(1)}, u32[]{:S(2)}, u32[]{:S(2)}) collective-permute-start(bf16[2,4,64,1024]{3,2,1,0:T(8,128)(2,1)} %get-tuple-element.45), channel_id=1, source_target_pairs={{0,32},{4,228},{32,64},{36,4},{64,96},{68,36},{96,128},{100,68},{1... | collective-permute-start | bytes 3145736 | tf_op jit(solution)/shard_map/ppermute | solution.py:423
  77.9 21.5 %collective-permute-start.6 = (bf16[4,64,1024]{2,1,0:T(8,128)(2,1)S(1)}, bf16[4,64,1024]{2,1,0:T(8,128)(2,1)S(1)}, u32[]{:S(2)}, u32[]{:S(2)}) collective-permute-start(bf16[4,64,1024]{2,1,0:T(8,128)(2,1)S(1)} %copy-done.27), channel_id=1, source_target_pairs={{0,16},{8,24},{16,0},{24,8},{1,17},{9,25},{17,1},{25,9},{2,18},{10... | collective-permute-start | bytes 1572872 | tf_op jit(solution)/shard_map/ppermute | solution.py:444
  79.9 27.5 %collective-permute-start.9 = (bf16[4,64,1024]{2,1,0:T(8,128)(2,1)}, bf16[4,64,1024]{2,1,0:T(8,128)(2,1)S(1)}, u32[]{:S(2)}, u32[]{:S(2)}) collective-permute-start(bf16[4,64,1024]{2,1,0:T(8,128)(2,1)} %get-tuple-element.42), channel_id=1, source_target_pairs={{0,8},{8,16},{16,24},{24,0},{1,9},{9,17},{17,25},{25,1},{2,10},{10... | collective-permute-start | bytes 1572872 | tf_op jit(solution)/shard_map/ppermute | solution.py:444
  95.6 13.6 %collective-permute-start.16 = (bf16[1,4,64,1024]{3,2,1,0:T(8,128)(2,1)}, bf16[1,4,64,1024]{3,2,1,0:T(8,128)(2,1)}, u32[]{:S(2)}, u32[]{:S(2)}) collective-permute-start(bf16[1,4,64,1024]{3,2,1,0:T(8,128)(2,1)} %get-tuple-element.50), channel_id=1, source_target_pairs={{0,32},{4,228},{32,64},{36,4},{64,96},{68,36},{96,128},{100,68},{1... | collective-permute-start | bytes 1572872 | tf_op jit(solution)/shard_map/ppermute | solution.py:423
  95.9 18.9 %collective-permute-start.10 = (bf16[4,64,1024]{2,1,0:T(8,128)(2,1)}, bf16[4,64,1024]{2,1,0:T(8,128)(2,1)S(1)}, u32[]{:S(2)}, u32[]{:S(2)}) collective-permute-start(bf16[4,64,1024]{2,1,0:T(8,128)(2,1)} %get-tuple-element.43), channel_id=1, source_target_pairs={{0,16},{8,24},{16,0},{24,8},{1,17},{9,25},{17,1},{25,9},{2,18},{10... | collective-permute-start | bytes 1572872 | tf_op jit(solution)/shard_map/ppermute | solution.py:444
  97.9 25.3 %collective-permute-start.11 = (bf16[4,64,1024]{2,1,0:T(8,128)(2,1)}, bf16[4,64,1024]{2,1,0:T(8,128)(2,1)S(1)}, u32[]{:S(2)}, u32[]{:S(2)}) collective-permute-start(bf16[4,64,1024]{2,1,0:T(8,128)(2,1)} %get-tuple-element.44), channel_id=1, source_target_pairs={{0,24},{8,0},{16,8},{24,16},{1,25},{9,1},{17,9},{25,17},{2,26},{10... | collective-permute-start | bytes 1572872 | tf_op jit(solution)/shard_map/ppermute | solution.py:444
  99.4 30.4 %collective-permute-start.13 = (bf16[4,64,1024]{2,1,0:T(8,128)(2,1)}, bf16[4,64,1024]{2,1,0:T(8,128)(2,1)S(1)}, u32[]{:S(2)}, u32[]{:S(2)}) collective-permute-start(bf16[4,64,1024]{2,1,0:T(8,128)(2,1)} %get-tuple-element.47), channel_id=1, source_target_pairs={{0,8},{8,16},{16,24},{24,0},{1,9},{9,17},{17,25},{25,1},{2,10},{10... | collective-permute-start | bytes 1572872 | tf_op jit(solution)/shard_map/ppermute | solution.py:444
  107.4 43.9 %collective-permute-start.14 = (bf16[4,64,1024]{2,1,0:T(8,128)(2,1)}, bf16[4,64,1024]{2,1,0:T(8,128)(2,1)S(1)}, u32[]{:S(2)}, u32[]{:S(2)}) collective-permute-start(bf16[4,64,1024]{2,1,0:T(8,128)(2,1)} %get-tuple-element.48), channel_id=1, source_target_pairs={{0,16},{8,24},{16,0},{24,8},{1,17},{9,25},{17,1},{25,9},{2,18},{10... | collective-permute-start | bytes 1572872 | tf_op jit(solution)/shard_map/ppermute | solution.py:444
  109.2 42.2 %collective-permute-start.15 = (bf16[4,64,1024]{2,1,0:T(8,128)(2,1)}, bf16[4,64,1024]{2,1,0:T(8,128)(2,1)}, u32[]{:S(2)}, u32[]{:S(2)}) collective-permute-start(bf16[4,64,1024]{2,1,0:T(8,128)(2,1)} %get-tuple-element.49), channel_id=1, source_target_pairs={{0,24},{8,0},{16,8},{24,16},{1,25},{9,1},{17,9},{25,17},{2,26},{10... | collective-permute-start | bytes 1572872 | tf_op jit(solution)/shard_map/ppermute | solution.py:444
  114.8 36.5 %collective-permute-start.17 = (bf16[2,64,1024]{2,1,0:T(8,128)(2,1)}, bf16[2,64,1024]{2,1,0:T(8,128)(2,1)S(1)}, u32[]{:S(2)}, u32[]{:S(2)}) collective-permute-start(bf16[2,64,1024]{2,1,0:T(8,128)(2,1)} %get-tuple-element.52), channel_id=1, source_target_pairs={{0,8},{8,16},{16,24},{24,0},{1,9},{9,17},{17,25},{25,1},{2,10},{10... | collective-permute-start | bytes 786440 | tf_op jit(solution)/shard_map/ppermute | solution.py:444
  123.1 28.3 %collective-permute-start.18 = (bf16[2,64,1024]{2,1,0:T(8,128)(2,1)}, bf16[2,64,1024]{2,1,0:T(8,128)(2,1)}, u32[]{:S(2)}, u32[]{:S(2)}) collective-permute-start(bf16[2,64,1024]{2,1,0:T(8,128)(2,1)} %get-tuple-element.53), channel_id=1, source_target_pairs={{0,16},{8,24},{16,0},{24,8},{1,17},{9,25},{17,1},{25,9},{2,18},{10... | collective-permute-start | bytes 786440 | tf_op jit(solution)/shard_map/ppermute | solution.py:444
  129.8 27.1 %collective-permute-start.19 = (bf16[2,64,1024]{2,1,0:T(8,128)(2,1)}, bf16[2,64,1024]{2,1,0:T(8,128)(2,1)}, u32[]{:S(2)}, u32[]{:S(2)}) collective-permute-start(bf16[2,64,1024]{2,1,0:T(8,128)(2,1)} %get-tuple-element.54), channel_id=1, source_target_pairs={{0,24},{8,0},{16,8},{24,16},{1,25},{9,1},{17,9},{25,17},{2,26},{10... | collective-permute-start | bytes 786440 | tf_op jit(solution)/shard_map/ppermute | solution.py:444
  169.5 18.1 %collective-permute-start.20 = (bf16[4,4,4,64,256]{4,3,2,1,0:T(8,128)(2,1)}, bf16[4,4,4,64,256]{4,3,2,1,0:T(8,128)(2,1)S(1)}, u32[]{:S(2)}, u32[]{:S(2)}) collective-permute-start(bf16[4,4,4,64,256]{4,3,2,1,0:T(8,128)(2,1)} %get-tuple-element.59), channel_id=1, source_target_pairs={{0,4},{4,0},{1,5},{5,1},{2,6},{6,2},{3,7},{7,3},{8,12},{12,8},{9,1... | collective-permute-start | bytes 6291464 | tf_op jit(solution)/shard_map/ppermute | solution.py:340
  190.9 26.5 %collective-permute-start.21 = (bf16[1024,256]{1,0:T(8,128)(2,1)}, bf16[1024,256]{1,0:T(8,128)(2,1)S(1)}, u32[]{:S(2)}, u32[]{:S(2)}) collective-permute-start(bf16[1024,256]{1,0:T(8,128)(2,1)} %bitcast.23), channel_id=1, source_target_pairs={{0,1},{1,2},{2,3},{3,0},{4,5},{5,6},{6,7},{7,4},{8,9},{9,10},{10,1... | collective-permute-start | bytes 1572872 | tf_op jit(solution)/shard_map/ppermute | solution.py:344
  191.9 25.4 %collective-permute-start.22 = (bf16[1024,256]{1,0:T(8,128)(2,1)S(1)}, bf16[1024,256]{1,0:T(8,128)(2,1)S(1)}, u32[]{:S(2)}, u32[]{:S(2)}) collective-permute-start(bf16[1024,256]{1,0:T(8,128)(2,1)S(1)} %bitcast.70), channel_id=1, source_target_pairs={{0,2},{1,3},{2,0},{3,1},{4,6},{5,7},{6,4},{7,5},{8,10},{9,11},{10,... | collective-permute-start | bytes 1572872 | tf_op jit(solution)/shard_map/ppermute | solution.py:344
  192.9 24.5 %collective-permute-start.23 = (bf16[1024,256]{1,0:T(8,128)(2,1)S(1)}, bf16[1024,256]{1,0:T(8,128)(2,1)S(1)}, u32[]{:S(2)}, u32[]{:S(2)}) collective-permute-start(bf16[1024,256]{1,0:T(8,128)(2,1)S(1)} %bitcast.69), channel_id=1, source_target_pairs={{0,3},{1,0},{2,1},{3,2},{4,7},{5,4},{6,5},{7,6},{8,11},{9,8},{10,9... | collective-permute-start | bytes 1572872 | tf_op jit(solution)/shard_map/ppermute | solution.py:344
  230.4 13.6 %collective-permute-start.27 = (bf16[32,4096]{1,0:T(8,128)(2,1)S(1)}, bf16[32,4096]{1,0:T(8,128)(2,1)S(1)}, u32[]{:S(2)}, u32[]{:S(2)}) collective-permute-start(bf16[32,4096]{1,0:T(8,128)(2,1)S(1)} %get-tuple-element.88), channel_id=1, source_target_pairs={{0,24},{8,0},{16,8},{24,16},{1,25},{9,1},{17,9},{25,17},{2,26},{10... | collective-permute-start | bytes 786440 | tf_op jit(solution)/shard_map/ppermute | solution.py:389
  233.3 14.4 %collective-permute-start.25 = (bf16[32,4096]{1,0:T(8,128)(2,1)S(1)}, bf16[32,4096]{1,0:T(8,128)(2,1)S(1)}, u32[]{:S(2)}, u32[]{:S(2)}) collective-permute-start(bf16[32,4096]{1,0:T(8,128)(2,1)S(1)} %get-tuple-element.87), channel_id=1, source_target_pairs={{0,8},{8,16},{16,24},{24,0},{1,9},{9,17},{17,25},{25,1},{2,10},{10... | collective-permute-start | bytes 786440 | tf_op jit(solution)/shard_map/ppermute | solution.py:389
  (38 other events, 410.4 us)
Sparse Core Ops, SparseCore 0:
  9.8 136.9 all-gather.1

commit v6 on v5

--- a/solution.py
+++ b/solution.py
@@ -148,17 +148,19 @@
             chunks[k, j, 0] = values[j * piece_rows : (j + 1) * piece_rows]
 
 
-def pick_kernel(table, place, from_ref, *refs, step, sizes, onward):
+def pick_kernel(table, place, from_ref, *refs, step, sizes, onward, carries):
     z_size, y_size, c_size = sizes
     sems = refs[-1]
-    outs = y_size + (onward > 0)
+    outs = y_size + (onward > 0) + carries
     to_refs = refs[-1 - outs : -1]
     count = from_ref.shape[0]
     back = jnp.where(place[2] == 0, step, z_size - step)
     z = lax.rem(place[3] - back + z_size, z_size)
     copies = []
     if onward:
-        copies.append(pltpu.make_async_copy(from_ref.at[pl.ds(0, onward)], to_refs[-1], sems.at[0]))
+        copies.append(pltpu.make_async_copy(from_ref.at[pl.ds(0, onward)], to_refs[y_size], sems.at[0]))
+    if carries:
+        copies.append(pltpu.make_async_copy(refs[0], to_refs[-1], sems.at[1]))
     for dy in range(y_size):
         y = lax.rem(place[1] + dy, y_size)
         for to in range(c_size):
@@ -166,7 +168,7 @@
                 source = z * c_size + lax.rem(place[2] + j, c_size)
                 block = table[source, y * c_size + lax.rem(place[2] + to, c_size)]
                 n = to * count + j
-                sem = sems.at[1 + dy * c_size * count + n]
+                sem = sems.at[2 + dy * c_size * count + n]
                 copies.append(pltpu.make_async_copy(from_ref.at[j, block], to_refs[dy].at[n], sem))
     for copy in copies:
         copy.start()
@@ -217,7 +219,6 @@
     peer_iota = jnp.arange(dp_count, dtype=jnp.int32)
     place = jnp.stack([x, y, c, z]).astype(jnp.int32)
     features = text_features.reshape(rows, feat_width)
-    feats = lax.all_gather(features, "x", axis=0, tiled=False)
 
     owners = jnp.where(hard_lists >= 0, hard_lists // blocks, -1).reshape(dp_count, blocks, -1)
     line = owners.reshape(z_size, y_size, c_size, blocks, -1)
@@ -232,28 +233,27 @@
     project = pl.pallas_call(
         project_kernel,
         grid=(feat_width // tile,),
-        out_shape=jax.ShapeDtypeStruct((x_size * c_size, rows, emb_width + EXTRA), BF16),
+        out_shape=jax.ShapeDtypeStruct((x_size, rows, emb_width + EXTRA), BF16),
         in_specs=[
             pl.BlockSpec((rows, tile), lambda i: (0, i)),
             pl.BlockSpec((tile, emb_width), lambda i: (i, 0)),
         ]
-        + [whole(pl.ANY)] * (y_size + 1),
-        out_specs=pl.BlockSpec((x_size * c_size, rows, emb_width + EXTRA), lambda i: (0, 0, 0)),
+        + [whole(pl.ANY)] * 2,
+        out_specs=pl.BlockSpec((x_size, rows, emb_width + EXTRA), lambda i: (0, 0, 0)),
         scratch_shapes=[pltpu.VMEM((rows, emb_width), F32)],
         compiler_params=pltpu.CompilerParams(vmem_limit_bytes=60 << 20),
         cost_estimate=pl.CostEstimate(flops=1, bytes_accessed=1, transcendentals=0),
         name="project",
     )
-    groups, text_emb = exchange_images(
+    groups, texts, sent_features = exchange_images(
         own_images,
         table,
         place,
         (z_size, y_size, c_size),
         lambda *first: project(features, head_weight, *first),
+        features,
     )
-
-    texts = lax.all_to_all(text_emb, ("x", "c"), split_axis=0, concat_axis=0, tiled=True)
-    texts = texts.reshape(x_size, c_size, rows, emb_width + EXTRA)
+    feats = lax.all_gather(sent_features, "x", axis=0, tiled=False)
 
     arrays, starts, slot_base, turns = [], [], [], 0
     for group in groups:
@@ -328,10 +328,9 @@
             *arrays,
         )
 
-    other_texts = lax.dynamic_index_in_dim(texts, 1 - c, 1, keepdims=False)
+    other_texts = lax.ppermute(texts, "c", shifted(c_size, 1))
     other_chunks, other_loss = pairs(dp_index + 1 - 2 * c, other_texts, False)
-    own_texts = lax.dynamic_index_in_dim(texts, c, 1, keepdims=False)
-    chunks, pair_loss, own_loss = pairs(dp_index, own_texts, True)
+    chunks, pair_loss, own_loss = pairs(dp_index, texts, True)
 
     returned = lax.all_to_all(
         jnp.concatenate([pair_loss, other_loss], axis=1), DP, split_axis=0, concat_axis=0, tiled=True
@@ -410,7 +409,7 @@
     return final.T
 
 
-def exchange_images(own_images, table, place, sizes, project):
+def exchange_images(own_images, table, place, sizes, project, features):
     z_size, y_size, c_size = sizes
     onward = []
     for z in range(z_size):
@@ -426,24 +425,38 @@
         outs = [jax.ShapeDtypeStruct(shape, BF16)] * y_size
         if keeps:
             outs.append(jax.ShapeDtypeStruct((keeps,) + own_images.shape, BF16))
-        before = [groups[step - 1][1], groups[step - 1][-1]] if step in (1, 2) else []
+        before = [groups[step - 1][1], groups[step - 1][-1]] if step else []
+        if step == last - 1:
+            before.append(groups[0][y_size // 2])
+        if step == last:
+            before += [groups[k][y_size // 2] for k in range(1, last - 1)]
         if step == 1:
-            text_emb = project(*groups[0], here)
+            text_emb = project(here, picked[0])
+            texts = lax.all_to_all(text_emb, "x", split_axis=0, concat_axis=0, tiled=True)
+        elif step == 2:
+            before.append(text_emb)
+        carried = [features] if step == 2 else [texts] if step == last else []
+        if carried:
+            outs.append(jax.ShapeDtypeStruct(carried[0].shape, carried[0].dtype))
         picked = pl.pallas_call(
-            functools.partial(pick_kernel, step=step, sizes=sizes, onward=keeps),
+            functools.partial(pick_kernel, step=step, sizes=sizes, onward=keeps, carries=len(carried)),
             out_shape=outs,
-            in_specs=[whole(pltpu.SMEM)] * 2 + [whole()] + [whole(pl.ANY)] * len(before),
+            in_specs=[whole(pltpu.SMEM)] * 2 + [whole()] * (1 + len(carried)) + [whole(pl.ANY)] * len(before),
             out_specs=[whole(pl.ANY)] * len(outs),
-            scratch_shapes=[pltpu.SemaphoreType.DMA((1 + y_size * shape[0],))],
+            scratch_shapes=[pltpu.SemaphoreType.DMA((2 + y_size * shape[0],))],
             cost_estimate=pl.CostEstimate(flops=1, bytes_accessed=1, transcendentals=0),
             name="pick",
-        )(table, place, here, *before)
+        )(table, place, here, *carried, *before)
         if keeps:
-            moving = picked[-1]
+            moving = picked[y_size]
+        if step == 2:
+            features = picked[-1]
+        if step == last:
+            texts = picked[-1]
         groups.append(
             [picked[0]] + [lax.ppermute(picked[n], "y", shifted(y_size, n)) for n in range(1, y_size)]
         )
-    return groups, text_emb
+    return groups, texts, features
 
 
 def solution(mesh):

time: 287 us -> 291 us (1.014)
  starting transfers between devices: 50.4 us -> 58.6 us
  other arithmetic: 15.2 us -> 19.5 us
    ppermute x15, waiting for transfers between devices: 47.4 us -> 66.8 us  [exchange_images(): lax.ppermute(picked[n], 'y', shifted(y_size, n))]
    all_to_all x1, waiting for transfers between devices: 16.6 us -> 0.01 us  [exchange_images(): lax.all_to_all(text_emb, 'x', split_axis=0, concat_axis=0, tiled=True)]
    pallas_call x2, Pallas kernels: 28.8 us -> 23.6 us  [pairs(): pl.pallas_call(functools.partial(pair_kernel, starts=starts, own=own), gr...]
    dynamic_slice x1 -> x0, local copies, waits for them, and re-layouts: 4.89 us -> none  [on_device(): other_texts = lax.dynamic_index_in_dim(texts, 1 - c, 1, keepdims=False)]
    ppermute x15, starting transfers between devices: 19.9 us -> 24.5 us  [exchange_images(): lax.ppermute(picked[n], 'y', shifted(y_size, n))]
    ppermute x2, waiting for transfers between devices: 5.74 us -> 1.92 us  [add_over_dp(): final = final + lax.ppermute(chunk, ('z', 'x'), pairs).astype(F32)]
    ppermute x1, starting transfers between devices: 3.39 us -> 0.09 us  [add_over_dp(): lax.ppermute(given, 'z', [(i, (i + z_size // 2) % z_size) for i in range(...]
    pallas_call x5, Pallas kernels: 13.3 us -> 16.5 us  [exchange_images(): pl.pallas_call(functools.partial(pick_kernel, step=step, sizes=sizes, onw...]
  transfers between devices with their start and end apart: 34 -> 35, of which waited for: 20 -> 22; matrix products, arithmetic and copies ran while one was open for 7% -> 7% of each run, Pallas kernels for 18% -> 14%
where the time goes in v6:
time: 291 us; the launch traced here: 289 us
  waiting for transfers between devices  110 us (38%)
  starting transfers between devices  58.6 us (20%)
  Pallas kernels  55.2 us (19%)
  other arithmetic  19.5 us (7%)
  blocking collectives  18.6 us (6%)
  between operations  15.9 us (5%)
  local copies, waits for them, and re-layouts  11.6 us (4%)
    ppermute x15, waiting for transfers between devices, exchange_images(): lax.ppermute(picked[n], 'y', shifted(y_size, n))  66.8 us
    ppermute x15, starting transfers between devices, exchange_images(): lax.ppermute(picked[n], 'y', shifted(y_size, n))  24.5 us
    pallas_call x2, Pallas kernels, pairs(): pl.pallas_call(functools.partial(pair_kernel, starts=starts, own=own), gr...  23.6 us
    all_to_all x1, blocking collectives, on_device(): lax.all_to_all(jnp.concatenate([pair_loss, other_loss], axis=1), DP, spli...  18.6 us
    pallas_call x5, Pallas kernels, exchange_images(): pl.pallas_call(functools.partial(pick_kernel, step=step, sizes=sizes, onw...  16.5 us
    ppermute x4, waiting for transfers between devices, exchange_images(): lax.ppermute(moving, ('z', 'c'), onward)  13.5 us
    ppermute x3, waiting for transfers between devices, add_over_dp(): lax.ppermute(total[k], 'y', shifted(y_size, k))  11.4 us
    ppermute x2, starting transfers between devices, add_over_dp(): final = final + lax.ppermute(chunk, ('z', 'x'), pairs).astype(F32)  9.68 us
  transfers between devices with their start and end apart: 35, of which 22 were waited for; matrix products, arithmetic and copies ran while one was open for 7% of the time, Pallas kernels for 14%

profile of v6, /device:TPU:4, one launch (start us, length us, event | category | flops | bytes accessed | tf_op | source)
XLA Modules:
  0.0 289.2 jit_solution(1813677376388756659)
XLA Ops:
  23.5 4.6 %collective-permute-done.2.refs_0_.refs_4_.refs_1_ = bf16[2,64,1024]{2,1,0:T(8,128)(2,1)S(1)} collective-permute-done((bf16[2,64,1024]{2,1,0:T(8,128)(2,1)}, bf16[2,64,1024]{2,1,0:T(8,128)(2,1)S(1)}, u32[]{:S(2)}, u32[]{:S(2)}) %collective-permute-start.2) | collective-permute-done | bytes 262176 | tf_op jit(solution)/shard_map/ppermute | solution.py:457
  38.7 7.7 %project.1.refs_3_ = bf16[4,256,1152]{2,1,0:T(8,128)(2,1)} custom-call(bf16[256,4096]{1,0:T(8,128)(2,1)} %bitcast.51, bf16[4096,1024]{1,0:T(8,128)(2,1)} %weight.1, bf16[2,4,64,1024]{3,2,1,0:T(8,128)(2,1)} %copy-done.6, bf16[2,64,1024]{2,1,0:T(8,128)(2,1)} %get-tuple-element.39.refs_1_.refs_3_.refs_0_), custom_call_target="tpu_custom_call" | custom-call | flops 1 | bytes 1 | tf_op jit(solution)/shard_map/project/pallas_call | solution.py:253
  48.8 4.2 %collective-permute-done.4.from_ref = bf16[2,4,64,1024]{3,2,1,0:T(8,128)(2,1)S(1)} collective-permute-done((bf16[2,4,64,1024]{3,2,1,0:T(8,128)(2,1)}, bf16[2,4,64,1024]{3,2,1,0:T(8,128)(2,1)S(1)}, u32[]{:S(2)}, u32[]{:S(2)}) %collective-permute-start.4) | collective-permute-done | bytes 1048608 | tf_op jit(solution)/shard_map/ppermute | solution.py:422
  54.0 4.6 %pick.7 = (bf16[4,64,1024]{2,1,0:T(8,128)(2,1)}, bf16[4,64,1024]{2,1,0:T(8,128)(2,1)}, bf16[4,64,1024]{2,1,0:T(8,128)(2,1)}, bf16[4,64,1024]{2,1,0:T(8,128)(2,1)...) custom-call(s32[16,8]{1,0:T(8,128)} %select_reduce_fusion.7.table, s32[4]{0:T(128)} %pad_add_fusion.place, ...), custom_call_target="tpu_custom_call" | custom-call | flops 1 | bytes 1 | tf_op jit(solution)/shard_map/pick/pallas_call | solution.py:441
  58.6 4.9 %all-to-all-start = ((bf16[4,256,1152]{2,1,0:T(8,128)(2,1)}), bf16[4,256,1152]{2,1,0:T(8,128)(2,1)S(1)}, u32[]{:S(2)}, u32[]{:S(2)}) async-start(bf16[4,256,1152]{2,1,0:T(8,128)(2,1)} %project.1.refs_3_), calls=%async_computation | async-start | bytes 4718592 | tf_op jit(solution)/shard_map/all_to_all | solution.py:435
  71.4 16.0 %collective-permute-done.10.refs_2_.refs_5_ = bf16[2,64,1024]{2,1,0:T(8,128)(2,1)S(1)} collective-permute-done((bf16[2,64,1024]{2,1,0:T(8,128)(2,1)S(1)}, bf16[2,64,1024]{2,1,0:T(8,128)(2,1)S(1)}, u32[]{:S(2)}, u32[]{:S(2)}) %collective-permute-start.10) | collective-permute-done | bytes 262176 | tf_op jit(solution)/shard_map/ppermute | solution.py:457
  88.8 19.5 %collective-permute-done.9.refs_1_.refs_14_.refs_11_ = bf16[4,64,1024]{2,1,0:T(8,128)(2,1)} collective-permute-done((bf16[4,64,1024]{2,1,0:T(8,128)(2,1)}, bf16[4,64,1024]{2,1,0:T(8,128)(2,1)}, u32[]{:S(2)}, u32[]{:S(2)}) %collective-permute-start.9) | collective-permute-done | bytes 524320 | tf_op jit(solution)/shard_map/ppermute | solution.py:457
  111.4 3.7 %collective-permute-start.13 = (bf16[4,64,1024]{2,1,0:T(8,128)(2,1)}, bf16[4,64,1024]{2,1,0:T(8,128)(2,1)}, u32[]{:S(2)}, u32[]{:S(2)}) collective-permute-start(bf16[4,64,1024]{2,1,0:T(8,128)(2,1)} %get-tuple-element.46), channel_id=1, source_target_pairs={{0,24},{8,0},{16,8},{24,16},{1,25},{9,1},{17,9},{25,17},{2,26},{10... | collective-permute-start | bytes 1572872 | tf_op jit(solution)/shard_map/ppermute | solution.py:457
  115.2 6.8 %collective-permute-done.11.from_ref = bf16[1,4,64,1024]{3,2,1,0:T(8,128)(2,1)} collective-permute-done((bf16[1,4,64,1024]{3,2,1,0:T(8,128)(2,1)}, bf16[1,4,64,1024]{3,2,1,0:T(8,128)(2,1)}, u32[]{:S(2)}, u32[]{:S(2)}) %collective-permute-start.11) | collective-permute-done | bytes 524320 | tf_op jit(solution)/shard_map/ppermute | solution.py:422
  122.0 5.3 %collective-permute-done.12.refs_1_.refs_16_.refs_13_ = bf16[4,64,1024]{2,1,0:T(8,128)(2,1)} collective-permute-done((bf16[4,64,1024]{2,1,0:T(8,128)(2,1)}, bf16[4,64,1024]{2,1,0:T(8,128)(2,1)}, u32[]{:S(2)}, u32[]{:S(2)}) %collective-permute-start.12) | collective-permute-done | bytes 524320 | tf_op jit(solution)/shard_map/ppermute | solution.py:457
  127.3 3.7 %pick.9 = (bf16[2,64,1024]{2,1,0:T(8,128)(2,1)}, bf16[2,64,1024]{2,1,0:T(8,128)(2,1)}, bf16[2,64,1024]{2,1,0:T(8,128)(2,1)}, bf16[2,64,1024]{2,1,0:T(8,128)(2,1)}, bf16[4,256,1152]{2,1,0:T(8,128)(2,1)}) custom-call(s32[16,8]{1,0:T(8,128)} %select_reduce_fusion.7.table, s32[4]{0:T(128)} %pad_add_fusion.place, ...), custom_call_target="tpu_custom_call" | custom-call | flops 1 | bytes 1 | tf_op jit(solution)/shard_map/pick/pallas_call | solution.py:441
  144.6 7.4 %collective-permute-done.16.refs_17_.refs_14_ = bf16[4,64,1024]{2,1,0:T(8,128)(2,1)S(1)} collective-permute-done((bf16[4,64,1024]{2,1,0:T(8,128)(2,1)}, bf16[4,64,1024]{2,1,0:T(8,128)(2,1)S(1)}, u32[]{:S(2)}, u32[]{:S(2)}) %collective-permute-start.16) | collective-permute-done | bytes 524320 | tf_op jit(solution)/shard_map/ppermute | solution.py:457
  152.0 5.5 %collective-permute-done.17.refs_20_.refs_17_ = bf16[2,64,1024]{2,1,0:T(8,128)(2,1)S(1)} collective-permute-done((bf16[2,64,1024]{2,1,0:T(8,128)(2,1)}, bf16[2,64,1024]{2,1,0:T(8,128)(2,1)S(1)}, u32[]{:S(2)}, u32[]{:S(2)}) %collective-permute-start.17) | collective-permute-done | bytes 262176 | tf_op jit(solution)/shard_map/ppermute | solution.py:457
  157.5 5.3 %collective-permute-done.18.refs_21_.refs_18_ = bf16[2,64,1024]{2,1,0:T(8,128)(2,1)S(1)} collective-permute-done((bf16[2,64,1024]{2,1,0:T(8,128)(2,1)}, bf16[2,64,1024]{2,1,0:T(8,128)(2,1)S(1)}, u32[]{:S(2)}, u32[]{:S(2)}) %collective-permute-start.18) | collective-permute-done | bytes 262176 | tf_op jit(solution)/shard_map/ppermute | solution.py:457
  164.8 10.7 %pairs.3 = (bf16[4,4,4,64,256]{4,3,2,1,0:T(8,128)(2,1)}, f32[64,1,64]{2,1,0:T(1,128)}) custom-call(s32[4,64]{1,0:T(4,128)} %get-tuple-element.71.sources, s32[4,64]{1,0:T(4,128)} %get-tuple-element.70.slots, s32[4]{0:T(128)} %get-tuple-element.76.counts, s32[4]{0:T(128)} %pad_add_fusion.place, f32[2]{0:T(128)} %pad_maximum_fusion.2.scale_bias, ...), custom_call_target="tpu_custom_call" | custom-call | flops 1 | bytes 1 | tf_op jit(solution)/shard_map/pairs/pallas_call | solution.py:297
  178.8 12.9 %pairs.2 = (bf16[4,4,4,64,256]{4,3,2,1,0:T(8,128)(2,1)}, f32[64,1,64]{2,1,0:T(1,128)}, f32[4,1,64]{2,1,0:T(1,128)}) custom-call(s32[4,64]{1,0:T(4,128)} %get-tuple-element.74.sources, s32[4,64]{1,0:T(4,128)} %get-tuple-element.75.slots, s32[4]{0:T(128)} %get-tuple-element.96.counts, s32[4]{0:T(128)} %pad_add_fusion.place, f32[2]{0:T(128)} %pad_maximum_fusion.2.scale_bias, ...), custom_call_target="tpu_custom_call" | custom-call | flops 1 | bytes 1 | tf_op jit(solution)/shard_map/pairs/pallas_call | solution.py:297
  198.4 18.6 %all_to_all.10 = f32[64,1,128]{2,1,0:T(1,128)S(1)} all-to-all(f32[64,1,128]{2,1,0:T(1,128)S(1)} %reshape.239), channel_id=1, replica_groups=mesh['z'=8,'y'=4,'c'=2,'x'=4] {'z','y','c'}, dimensions={0} | all-to-all | bytes 65536 | tf_op jit(solution)/shard_map/all_to_all | solution.py:335
  222.1 7.4 %head.1 = (bf16[128,4096]{1,0:T(8,128)(2,1)}, bf16[128,4096]{1,0:T(8,128)(2,1)}) custom-call(s32[4]{0:T(128)} %pad_add_fusion.place, bf16[1024,256]{1,0:T(8,128)(2,1)} %bitcast.55, bf16[1024,256]{1,0:T(8,128)(2,1)} %copy-done.19, bf16[1024,256]{1,0:T(8,128)(2,1)} %copy-done.20, bf16[1024,256]{1,0:T(8,128)(2,1)} %copy-done.21, ...), custom_call_target="tpu_custom_call" | custom-call | flops 2147483648 | bytes 16777216 | tf_op jit(solution)/shard_map/head/pallas_call | solution.py:346
  235.4 4.0 %collective-permute-start.28 = (bf16[32,4096]{1,0:T(8,128)(2,1)S(1)}, bf16[32,4096]{1,0:T(8,128)(2,1)S(1)}, u32[]{:S(2)}, u32[]{:S(2)}) collective-permute-start(bf16[32,4096]{1,0:T(8,128)(2,1)S(1)} %get-tuple-element.90), channel_id=1, source_target_pairs={{0,24},{8,0},{16,8},{24,16},{1,25},{9,1},{17,9},{25,17},{2,26},{10... | collective-permute-start | bytes 786440 | tf_op jit(solution)/shard_map/ppermute | solution.py:388
  243.2 3.7 %collective-permute-done.28 = bf16[32,4096]{1,0:T(8,128)(2,1)S(1)} collective-permute-done((bf16[32,4096]{1,0:T(8,128)(2,1)S(1)}, bf16[32,4096]{1,0:T(8,128)(2,1)S(1)}, u32[]{:S(2)}, u32[]{:S(2)}) %collective-permute-start.28) | collective-permute-done | bytes 262176 | tf_op jit(solution)/shard_map/ppermute | solution.py:388
  250.1 4.4 %collective-permute-done.26 = bf16[32,4096]{1,0:T(8,128)(2,1)S(1)} collective-permute-done((bf16[32,4096]{1,0:T(8,128)(2,1)S(1)}, bf16[32,4096]{1,0:T(8,128)(2,1)S(1)}, u32[]{:S(2)}, u32[]{:S(2)}) %collective-permute-start.26) | collective-permute-done | bytes 262176 | tf_op jit(solution)/shard_map/ppermute | solution.py:388
  257.0 3.5 %collective-permute-done.29 = bf16[16,4096]{1,0:T(8,128)(2,1)S(1)} collective-permute-done((bf16[16,4096]{1,0:T(8,128)(2,1)S(1)}, bf16[16,4096]{1,0:T(8,128)(2,1)S(1)}, u32[]{:S(2)}, u32[]{:S(2)}) %collective-permute-start.29) | collective-permute-done | bytes 131104 | tf_op jit(solution)/shard_map/ppermute | solution.py:393
  261.1 8.0 %collective-permute-done.30 = bf16[16,2048]{1,0:T(8,128)(2,1)S(1)} collective-permute-done((bf16[16,2048]{1,0:T(8,128)(2,1)S(1)}, bf16[16,2048]{1,0:T(8,128)(2,1)S(1)}, u32[]{:S(2)}, u32[]{:S(2)}) %collective-permute-start.30) | collective-permute-done | bytes 65568 | tf_op jit(solution)/shard_map/ppermute | solution.py:397
  269.6 9.6 %collective-permute-start.31 = (bf16[16,1024]{1,0:T(8,128)(2,1)S(1)}, bf16[16,1024]{1,0:T(8,128)(2,1)S(1)}, u32[]{:S(2)}, u32[]{:S(2)}) collective-permute-start(bf16[16,1024]{1,0:T(8,128)(2,1)S(1)} %bitcast.68), channel_id=1, source_target_pairs={{0,0},{1,64},{2,128},{3,192},{32,32},{33,96},{34,160},{35,224},{64... | collective-permute-start | bytes 98312 | tf_op jit(solution)/shard_map/ppermute | solution.py:408
  (171 shorter events, 91.0 us)
Async XLA Ops:
  7.2 214.1 %all-gather.3.cloned.1.call-start = ((), (), s32[]{:S(2)}) async-start(), calls=%async_computation.2 | async-start | bytes 10485760 | tf_op jit(solution)/shard_map/all_gather | solution.py:256
  12.2 18.7 %collective-permute-start.1 = (bf16[2,4,64,1024]{3,2,1,0:T(8,128)(2,1)S(1)}, bf16[2,4,64,1024]{3,2,1,0:T(8,128)(2,1)S(1)}, u32[]{:S(2)}, u32[]{:S(2)}) collective-permute-start(bf16[2,4,64,1024]{3,2,1,0:T(8,128)(2,1)S(1)} %pad_maximum_fusion), channel_id=1, source_target_pairs={{0,32},{4,228},{32,64},{36,4},{64,96},{68,36},{96,128},{100,68},{1... | collective-permute-start | bytes 3145736 | tf_op jit(solution)/shard_map/ppermute | solution.py:422
  35.1 17.9 %collective-permute-start.4 = (bf16[2,4,64,1024]{3,2,1,0:T(8,128)(2,1)}, bf16[2,4,64,1024]{3,2,1,0:T(8,128)(2,1)S(1)}, u32[]{:S(2)}, u32[]{:S(2)}) collective-permute-start(bf16[2,4,64,1024]{3,2,1,0:T(8,128)(2,1)} %get-tuple-element.36), channel_id=1, source_target_pairs={{0,32},{4,228},{32,64},{36,4},{64,96},{68,36},{96,128},{100,68},{1... | collective-permute-start | bytes 3145736 | tf_op jit(solution)/shard_map/ppermute | solution.py:422
  35.4 12.7 %collective-permute-start.5 = (bf16[4,64,1024]{2,1,0:T(8,128)(2,1)}, bf16[4,64,1024]{2,1,0:T(8,128)(2,1)S(1)}, u32[]{:S(2)}, u32[]{:S(2)}) collective-permute-start(bf16[4,64,1024]{2,1,0:T(8,128)(2,1)} %get-tuple-element.37), channel_id=1, source_target_pairs={{0,8},{8,16},{16,24},{24,0},{1,9},{9,17},{17,25},{25,1},{2,10},{10... | collective-permute-start | bytes 1572872 | tf_op jit(solution)/shard_map/ppermute | solution.py:457
  58.6 56.6 %all-to-all-start = ((bf16[4,256,1152]{2,1,0:T(8,128)(2,1)}), bf16[4,256,1152]{2,1,0:T(8,128)(2,1)S(1)}, u32[]{:S(2)}, u32[]{:S(2)}) async-start(bf16[4,256,1152]{2,1,0:T(8,128)(2,1)} %project.1.refs_3_), calls=%async_computation | async-start | bytes 4718592 | tf_op jit(solution)/shard_map/all_to_all | solution.py:435
  63.5 44.8 %collective-permute-start.7 = (bf16[2,4,64,1024]{3,2,1,0:T(8,128)(2,1)}, bf16[2,4,64,1024]{3,2,1,0:T(8,128)(2,1)}, u32[]{:S(2)}, u32[]{:S(2)}) collective-permute-start(bf16[2,4,64,1024]{3,2,1,0:T(8,128)(2,1)} %get-tuple-element.40), channel_id=1, source_target_pairs={{0,32},{4,228},{32,64},{36,4},{64,96},{68,36},{96,128},{100,68},{1... | collective-permute-start | bytes 3145736 | tf_op jit(solution)/shard_map/ppermute | solution.py:422
  64.7 24.2 %collective-permute-start.8 = (bf16[4,64,1024]{2,1,0:T(8,128)(2,1)}, bf16[4,64,1024]{2,1,0:T(8,128)(2,1)}, u32[]{:S(2)}, u32[]{:S(2)}) collective-permute-start(bf16[4,64,1024]{2,1,0:T(8,128)(2,1)} %get-tuple-element.41), channel_id=1, source_target_pairs={{0,8},{8,16},{16,24},{24,0},{1,9},{9,17},{17,25},{25,1},{2,10},{10... | collective-permute-start | bytes 1572872 | tf_op jit(solution)/shard_map/ppermute | solution.py:457
  66.0 42.4 %collective-permute-start.9 = (bf16[4,64,1024]{2,1,0:T(8,128)(2,1)}, bf16[4,64,1024]{2,1,0:T(8,128)(2,1)}, u32[]{:S(2)}, u32[]{:S(2)}) collective-permute-start(bf16[4,64,1024]{2,1,0:T(8,128)(2,1)} %get-tuple-element.42), channel_id=1, source_target_pairs={{0,24},{8,0},{16,8},{24,16},{1,25},{9,1},{17,9},{25,17},{2,26},{10... | collective-permute-start | bytes 1572872 | tf_op jit(solution)/shard_map/ppermute | solution.py:457
  67.9 19.5 %collective-permute-start.10 = (bf16[2,64,1024]{2,1,0:T(8,128)(2,1)S(1)}, bf16[2,64,1024]{2,1,0:T(8,128)(2,1)S(1)}, u32[]{:S(2)}, u32[]{:S(2)}) collective-permute-start(bf16[2,64,1024]{2,1,0:T(8,128)(2,1)S(1)} %copy-done.26), channel_id=1, source_target_pairs={{0,16},{8,24},{16,0},{24,8},{1,17},{9,25},{17,1},{25,9},{2,18},{10... | collective-permute-start | bytes 786440 | tf_op jit(solution)/shard_map/ppermute | solution.py:457
  69.4 45.8 %collective-permute-start.14 = (bf16[4,64,1024]{2,1,0:T(8,128)(2,1)}, bf16[4,64,1024]{2,1,0:T(8,128)(2,1)S(1)}, u32[]{:S(2)}, u32[]{:S(2)}) collective-permute-start(bf16[4,64,1024]{2,1,0:T(8,128)(2,1)} %get-tuple-element.47), channel_id=1, source_target_pairs={{0,16},{8,24},{16,0},{24,8},{1,17},{9,25},{17,1},{25,9},{2,18},{10... | collective-permute-start | bytes 1572872 | tf_op jit(solution)/shard_map/ppermute | solution.py:457
  88.1 27.0 %collective-permute-start.15 = (bf16[4,64,1024]{2,1,0:T(8,128)(2,1)}, bf16[4,64,1024]{2,1,0:T(8,128)(2,1)S(1)}, u32[]{:S(2)}, u32[]{:S(2)}) collective-permute-start(bf16[4,64,1024]{2,1,0:T(8,128)(2,1)} %get-tuple-element.48), channel_id=1, source_target_pairs={{0,16},{8,24},{16,0},{24,8},{1,17},{9,25},{17,1},{25,9},{2,18},{10... | collective-permute-start | bytes 1572872 | tf_op jit(solution)/shard_map/ppermute | solution.py:457
  111.3 16.0 %collective-permute-start.12 = (bf16[4,64,1024]{2,1,0:T(8,128)(2,1)}, bf16[4,64,1024]{2,1,0:T(8,128)(2,1)}, u32[]{:S(2)}, u32[]{:S(2)}) collective-permute-start(bf16[4,64,1024]{2,1,0:T(8,128)(2,1)} %get-tuple-element.45), channel_id=1, source_target_pairs={{0,8},{8,16},{16,24},{24,0},{1,9},{9,17},{17,25},{25,1},{2,10},{10... | collective-permute-start | bytes 1572872 | tf_op jit(solution)/shard_map/ppermute | solution.py:457
  111.4 15.9 %collective-permute-start.13 = (bf16[4,64,1024]{2,1,0:T(8,128)(2,1)}, bf16[4,64,1024]{2,1,0:T(8,128)(2,1)}, u32[]{:S(2)}, u32[]{:S(2)}) collective-permute-start(bf16[4,64,1024]{2,1,0:T(8,128)(2,1)} %get-tuple-element.46), channel_id=1, source_target_pairs={{0,24},{8,0},{16,8},{24,16},{1,25},{9,1},{17,9},{25,17},{2,26},{10... | collective-permute-start | bytes 1572872 | tf_op jit(solution)/shard_map/ppermute | solution.py:457
  131.0 32.2 %collective-permute-start.20 = (bf16[4,256,1152]{2,1,0:T(8,128)(2,1)}, bf16[4,256,1152]{2,1,0:T(8,128)(2,1)S(1)}, u32[]{:S(2)}, u32[]{:S(2)}) collective-permute-start(bf16[4,256,1152]{2,1,0:T(8,128)(2,1)} %get-tuple-element.49), channel_id=1, source_target_pairs={{0,4},{4,0},{1,5},{5,1},{2,6},{6,2},{3,7},{7,3},{8,12},{12,8},{9,1... | collective-permute-start | bytes 7077896 | tf_op jit(solution)/shard_map/ppermute | solution.py:331
  135.4 16.6 %collective-permute-start.16 = (bf16[4,64,1024]{2,1,0:T(8,128)(2,1)}, bf16[4,64,1024]{2,1,0:T(8,128)(2,1)S(1)}, u32[]{:S(2)}, u32[]{:S(2)}) collective-permute-start(bf16[4,64,1024]{2,1,0:T(8,128)(2,1)} %get-tuple-element.53), channel_id=1, source_target_pairs={{0,16},{8,24},{16,0},{24,8},{1,17},{9,25},{17,1},{25,9},{2,18},{10... | collective-permute-start | bytes 1572872 | tf_op jit(solution)/shard_map/ppermute | solution.py:457
  139.2 18.4 %collective-permute-start.17 = (bf16[2,64,1024]{2,1,0:T(8,128)(2,1)}, bf16[2,64,1024]{2,1,0:T(8,128)(2,1)S(1)}, u32[]{:S(2)}, u32[]{:S(2)}) collective-permute-start(bf16[2,64,1024]{2,1,0:T(8,128)(2,1)} %get-tuple-element.55), channel_id=1, source_target_pairs={{0,8},{8,16},{16,24},{24,0},{1,9},{9,17},{17,25},{25,1},{2,10},{10... | collective-permute-start | bytes 786440 | tf_op jit(solution)/shard_map/ppermute | solution.py:457
  140.1 22.7 %collective-permute-start.18 = (bf16[2,64,1024]{2,1,0:T(8,128)(2,1)}, bf16[2,64,1024]{2,1,0:T(8,128)(2,1)S(1)}, u32[]{:S(2)}, u32[]{:S(2)}) collective-permute-start(bf16[2,64,1024]{2,1,0:T(8,128)(2,1)} %get-tuple-element.56), channel_id=1, source_target_pairs={{0,16},{8,24},{16,0},{24,8},{1,17},{9,25},{17,1},{25,9},{2,18},{10... | collective-permute-start | bytes 786440 | tf_op jit(solution)/shard_map/ppermute | solution.py:457
  141.5 21.7 %collective-permute-start.19 = (bf16[2,64,1024]{2,1,0:T(8,128)(2,1)}, bf16[2,64,1024]{2,1,0:T(8,128)(2,1)S(1)}, u32[]{:S(2)}, u32[]{:S(2)}) collective-permute-start(bf16[2,64,1024]{2,1,0:T(8,128)(2,1)} %get-tuple-element.57), channel_id=1, source_target_pairs={{0,24},{8,0},{16,8},{24,16},{1,25},{9,1},{17,9},{25,17},{2,26},{10... | collective-permute-start | bytes 786440 | tf_op jit(solution)/shard_map/ppermute | solution.py:457
  175.5 16.3 %collective-permute-start.21 = (bf16[4,4,4,64,256]{4,3,2,1,0:T(8,128)(2,1)}, bf16[4,4,4,64,256]{4,3,2,1,0:T(8,128)(2,1)S(1)}, u32[]{:S(2)}, u32[]{:S(2)}) collective-permute-start(bf16[4,4,4,64,256]{4,3,2,1,0:T(8,128)(2,1)} %get-tuple-element.62), channel_id=1, source_target_pairs={{0,4},{4,0},{1,5},{5,1},{2,6},{6,2},{3,7},{7,3},{8,12},{12,8},{9,1... | collective-permute-start | bytes 6291464 | tf_op jit(solution)/shard_map/ppermute | solution.py:339
  195.1 24.0 %collective-permute-start.22 = (bf16[1024,256]{1,0:T(8,128)(2,1)}, bf16[1024,256]{1,0:T(8,128)(2,1)S(1)}, u32[]{:S(2)}, u32[]{:S(2)}) collective-permute-start(bf16[1024,256]{1,0:T(8,128)(2,1)} %bitcast.22), channel_id=1, source_target_pairs={{0,1},{1,2},{2,3},{3,0},{4,5},{5,6},{6,7},{7,4},{8,9},{9,10},{10,1... | collective-permute-start | bytes 1572872 | tf_op jit(solution)/shard_map/ppermute | solution.py:343
  196.2 22.8 %collective-permute-start.23 = (bf16[1024,256]{1,0:T(8,128)(2,1)S(1)}, bf16[1024,256]{1,0:T(8,128)(2,1)S(1)}, u32[]{:S(2)}, u32[]{:S(2)}) collective-permute-start(bf16[1024,256]{1,0:T(8,128)(2,1)S(1)} %bitcast.62), channel_id=1, source_target_pairs={{0,2},{1,3},{2,0},{3,1},{4,6},{5,7},{6,4},{7,5},{8,10},{9,11},{10,... | collective-permute-start | bytes 1572872 | tf_op jit(solution)/shard_map/ppermute | solution.py:343
  197.1 24.2 %collective-permute-start.24 = (bf16[1024,256]{1,0:T(8,128)(2,1)S(1)}, bf16[1024,256]{1,0:T(8,128)(2,1)S(1)}, u32[]{:S(2)}, u32[]{:S(2)}) collective-permute-start(bf16[1024,256]{1,0:T(8,128)(2,1)S(1)} %bitcast.61), channel_id=1, source_target_pairs={{0,3},{1,0},{2,1},{3,2},{4,7},{5,4},{6,5},{7,6},{8,11},{9,8},{10,9... | collective-permute-start | bytes 1572872 | tf_op jit(solution)/shard_map/ppermute | solution.py:343
  241.8 12.7 %collective-permute-start.26 = (bf16[32,4096]{1,0:T(8,128)(2,1)S(1)}, bf16[32,4096]{1,0:T(8,128)(2,1)S(1)}, u32[]{:S(2)}, u32[]{:S(2)}) collective-permute-start(bf16[32,4096]{1,0:T(8,128)(2,1)S(1)} %get-tuple-element.89), channel_id=1, source_target_pairs={{0,8},{8,16},{16,24},{24,0},{1,9},{9,17},{17,25},{25,1},{2,10},{10... | collective-permute-start | bytes 786440 | tf_op jit(solution)/shard_map/ppermute | solution.py:388
  269.6 12.1 %collective-permute-start.31 = (bf16[16,1024]{1,0:T(8,128)(2,1)S(1)}, bf16[16,1024]{1,0:T(8,128)(2,1)S(1)}, u32[]{:S(2)}, u32[]{:S(2)}) collective-permute-start(bf16[16,1024]{1,0:T(8,128)(2,1)S(1)} %bitcast.68), channel_id=1, source_target_pairs={{0,0},{1,64},{2,128},{3,192},{32,32},{33,96},{34,160},{35,224},{64... | collective-permute-start | bytes 98312 | tf_op jit(solution)/shard_map/ppermute | solution.py:408
  (38 other events, 259.0 us)
Sparse Core Ops, SparseCore 0:
  58.7 100.2 all-gather.2

commit v7 on v6

--- a/solution.py
+++ b/solution.py
@@ -425,11 +425,11 @@
         outs = [jax.ShapeDtypeStruct(shape, BF16)] * y_size
         if keeps:
             outs.append(jax.ShapeDtypeStruct((keeps,) + own_images.shape, BF16))
-        before = [groups[step - 1][1], groups[step - 1][-1]] if step else []
-        if step == last - 1:
+        before = [groups[step - 1][1], groups[step - 1][-1]] if step in (1, 2, last) else []
+        if step == 2:
             before.append(groups[0][y_size // 2])
         if step == last:
-            before += [groups[k][y_size // 2] for k in range(1, last - 1)]
+            before += [groups[k][y_size // 2] for k in range(1, last - 1)] + groups[last - 2][1:]
         if step == 1:
             text_emb = project(here, picked[0])
             texts = lax.all_to_all(text_emb, "x", split_axis=0, concat_axis=0, tiled=True)

time: 291 us -> 284 us (0.976)
  waiting for transfers between devices: 110 us -> 106 us
    ppermute x15, waiting for transfers between devices: 66.8 us -> 59.2 us  [exchange_images(): lax.ppermute(picked[n], 'y', shifted(y_size, n))]
    ppermute x3, waiting for transfers between devices: 2.24 us -> 7.25 us  [on_device(): grads.append(lax.ppermute(total, 'x', shifted(x_size, k)) if k else total)]
    ppermute x3, starting transfers between devices: 6.77 us -> 3.64 us  [add_over_dp(): lax.ppermute(total[k], 'y', shifted(y_size, k))]
    all_to_all x1, blocking collectives: 18.6 us -> 15.7 us  [on_device(): lax.all_to_all(jnp.concatenate([pair_loss, other_loss], axis=1), DP, spli...]
    unnamed x60 -> x58, local copies, waits for them, and re-layouts: 7.73 us -> 8.09 us
  transfers between devices with their start and end apart: 35 -> 35, of which waited for: 22 -> 20; matrix products, arithmetic and copies ran while one was open for 7% -> 7% of each run, Pallas kernels for 14% -> 15%
where the time goes in v7:
time: 284 us; the launch traced here: 283 us
  waiting for transfers between devices  106 us (37%)
  starting transfers between devices  57 us (20%)
  Pallas kernels  56.6 us (20%)
  other arithmetic  19.6 us (7%)
  between operations  15.9 us (6%)
  blocking collectives  15.7 us (6%)
  local copies, waits for them, and re-layouts  11.9 us (4%)
    ppermute x15, waiting for transfers between devices, exchange_images(): lax.ppermute(picked[n], 'y', shifted(y_size, n))  59.2 us
    pallas_call x2, Pallas kernels, pairs(): pl.pallas_call(functools.partial(pair_kernel, starts=starts, own=own), gr...  25.3 us
    ppermute x15, starting transfers between devices, exchange_images(): lax.ppermute(picked[n], 'y', shifted(y_size, n))  24.1 us
    pallas_call x5, Pallas kernels, exchange_images(): pl.pallas_call(functools.partial(pick_kernel, step=step, sizes=sizes, onw...  16.2 us
    all_to_all x1, blocking collectives, on_device(): lax.all_to_all(jnp.concatenate([pair_loss, other_loss], axis=1), DP, spli...  15.7 us
    ppermute x4, waiting for transfers between devices, exchange_images(): lax.ppermute(moving, ('z', 'c'), onward)  11.2 us
    ppermute x3, waiting for transfers between devices, add_over_dp(): lax.ppermute(total[k], 'y', shifted(y_size, k))  11 us
    ppermute x2, starting transfers between devices, add_over_dp(): final = final + lax.ppermute(chunk, ('z', 'x'), pairs).astype(F32)  9.79 us
  transfers between devices with their start and end apart: 35, of which 20 were waited for; matrix products, arithmetic and copies ran while one was open for 7% of the time, Pallas kernels for 15%

profile of v7, /device:TPU:4, one launch (start us, length us, event | category | flops | bytes accessed | tf_op | source)
XLA Modules:
  0.0 282.7 jit_solution(9680206928456776170)
XLA Ops:
  23.5 4.6 %collective-permute-done.2.refs_0_.refs_4_.refs_1_ = bf16[2,64,1024]{2,1,0:T(8,128)(2,1)S(1)} collective-permute-done((bf16[2,64,1024]{2,1,0:T(8,128)(2,1)}, bf16[2,64,1024]{2,1,0:T(8,128)(2,1)S(1)}, u32[]{:S(2)}, u32[]{:S(2)}) %collective-permute-start.2) | collective-permute-done | bytes 262176 | tf_op jit(solution)/shard_map/ppermute | solution.py:457
  40.4 7.6 %project.1.refs_4_ = bf16[4,256,1152]{2,1,0:T(8,128)(2,1)} custom-call(bf16[256,4096]{1,0:T(8,128)(2,1)} %bitcast.51, bf16[4096,1024]{1,0:T(8,128)(2,1)} %weight.1, bf16[2,4,64,1024]{3,2,1,0:T(8,128)(2,1)} %copy-done.6, bf16[2,64,1024]{2,1,0:T(8,128)(2,1)} %get-tuple-element.40.refs_1_.refs_3_.refs_0_), custom_call_target="tpu_custom_call" | custom-call | flops 1 | bytes 1 | tf_op jit(solution)/shard_map/project/pallas_call | solution.py:253
  48.0 6.8 %collective-permute-done.7.refs_3_.refs_5_.refs_2_ = bf16[2,64,1024]{2,1,0:T(8,128)(2,1)S(1)} collective-permute-done((bf16[2,64,1024]{2,1,0:T(8,128)(2,1)}, bf16[2,64,1024]{2,1,0:T(8,128)(2,1)S(1)}, u32[]{:S(2)}, u32[]{:S(2)}) %collective-permute-start.7) | collective-permute-done | bytes 262176 | tf_op jit(solution)/shard_map/ppermute | solution.py:457
  56.9 4.4 %pick.7 = (bf16[4,64,1024]{2,1,0:T(8,128)(2,1)}, bf16[4,64,1024]{2,1,0:T(8,128)(2,1)}, bf16[4,64,1024]{2,1,0:T(8,128)(2,1)}, bf16[4,64,1024]{2,1,0:T(8,128)(2,1)...) custom-call(s32[16,8]{1,0:T(8,128)} %select_reduce_fusion.7.table, s32[4]{0:T(128)} %pad_add_fusion.place, ...), custom_call_target="tpu_custom_call" | custom-call | flops 1 | bytes 1 | tf_op jit(solution)/shard_map/pick/pallas_call | solution.py:441
  61.3 6.9 %all-to-all-start = ((bf16[4,256,1152]{2,1,0:T(8,128)(2,1)}), bf16[4,256,1152]{2,1,0:T(8,128)(2,1)S(1)}, u32[]{:S(2)}, u32[]{:S(2)}) async-start(bf16[4,256,1152]{2,1,0:T(8,128)(2,1)} %project.1.refs_4_), calls=%async_computation | async-start | bytes 4718592 | tf_op jit(solution)/shard_map/all_to_all | solution.py:435
  77.9 8.8 %collective-permute-done.8.from_ref = bf16[2,4,64,1024]{3,2,1,0:T(8,128)(2,1)} collective-permute-done((bf16[2,4,64,1024]{3,2,1,0:T(8,128)(2,1)}, bf16[2,4,64,1024]{3,2,1,0:T(8,128)(2,1)}, u32[]{:S(2)}, u32[]{:S(2)}) %collective-permute-start.8) | collective-permute-done | bytes 1048608 | tf_op jit(solution)/shard_map/ppermute | solution.py:422
  90.8 8.1 %collective-permute-done.13.refs_4_.refs_6_.refs_13_.refs_10_ = bf16[4,64,1024]{2,1,0:T(8,128)(2,1)S(1)} collective-permute-done((bf16[4,64,1024]{2,1,0:T(8,128)(2,1)}, bf16[4,64,1024]{2,1,0:T(8,128)(2,1)S(1)}, u32[]{:S(2)}, u32[]{:S(2)}) %collective-permute-start.13) | collective-permute-done | bytes 524320 | tf_op jit(solution)/shard_map/ppermute | solution.py:457
  100.5 9.7 %collective-permute-done.14.refs_5_.refs_12_.refs_9_ = bf16[4,64,1024]{2,1,0:T(8,128)(2,1)} collective-permute-done((bf16[4,64,1024]{2,1,0:T(8,128)(2,1)}, bf16[4,64,1024]{2,1,0:T(8,128)(2,1)}, u32[]{:S(2)}, u32[]{:S(2)}) %collective-permute-start.14) | collective-permute-done | bytes 524320 | tf_op jit(solution)/shard_map/ppermute | solution.py:457
  110.2 11.2 %collective-permute-done.10.refs_1_.refs_16_.refs_13_ = bf16[4,64,1024]{2,1,0:T(8,128)(2,1)} collective-permute-done((bf16[4,64,1024]{2,1,0:T(8,128)(2,1)}, bf16[4,64,1024]{2,1,0:T(8,128)(2,1)}, u32[]{:S(2)}, u32[]{:S(2)}) %collective-permute-start.10) | collective-permute-done | bytes 524320 | tf_op jit(solution)/shard_map/ppermute | solution.py:457
  121.4 3.7 %pick.9 = (bf16[2,64,1024]{2,1,0:T(8,128)(2,1)}, bf16[2,64,1024]{2,1,0:T(8,128)(2,1)}, bf16[2,64,1024]{2,1,0:T(8,128)(2,1)}, bf16[2,64,1024]{2,1,0:T(8,128)(2,1)}, bf16[4,256,1152]{2,1,0:T(8,128)(2,1)}) custom-call(s32[16,8]{1,0:T(8,128)} %select_reduce_fusion.7.table, s32[4]{0:T(128)} %pad_add_fusion.place, ...), custom_call_target="tpu_custom_call" | custom-call | flops 1 | bytes 1 | tf_op jit(solution)/shard_map/pick/pallas_call | solution.py:441
  138.3 7.8 %collective-permute-done.16.refs_17_.refs_14_ = bf16[4,64,1024]{2,1,0:T(8,128)(2,1)S(1)} collective-permute-done((bf16[4,64,1024]{2,1,0:T(8,128)(2,1)}, bf16[4,64,1024]{2,1,0:T(8,128)(2,1)S(1)}, u32[]{:S(2)}, u32[]{:S(2)}) %collective-permute-start.16) | collective-permute-done | bytes 524320 | tf_op jit(solution)/shard_map/ppermute | solution.py:457
  146.1 5.5 %collective-permute-done.17.refs_20_.refs_17_ = bf16[2,64,1024]{2,1,0:T(8,128)(2,1)S(1)} collective-permute-done((bf16[2,64,1024]{2,1,0:T(8,128)(2,1)}, bf16[2,64,1024]{2,1,0:T(8,128)(2,1)S(1)}, u32[]{:S(2)}, u32[]{:S(2)}) %collective-permute-start.17) | collective-permute-done | bytes 262176 | tf_op jit(solution)/shard_map/ppermute | solution.py:457
  151.6 5.3 %collective-permute-done.18.refs_21_.refs_18_ = bf16[2,64,1024]{2,1,0:T(8,128)(2,1)S(1)} collective-permute-done((bf16[2,64,1024]{2,1,0:T(8,128)(2,1)}, bf16[2,64,1024]{2,1,0:T(8,128)(2,1)S(1)}, u32[]{:S(2)}, u32[]{:S(2)}) %collective-permute-start.18) | collective-permute-done | bytes 262176 | tf_op jit(solution)/shard_map/ppermute | solution.py:457
  158.5 11.5 %pairs.3 = (bf16[4,4,4,64,256]{4,3,2,1,0:T(8,128)(2,1)}, f32[64,1,64]{2,1,0:T(1,128)}) custom-call(s32[4,64]{1,0:T(4,128)} %get-tuple-element.71.sources, s32[4,64]{1,0:T(4,128)} %get-tuple-element.70.slots, s32[4]{0:T(128)} %get-tuple-element.76.counts, s32[4]{0:T(128)} %pad_add_fusion.place, f32[2]{0:T(128)} %pad_maximum_fusion.2.scale_bias, ...), custom_call_target="tpu_custom_call" | custom-call | flops 1 | bytes 1 | tf_op jit(solution)/shard_map/pairs/pallas_call | solution.py:297
  174.2 13.8 %pairs.2 = (bf16[4,4,4,64,256]{4,3,2,1,0:T(8,128)(2,1)}, f32[64,1,64]{2,1,0:T(1,128)}, f32[4,1,64]{2,1,0:T(1,128)}) custom-call(s32[4,64]{1,0:T(4,128)} %get-tuple-element.74.sources, s32[4,64]{1,0:T(4,128)} %get-tuple-element.75.slots, s32[4]{0:T(128)} %get-tuple-element.96.counts, s32[4]{0:T(128)} %pad_add_fusion.place, f32[2]{0:T(128)} %pad_maximum_fusion.2.scale_bias, ...), custom_call_target="tpu_custom_call" | custom-call | flops 1 | bytes 1 | tf_op jit(solution)/shard_map/pairs/pallas_call | solution.py:297
  188.0 3.3 %add_convert_fusion.1 = (bf16[1,4,4,64,256]{4,3,2,1,0:T(8,128)(2,1)S(1)}, bf16[1,4,4,64,256]{4,3,2,1,0:T(8,128)(2,1)S(1)}, bf16[1,4,4,64,256]{4,3,2,1,0:T(8,128)(2,1)}, bf16[1,4,4,64,256]{4,3,2,1,0:T(8,128)(2,1)}) fusion(bf16[4,4,4,64,256]{4,3,2,1,0:T(8,128)(2,1)S(1)} %collective-permute-done.21, bf16[4,4,4,64,256]{4,3,2,1,0:T(8,128)(2,1)} %get-tuple-element.61), kind=kLoop, calls=%fused_computation.6 | loop fusion | flops 4194304 | bytes 6291456 | tf_op jit(solution)/shard_map/convert_element_type | solution.py:342
  194.3 15.7 %all_to_all.10 = f32[64,1,128]{2,1,0:T(1,128)S(1)} all-to-all(f32[64,1,128]{2,1,0:T(1,128)S(1)} %reshape.239), channel_id=1, replica_groups=mesh['z'=8,'y'=4,'c'=2,'x'=4] {'z','y','c'}, dimensions={0} | all-to-all | bytes 65536 | tf_op jit(solution)/shard_map/all_to_all | solution.py:335
  211.9 5.0 %collective-permute-done.23.grad_2 = bf16[1024,256]{1,0:T(8,128)(2,1)S(1)} collective-permute-done((bf16[1024,256]{1,0:T(8,128)(2,1)S(1)}, bf16[1024,256]{1,0:T(8,128)(2,1)S(1)}, u32[]{:S(2)}, u32[]{:S(2)}) %collective-permute-start.23) | collective-permute-done | bytes 524320 | tf_op jit(solution)/shard_map/ppermute | solution.py:343
  220.0 7.4 %head.1 = (bf16[128,4096]{1,0:T(8,128)(2,1)}, bf16[128,4096]{1,0:T(8,128)(2,1)}) custom-call(s32[4]{0:T(128)} %pad_add_fusion.place, bf16[1024,256]{1,0:T(8,128)(2,1)} %bitcast.55, bf16[1024,256]{1,0:T(8,128)(2,1)} %copy-done.19, bf16[1024,256]{1,0:T(8,128)(2,1)} %copy-done.20, bf16[1024,256]{1,0:T(8,128)(2,1)} %copy-done.21, ...), custom_call_target="tpu_custom_call" | custom-call | flops 2147483648 | bytes 16777216 | tf_op jit(solution)/shard_map/head/pallas_call | solution.py:346
  236.6 4.5 %collective-permute-done.28 = bf16[32,4096]{1,0:T(8,128)(2,1)S(1)} collective-permute-done((bf16[32,4096]{1,0:T(8,128)(2,1)S(1)}, bf16[32,4096]{1,0:T(8,128)(2,1)S(1)}, u32[]{:S(2)}, u32[]{:S(2)}) %collective-permute-start.28) | collective-permute-done | bytes 262176 | tf_op jit(solution)/shard_map/ppermute | solution.py:388
  242.8 4.8 %collective-permute-done.26 = bf16[32,4096]{1,0:T(8,128)(2,1)S(1)} collective-permute-done((bf16[32,4096]{1,0:T(8,128)(2,1)S(1)}, bf16[32,4096]{1,0:T(8,128)(2,1)S(1)}, u32[]{:S(2)}, u32[]{:S(2)}) %collective-permute-start.26) | collective-permute-done | bytes 262176 | tf_op jit(solution)/shard_map/ppermute | solution.py:388
  249.3 4.0 %collective-permute-done.29 = bf16[16,4096]{1,0:T(8,128)(2,1)S(1)} collective-permute-done((bf16[16,4096]{1,0:T(8,128)(2,1)S(1)}, bf16[16,4096]{1,0:T(8,128)(2,1)S(1)}, u32[]{:S(2)}, u32[]{:S(2)}) %collective-permute-start.29) | collective-permute-done | bytes 131104 | tf_op jit(solution)/shard_map/ppermute | solution.py:393
  253.9 8.7 %collective-permute-done.30 = bf16[16,2048]{1,0:T(8,128)(2,1)S(1)} collective-permute-done((bf16[16,2048]{1,0:T(8,128)(2,1)S(1)}, bf16[16,2048]{1,0:T(8,128)(2,1)S(1)}, u32[]{:S(2)}, u32[]{:S(2)}) %collective-permute-start.30) | collective-permute-done | bytes 65568 | tf_op jit(solution)/shard_map/ppermute | solution.py:397
  263.0 9.7 %collective-permute-start.31 = (bf16[16,1024]{1,0:T(8,128)(2,1)S(1)}, bf16[16,1024]{1,0:T(8,128)(2,1)S(1)}, u32[]{:S(2)}, u32[]{:S(2)}) collective-permute-start(bf16[16,1024]{1,0:T(8,128)(2,1)S(1)} %bitcast.68), channel_id=1, source_target_pairs={{0,0},{1,64},{2,128},{3,192},{32,32},{33,96},{34,160},{35,224},{64... | collective-permute-start | bytes 98312 | tf_op jit(solution)/shard_map/ppermute | solution.py:408
  (169 shorter events, 88.0 us)
Async XLA Ops:
  7.2 212.0 %all-gather.3.cloned.1.call-start = ((), (), s32[]{:S(2)}) async-start(), calls=%async_computation.2 | async-start | bytes 10485760 | tf_op jit(solution)/shard_map/all_gather | solution.py:256
  12.2 18.7 %collective-permute-start.1 = (bf16[2,4,64,1024]{3,2,1,0:T(8,128)(2,1)S(1)}, bf16[2,4,64,1024]{3,2,1,0:T(8,128)(2,1)S(1)}, u32[]{:S(2)}, u32[]{:S(2)}) collective-permute-start(bf16[2,4,64,1024]{3,2,1,0:T(8,128)(2,1)S(1)} %pad_maximum_fusion), channel_id=1, source_target_pairs={{0,32},{4,228},{32,64},{36,4},{64,96},{68,36},{96,128},{100,68},{1... | collective-permute-start | bytes 3145736 | tf_op jit(solution)/shard_map/ppermute | solution.py:422
  35.0 19.9 %collective-permute-start.4 = (bf16[2,4,64,1024]{3,2,1,0:T(8,128)(2,1)}, bf16[2,4,64,1024]{3,2,1,0:T(8,128)(2,1)S(1)}, u32[]{:S(2)}, u32[]{:S(2)}) collective-permute-start(bf16[2,4,64,1024]{3,2,1,0:T(8,128)(2,1)} %get-tuple-element.36), channel_id=1, source_target_pairs={{0,32},{4,228},{32,64},{36,4},{64,96},{68,36},{96,128},{100,68},{1... | collective-permute-start | bytes 3145736 | tf_op jit(solution)/shard_map/ppermute | solution.py:422
  35.4 19.4 %collective-permute-start.5 = (bf16[4,64,1024]{2,1,0:T(8,128)(2,1)}, bf16[4,64,1024]{2,1,0:T(8,128)(2,1)S(1)}, u32[]{:S(2)}, u32[]{:S(2)}) collective-permute-start(bf16[4,64,1024]{2,1,0:T(8,128)(2,1)} %get-tuple-element.37), channel_id=1, source_target_pairs={{0,8},{8,16},{16,24},{24,0},{1,9},{9,17},{17,25},{25,1},{2,10},{10... | collective-permute-start | bytes 1572872 | tf_op jit(solution)/shard_map/ppermute | solution.py:457
  36.9 17.9 %collective-permute-start.6 = (bf16[4,64,1024]{2,1,0:T(8,128)(2,1)}, bf16[4,64,1024]{2,1,0:T(8,128)(2,1)S(1)}, u32[]{:S(2)}, u32[]{:S(2)}) collective-permute-start(bf16[4,64,1024]{2,1,0:T(8,128)(2,1)} %get-tuple-element.38), channel_id=1, source_target_pairs={{0,24},{8,0},{16,8},{24,16},{1,25},{9,1},{17,9},{25,17},{2,26},{10... | collective-permute-start | bytes 1572872 | tf_op jit(solution)/shard_map/ppermute | solution.py:457
  38.6 16.2 %collective-permute-start.7 = (bf16[2,64,1024]{2,1,0:T(8,128)(2,1)}, bf16[2,64,1024]{2,1,0:T(8,128)(2,1)S(1)}, u32[]{:S(2)}, u32[]{:S(2)}) collective-permute-start(bf16[2,64,1024]{2,1,0:T(8,128)(2,1)} %get-tuple-element.39), channel_id=1, source_target_pairs={{0,16},{8,24},{16,0},{24,8},{1,17},{9,25},{17,1},{25,9},{2,18},{10... | collective-permute-start | bytes 786440 | tf_op jit(solution)/shard_map/ppermute | solution.py:457
  61.3 48.9 %all-to-all-start = ((bf16[4,256,1152]{2,1,0:T(8,128)(2,1)}), bf16[4,256,1152]{2,1,0:T(8,128)(2,1)S(1)}, u32[]{:S(2)}, u32[]{:S(2)}) async-start(bf16[4,256,1152]{2,1,0:T(8,128)(2,1)} %project.1.refs_4_), calls=%async_computation | async-start | bytes 4718592 | tf_op jit(solution)/shard_map/all_to_all | solution.py:435
  68.2 18.4 %collective-permute-start.8 = (bf16[2,4,64,1024]{3,2,1,0:T(8,128)(2,1)}, bf16[2,4,64,1024]{3,2,1,0:T(8,128)(2,1)}, u32[]{:S(2)}, u32[]{:S(2)}) collective-permute-start(bf16[2,4,64,1024]{3,2,1,0:T(8,128)(2,1)} %get-tuple-element.41), channel_id=1, source_target_pairs={{0,32},{4,228},{32,64},{36,4},{64,96},{68,36},{96,128},{100,68},{1... | collective-permute-start | bytes 3145736 | tf_op jit(solution)/shard_map/ppermute | solution.py:422
  71.1 18.5 %collective-permute-start.12 = (bf16[4,64,1024]{2,1,0:T(8,128)(2,1)}, bf16[4,64,1024]{2,1,0:T(8,128)(2,1)S(1)}, u32[]{:S(2)}, u32[]{:S(2)}) collective-permute-start(bf16[4,64,1024]{2,1,0:T(8,128)(2,1)} %get-tuple-element.45), channel_id=1, source_target_pairs={{0,16},{8,24},{16,0},{24,8},{1,17},{9,25},{17,1},{25,9},{2,18},{10... | collective-permute-start | bytes 1572872 | tf_op jit(solution)/shard_map/ppermute | solution.py:457
  71.8 27.1 %collective-permute-start.13 = (bf16[4,64,1024]{2,1,0:T(8,128)(2,1)}, bf16[4,64,1024]{2,1,0:T(8,128)(2,1)S(1)}, u32[]{:S(2)}, u32[]{:S(2)}) collective-permute-start(bf16[4,64,1024]{2,1,0:T(8,128)(2,1)} %get-tuple-element.46), channel_id=1, source_target_pairs={{0,16},{8,24},{16,0},{24,8},{1,17},{9,25},{17,1},{25,9},{2,18},{10... | collective-permute-start | bytes 1572872 | tf_op jit(solution)/shard_map/ppermute | solution.py:457
  74.6 35.5 %collective-permute-start.14 = (bf16[4,64,1024]{2,1,0:T(8,128)(2,1)}, bf16[4,64,1024]{2,1,0:T(8,128)(2,1)}, u32[]{:S(2)}, u32[]{:S(2)}) collective-permute-start(bf16[4,64,1024]{2,1,0:T(8,128)(2,1)} %get-tuple-element.47), channel_id=1, source_target_pairs={{0,8},{8,16},{16,24},{24,0},{1,9},{9,17},{17,25},{25,1},{2,10},{10... | collective-permute-start | bytes 1572872 | tf_op jit(solution)/shard_map/ppermute | solution.py:457
  75.8 34.4 %collective-permute-start.15 = (bf16[4,64,1024]{2,1,0:T(8,128)(2,1)}, bf16[4,64,1024]{2,1,0:T(8,128)(2,1)}, u32[]{:S(2)}, u32[]{:S(2)}) collective-permute-start(bf16[4,64,1024]{2,1,0:T(8,128)(2,1)} %get-tuple-element.48), channel_id=1, source_target_pairs={{0,24},{8,0},{16,8},{24,16},{1,25},{9,1},{17,9},{25,17},{2,26},{10... | collective-permute-start | bytes 1572872 | tf_op jit(solution)/shard_map/ppermute | solution.py:457
  89.5 20.7 %collective-permute-start.9 = (bf16[1,4,64,1024]{3,2,1,0:T(8,128)(2,1)}, bf16[1,4,64,1024]{3,2,1,0:T(8,128)(2,1)}, u32[]{:S(2)}, u32[]{:S(2)}) collective-permute-start(bf16[1,4,64,1024]{3,2,1,0:T(8,128)(2,1)} %get-tuple-element.42), channel_id=1, source_target_pairs={{0,32},{4,228},{32,64},{36,4},{64,96},{68,36},{96,128},{100,68},{1... | collective-permute-start | bytes 1572872 | tf_op jit(solution)/shard_map/ppermute | solution.py:422
  89.6 31.7 %collective-permute-start.10 = (bf16[4,64,1024]{2,1,0:T(8,128)(2,1)}, bf16[4,64,1024]{2,1,0:T(8,128)(2,1)}, u32[]{:S(2)}, u32[]{:S(2)}) collective-permute-start(bf16[4,64,1024]{2,1,0:T(8,128)(2,1)} %get-tuple-element.43), channel_id=1, source_target_pairs={{0,8},{8,16},{16,24},{24,0},{1,9},{9,17},{17,25},{25,1},{2,10},{10... | collective-permute-start | bytes 1572872 | tf_op jit(solution)/shard_map/ppermute | solution.py:457
  98.9 22.4 %collective-permute-start.11 = (bf16[4,64,1024]{2,1,0:T(8,128)(2,1)}, bf16[4,64,1024]{2,1,0:T(8,128)(2,1)}, u32[]{:S(2)}, u32[]{:S(2)}) collective-permute-start(bf16[4,64,1024]{2,1,0:T(8,128)(2,1)} %get-tuple-element.44), channel_id=1, source_target_pairs={{0,24},{8,0},{16,8},{24,16},{1,25},{9,1},{17,9},{25,17},{2,26},{10... | collective-permute-start | bytes 1572872 | tf_op jit(solution)/shard_map/ppermute | solution.py:457
  125.1 31.8 %collective-permute-start.20 = (bf16[4,256,1152]{2,1,0:T(8,128)(2,1)}, bf16[4,256,1152]{2,1,0:T(8,128)(2,1)S(1)}, u32[]{:S(2)}, u32[]{:S(2)}) collective-permute-start(bf16[4,256,1152]{2,1,0:T(8,128)(2,1)} %get-tuple-element.49), channel_id=1, source_target_pairs={{0,4},{4,0},{1,5},{5,1},{2,6},{6,2},{3,7},{7,3},{8,12},{12,8},{9,1... | collective-permute-start | bytes 7077896 | tf_op jit(solution)/shard_map/ppermute | solution.py:331
  129.5 16.6 %collective-permute-start.16 = (bf16[4,64,1024]{2,1,0:T(8,128)(2,1)}, bf16[4,64,1024]{2,1,0:T(8,128)(2,1)S(1)}, u32[]{:S(2)}, u32[]{:S(2)}) collective-permute-start(bf16[4,64,1024]{2,1,0:T(8,128)(2,1)} %get-tuple-element.53), channel_id=1, source_target_pairs={{0,16},{8,24},{16,0},{24,8},{1,17},{9,25},{17,1},{25,9},{2,18},{10... | collective-permute-start | bytes 1572872 | tf_op jit(solution)/shard_map/ppermute | solution.py:457
  131.7 19.9 %collective-permute-start.17 = (bf16[2,64,1024]{2,1,0:T(8,128)(2,1)}, bf16[2,64,1024]{2,1,0:T(8,128)(2,1)S(1)}, u32[]{:S(2)}, u32[]{:S(2)}) collective-permute-start(bf16[2,64,1024]{2,1,0:T(8,128)(2,1)} %get-tuple-element.55), channel_id=1, source_target_pairs={{0,8},{8,16},{16,24},{24,0},{1,9},{9,17},{17,25},{25,1},{2,10},{10... | collective-permute-start | bytes 786440 | tf_op jit(solution)/shard_map/ppermute | solution.py:457
  132.1 24.8 %collective-permute-start.18 = (bf16[2,64,1024]{2,1,0:T(8,128)(2,1)}, bf16[2,64,1024]{2,1,0:T(8,128)(2,1)S(1)}, u32[]{:S(2)}, u32[]{:S(2)}) collective-permute-start(bf16[2,64,1024]{2,1,0:T(8,128)(2,1)} %get-tuple-element.56), channel_id=1, source_target_pairs={{0,16},{8,24},{16,0},{24,8},{1,17},{9,25},{17,1},{25,9},{2,18},{10... | collective-permute-start | bytes 786440 | tf_op jit(solution)/shard_map/ppermute | solution.py:457
  135.3 21.6 %collective-permute-start.19 = (bf16[2,64,1024]{2,1,0:T(8,128)(2,1)}, bf16[2,64,1024]{2,1,0:T(8,128)(2,1)S(1)}, u32[]{:S(2)}, u32[]{:S(2)}) collective-permute-start(bf16[2,64,1024]{2,1,0:T(8,128)(2,1)} %get-tuple-element.57), channel_id=1, source_target_pairs={{0,24},{8,0},{16,8},{24,16},{1,25},{9,1},{17,9},{25,17},{2,26},{10... | collective-permute-start | bytes 786440 | tf_op jit(solution)/shard_map/ppermute | solution.py:457
  170.1 17.9 %collective-permute-start.21 = (bf16[4,4,4,64,256]{4,3,2,1,0:T(8,128)(2,1)}, bf16[4,4,4,64,256]{4,3,2,1,0:T(8,128)(2,1)S(1)}, u32[]{:S(2)}, u32[]{:S(2)}) collective-permute-start(bf16[4,4,4,64,256]{4,3,2,1,0:T(8,128)(2,1)} %get-tuple-element.62), channel_id=1, source_target_pairs={{0,4},{4,0},{1,5},{5,1},{2,6},{6,2},{3,7},{7,3},{8,12},{12,8},{9,1... | collective-permute-start | bytes 6291464 | tf_op jit(solution)/shard_map/ppermute | solution.py:339
  191.4 20.6 %collective-permute-start.22 = (bf16[1024,256]{1,0:T(8,128)(2,1)}, bf16[1024,256]{1,0:T(8,128)(2,1)S(1)}, u32[]{:S(2)}, u32[]{:S(2)}) collective-permute-start(bf16[1024,256]{1,0:T(8,128)(2,1)} %bitcast.22), channel_id=1, source_target_pairs={{0,1},{1,2},{2,3},{3,0},{4,5},{5,6},{6,7},{7,4},{8,9},{9,10},{10,1... | collective-permute-start | bytes 1572872 | tf_op jit(solution)/shard_map/ppermute | solution.py:343
  192.6 24.4 %collective-permute-start.23 = (bf16[1024,256]{1,0:T(8,128)(2,1)S(1)}, bf16[1024,256]{1,0:T(8,128)(2,1)S(1)}, u32[]{:S(2)}, u32[]{:S(2)}) collective-permute-start(bf16[1024,256]{1,0:T(8,128)(2,1)S(1)} %bitcast.62), channel_id=1, source_target_pairs={{0,2},{1,3},{2,0},{3,1},{4,6},{5,7},{6,4},{7,5},{8,10},{9,11},{10,... | collective-permute-start | bytes 1572872 | tf_op jit(solution)/shard_map/ppermute | solution.py:343
  193.4 25.8 %collective-permute-start.24 = (bf16[1024,256]{1,0:T(8,128)(2,1)S(1)}, bf16[1024,256]{1,0:T(8,128)(2,1)S(1)}, u32[]{:S(2)}, u32[]{:S(2)}) collective-permute-start(bf16[1024,256]{1,0:T(8,128)(2,1)S(1)} %bitcast.61), channel_id=1, source_target_pairs={{0,3},{1,0},{2,1},{3,2},{4,7},{5,4},{6,5},{7,6},{8,11},{9,8},{10,9... | collective-permute-start | bytes 1572872 | tf_op jit(solution)/shard_map/ppermute | solution.py:343
  (37 other events, 272.8 us)
Sparse Core Ops, SparseCore 0:
  61.4 102.7 all-gather.2
